TPU v7x, 128 devices: a whole 4x4x4 slice. The times are simulated.
128 devices in a mesh: ctx: 16 (over y, z), exp: 8 (over x, core).
Axes of the slice: x: 4, y: 4, z: 4, core: 2. Of those that a mesh axis runs over, the one named last changes fastest.
Arguments:
- residual_in: bfloat16 [16384, 2048], P(('ctx', 'exp')), may hold values from -6 to 6
- queries: bfloat16 [16384, 2048], P('ctx', 'exp'), may hold values from -6 to 6
- key_rows: bfloat16 [16384, 2048], P('ctx', 'exp'), may hold values from -6 to 6
- values: bfloat16 [16384, 2048], P('ctx', 'exp'), may hold values from -6 to 6
- log_decay: float32 [16, 16384], P('exp', 'ctx'), may hold values from -1 to 0
- attn_gain: float32 [2048], P('exp'), may hold values from 0.5 to 1.5
- out_proj: bfloat16 [2048, 2048], P('exp'), may hold values from -0.125 to 0.125
- ffn_gain: float32 [2048], replicated, may hold values from 0.5 to 1.5
- router: bfloat16 [2048, 64], replicated, may hold values from -0.25 to 0.25
- route_ids: int32 [16384, 6], P(('ctx', 'exp')), may hold values from 0 to 63, as said below
- w_gate: bfloat16 [8, 2048, 1408], P('exp'), may hold values from -0.125 to 0.125
- w_up: bfloat16 [8, 2048, 1408], P('exp'), may hold values from -0.125 to 0.125
- w_down: bfloat16 [8, 1408, 2048], P('exp'), may hold values from -0.4375 to 0.4375
- shared_gate: bfloat16 [2048, 2816], P(None, 'ctx'), may hold values from -0.125 to 0.125
- shared_up: bfloat16 [2048, 2816], P(None, 'ctx'), may hold values from -0.125 to 0.125
- shared_down: bfloat16 [2816, 2048], P('ctx'), may hold values from -0.109375 to 0.109375
Outputs:
- layer_out: bfloat16 [16384, 2048], P(('ctx', 'exp'))
Inputs may be any that keep to these rules, and one draw needn't show every extreme that they name: `route_ids`: each row names 6 different experts. In each aligned block of 128 rows (the rows of one device) no expert below 8 is named by more than 24 rows, and one such expert, the same in all blocks of a draw, is named by exactly 24 rows in every block.
All inputs are finite; a program needn't handle non-finite values.
Results may differ from a plain program's by a relative error of at most 0.02.
Values may be sent and summed in bfloat16 or wider, within the bound.
No kernel may reach another device: no remote copies, remote signals or barrier semaphores. Data moves between devices by JAX's collectives and lax.ppermute only.
A program may use at most 192 MiB of HBM per device.

v0:
```python
import jax
import jax.numpy as jnp
from jax import lax
from jax.sharding import PartitionSpec as P

BLOCK = 512
CAP = 24


finest = lax.Precision.HIGHEST


def prefix(x, axis, join, neutral):
    place = lax.axis_index(axis)
    gathered = jax.tree.map(
        lambda a, kind: lax.all_gather(a.astype(kind), axis), x, (jnp.bfloat16, jnp.bfloat16)
    )
    state = jax.tree.map(lambda a, e: jnp.zeros_like(a) + jnp.asarray(e, a.dtype), x, neutral)

    def one(step, state):
        return join(
            state,
            jax.tree.map(
                lambda a, own: lax.dynamic_index_in_dim(a, step, 0, False).astype(own.dtype),
                gathered,
                x,
            ),
        )

    return lax.fori_loop(0, place, one, state)


def head_blocks(queries, key_rows, values, log_decay):
    head_count = log_decay.shape[0]
    row_count = queries.shape[0]
    head_width = queries.shape[1] // head_count
    blocks_here = row_count // BLOCK
    block_shape = (blocks_here, BLOCK, head_count, head_width)
    decay_rows = log_decay.T.reshape(blocks_here, BLOCK, head_count)
    causal = jnp.arange(BLOCK)[:, None] >= jnp.arange(BLOCK)[None, :]

    def advance(carry, pieces):
        carried, offset = carry
        query_block, key_block, value_block, decay_block = pieces
        within = jnp.cumsum(decay_block, axis=0)
        scores = jnp.einsum(
            "thd,shd->hts", query_block, key_block, preferred_element_type=jnp.float32
        )
        spread = within.T[:, :, None] - within.T[:, None, :]
        near = jnp.where(causal, scores * jnp.exp(jnp.where(causal, spread, 0.0)), 0.0).astype(
            jnp.bfloat16
        )
        inner = jnp.einsum("hts,shd->thd", near, value_block, preferred_element_type=jnp.float32)
        query_wide = query_block.astype(jnp.float32)
        earlier = jnp.einsum(
            "thd,hde->the", query_wide * jnp.exp(within)[:, :, None], carried, precision=finest
        )
        ending = within[-1]
        key_wide = key_block.astype(jnp.float32) * jnp.exp(ending[None, :] - within)[:, :, None]
        carried = jnp.exp(ending)[:, None, None] * carried + jnp.einsum(
            "thd,the->hde", key_wide, value_block.astype(jnp.float32), precision=finest
        )
        reach_rows = query_wide * jnp.exp(offset[None, :] + within)[:, :, None]
        return ((carried, offset + ending), (inner + earlier, reach_rows))

    initial = (
        jnp.zeros((head_count, head_width, head_width), jnp.float32),
        jnp.zeros((head_count,), jnp.float32),
    )
    (carried, decay_total), (local_out, reach_rows) = lax.scan(
        advance,
        initial,
        (
            queries.reshape(block_shape),
            key_rows.reshape(block_shape),
            values.reshape(block_shape),
            decay_rows,
        ),
    )
    return (
        carried,
        decay_total,
        local_out.reshape(row_count, head_count, head_width),
        reach_rows.reshape(row_count, head_count, head_width),
    )


def link(earlier, later):
    return (earlier[0] + later[0], jnp.exp(later[0])[:, None, None] * earlier[1] + later[1])


def swiglu(rows_in, gate_w, up_w):
    gate_part = jnp.dot(rows_in, gate_w, preferred_element_type=jnp.float32)
    up_part = jnp.dot(rows_in, up_w, preferred_element_type=jnp.float32)
    return (jax.nn.silu(gate_part) * up_part).astype(jnp.bfloat16)


def on_device(
    residual_in,
    queries,
    key_rows,
    values,
    log_decay,
    attn_gain,
    out_proj,
    ffn_gain,
    router,
    route_ids,
    w_gate,
    w_up,
    w_down,
    shared_gate,
    shared_up,
    shared_down,
):
    carried, decay_total, local_out, reach_rows = head_blocks(queries, key_rows, values, log_decay)
    head_count = local_out.shape[1]
    head_width = local_out.shape[2]
    identity_pair = (jnp.zeros_like(decay_total), jnp.zeros_like(carried))
    incoming = prefix((decay_total, carried), "ctx", link, identity_pair)[1]
    mixed = local_out + jnp.einsum("thd,hde->the", reach_rows, incoming, precision=finest)
    scale = lax.rsqrt(jnp.mean(mixed * mixed, axis=2, keepdims=True) + 1e-06)
    normed = (
        (mixed * scale * attn_gain.reshape(head_count, head_width))
        .astype(jnp.bfloat16)
        .reshape(mixed.shape[0], head_count * head_width)
    )
    tokens_here = residual_in.shape[0]
    attended = lax.psum_scatter(
        jnp.dot(normed, out_proj, preferred_element_type=jnp.float32).astype(jnp.bfloat16),
        "exp",
        scatter_dimension=0,
        tiled=True,
    ).astype(jnp.float32)
    stream = residual_in.astype(jnp.float32) + attended
    normed_ffn = (
        stream * lax.rsqrt(jnp.mean(stream * stream, axis=1, keepdims=True) + 1e-06) * ffn_gain
    ).astype(jnp.bfloat16)
    affinity = jax.nn.sigmoid(jnp.dot(normed_ffn, router, preferred_element_type=jnp.float32))
    expert_iota = jnp.arange(router.shape[1], dtype=jnp.int32)
    picked = jnp.sum(
        jnp.where(route_ids[:, :, None] == expert_iota[None, None, :], affinity[:, None, :], 0.0),
        axis=2,
    )
    gates = picked / jnp.sum(picked, axis=1, keepdims=True)
    owners = lax.axis_size("exp")
    routes_each = route_ids.shape[1]
    flat_ids = route_ids.reshape(-1)
    owner_hits = (flat_ids[:, None] == jnp.arange(owners, dtype=jnp.int32)[None, :]).astype(
        jnp.int32
    )
    ranks = jnp.sum((jnp.cumsum(owner_hits, axis=0) - owner_hits) * owner_hits, axis=1)
    target = jnp.where(flat_ids < owners, flat_ids * CAP + ranks, -1)
    places = (target[:, None] == jnp.arange(owners * CAP, dtype=jnp.int32)[None, :]).reshape(
        tokens_here, routes_each, owners * CAP
    )
    selector = jnp.any(places, axis=1).astype(jnp.bfloat16)
    outgoing = (
        lax.dot_general(
            selector, normed_ffn, (((0,), (0,)), ((), ())), preferred_element_type=jnp.float32
        )
        .astype(jnp.bfloat16)
        .reshape(owners, CAP, normed_ffn.shape[1])
    )
    arrived = lax.all_to_all(outgoing, "exp", split_axis=0, concat_axis=0, tiled=True)
    source_count = arrived.shape[0]
    slot_count = arrived.shape[1]
    model_width = arrived.shape[2]
    flat_rows = arrived.reshape(source_count * slot_count, model_width)
    hidden = swiglu(flat_rows, w_gate[0], w_up[0])
    result = jnp.dot(hidden, w_down[0], preferred_element_type=jnp.float32).astype(jnp.bfloat16)
    returned = lax.all_to_all(
        result.reshape(source_count, slot_count, model_width),
        "exp",
        split_axis=0,
        concat_axis=0,
        tiled=True,
    )
    weights_back = jnp.sum(jnp.where(places, gates[:, :, None], 0.0), axis=1)
    routed = jnp.dot(
        weights_back, returned.reshape(owners * CAP, -1).astype(jnp.float32), precision=finest
    )
    shared_mid = swiglu(
        lax.all_gather(normed_ffn, "ctx", axis=0, tiled=True), shared_gate, shared_up
    )
    shared_out = lax.psum_scatter(
        jnp.dot(shared_mid, shared_down, preferred_element_type=jnp.float32).astype(jnp.bfloat16),
        "ctx",
        scatter_dimension=0,
        tiled=True,
    ).astype(jnp.float32)
    return (stream + shared_out + routed).astype(jnp.bfloat16)


def solution(mesh):
    return jax.shard_map(
        on_device,
        mesh=mesh,
        in_specs=(
            P(("ctx", "exp"), None),
            P("ctx", "exp"),
            P("ctx", "exp"),
            P("ctx", "exp"),
            P("exp", "ctx"),
            P("exp"),
            P("exp", None),
            P(),
            P(),
            P(("ctx", "exp"), None),
            P("exp", None, None),
            P("exp", None, None),
            P("exp", None, None),
            P(None, "ctx"),
            P(None, "ctx"),
            P("ctx", None),
        ),
        out_specs=P(("ctx", "exp"), None),
        check_vma=False,
    )
```

profile of v0, /device:TPU:1, one launch (start us, length us, event | category | flops | bytes accessed | tf_op | source)
XLA Modules:
  0.0 336.3 jit_solution(9038108387699996867)
XLA Ops:
  6.6 1.3 reshape.161
  7.9 2.0 reshape.162
  9.8 0.9 reshape.163
  10.7 35.0 %while.31 = (s32[]{:T(128)}, f32[2,128,128]{2,1,0:T(8,128)S(1)}, f32[2]{0:T(128)S(1)}, f32[2,512,2,128]{1,0,3,2:T(2,128)}, f32[2,512,2,128]{3,1,0,2:T(8,128)}, /...) while((s32[]{:T(128)}, f32[2,128,128]{2,1,0:T(8,128)S(1)}, ...), condition=%wide.region_3.4_spmd.clone.clone, body=%wide.region_0.3_spmd.clone.clone.sunk | while | flops 675153920 | bytes 8594321 | solution.py:70
  10.8 0.6 reduce-window.28
  11.4 0.2 slice_reduce_fusion.4
  11.5 0.2 reduce-window.29
  11.8 0.2 slice_reduce_fusion.5
  12.1 1.4 constant_dynamic-slice_fusion.6
  13.5 0.2 constant_dynamic-slice_fusion.5
  13.8 1.0 fusion.90
  14.8 0.8 fusion.91
  15.6 0.5 copy.196
  16.2 10.3 %dynamic_update_slice.15 = f32[2,512,2,128]{1,0,3,2:T(2,128)} dynamic-update-slice(f32[2,512,2,128]{1,0,3,2:T(2,128)} %get-tuple-element.384, f32[1,512,2,128]{1,0,3,2:T(1,128)S(1)} %copy.196, s32[]{:T(128)} %get-tuple-element.381, s32[]{:T(128)} %constant.62.clone.1..sunk.1, s32[]{:T(128)} %constant.62.clone.1..sunk.1, s32[]{:T(128)} %constant.62.clone.1..sunk.1) | dynamic-update-slice | bytes 1048580 | tf_op jit(solution)/shard_map/while/body/jit(dynamic_update_index_in_dim)/dynamic_update_slice | solution.py:70
  26.5 1.0 bitcast_dynamic-update-slice_fusion.2
  27.5 0.8 convolution_add_fusion.3
  28.3 0.6 reduce-window.28
  28.9 0.2 slice_reduce_fusion.4
  29.1 0.2 reduce-window.29
  29.3 0.2 slice_reduce_fusion.5
  29.6 1.4 constant_dynamic-slice_fusion.6
  31.0 0.2 constant_dynamic-slice_fusion.5
  31.3 1.0 fusion.90
  32.4 0.8 fusion.91
  33.1 0.5 copy.196
  33.7 10.3 %dynamic_update_slice.15 = f32[2,512,2,128]{1,0,3,2:T(2,128)} dynamic-update-slice(f32[2,512,2,128]{1,0,3,2:T(2,128)} %get-tuple-element.384, f32[1,512,2,128]{1,0,3,2:T(1,128)S(1)} %copy.196, s32[]{:T(128)} %get-tuple-element.381, s32[]{:T(128)} %constant.62.clone.1..sunk.1, s32[]{:T(128)} %constant.62.clone.1..sunk.1, s32[]{:T(128)} %constant.62.clone.1..sunk.1) | dynamic-update-slice | bytes 1048580 | tf_op jit(solution)/shard_map/while/body/jit(dynamic_update_index_in_dim)/dynamic_update_slice | solution.py:70
  44.0 1.0 bitcast_dynamic-update-slice_fusion.2
  45.0 0.8 convolution_add_fusion.3
  45.8 0.6 convert_element_type.82
  46.6 0.6 dynamic-slice
  47.7 0.2 dynamic-update-slice
  47.9 35.8 %all-reduce = bf16[32]{0:T(256)(128)(2,1)S(1)} all-reduce(bf16[32]{0:T(256)(128)(2,1)S(1)} %dynamic-update-slice), channel_id=2, replica_groups=mesh['ctx'=16,'exp'=8] {'ctx'}, use_global_device_ids=true, to_apply=%add | all-reduce | flops 32 | bytes 128
  83.7 0.1 reshape.175
  83.8 2.2 reshape.164
  85.9 5.4 %all-gather.7.cloned.1.call-done = bf16[32,128,128]{2,1,0:T(8,128)(2,1)} async-done(((bf16[2,128,128]{2,1,0:T(8,128)(2,1)}), bf16[32,128,128]{2,1,0:T(8,128)(2,1)}) %all-gather.7.cloned.1.call-update) | async-done | bytes 1048592 | tf_op jit(solution)/shard_map/all_gather | solution.py:16
  91.4 1.1 multiply_reduce_fusion.1
  92.5 0.1 multiply_convert_fusion.1
  92.7 3.2 convolution_convert_fusion.1
  96.0 49.5 %reduce-scatter.3.cloned.1.call-done = bf16[128,2048]{1,0:T(8,128)(2,1)} async-done(((bf16[1024,2048]{1,0:T(8,128)(2,1)}), bf16[128,2048]{1,0:T(8,128)(2,1)}) %reduce-scatter.3.cloned.1.call-update) | async-done | bytes 524304 | tf_op jit(solution)/shard_map/reduce_scatter | solution.py:129
  145.5 1.3 multiply_reduce_fusion
  146.8 2.0 multiply_convert_fusion
  148.9 0.2 reduce-scatter.5.cloned.1.call-start
  149.1 72.7 %all-gather.5.cloned.1.call-done = bf16[2048,2048]{1,0:T(8,128)(2,1)} async-done(((bf16[128,2048]{1,0:T(8,128)(2,1)}), bf16[2048,2048]{1,0:T(8,128)(2,1)}) %all-gather.5.cloned.1.call-update) | async-done | bytes 8388624 | tf_op jit(solution)/shard_map/all_gather | solution.py:184
  221.8 7.4 %fusion.60 = f32[2048,176]{0,1:T(8,128)} fusion(bf16[2048,2048]{1,0:T(8,128)(2,1)} %all-gather.5.cloned.1.call-done, bf16[2048,176]{0,1:T(8,128)(2,1)S(1)} %copy-done.10), kind=kOutput, calls=%fused_computation.94 | convolution fusion | flops 1476395008 | bytes 10551296 | tf_op jit(solution)/shard_map/dot_general | solution.py:93
  229.2 14.3 %convolution_convert_fusion = bf16[2048,2048]{1,0:T(8,128)(2,1)} fusion(bf16[176,2048]{1,0:T(8,128)(2,1)S(1)} %copy-done.11, bf16[2048,2048]{1,0:T(8,128)(2,1)} %all-gather.5.cloned.1.call-done, bf16[2048,176]{0,1:T(8,128)(2,1)} %param.34, f32[2048,176]{0,1:T(8,128)} %fusion.60), kind=kOutput, calls=%fused_computation.46 | convolution fusion | flops 2959147008 | bytes 19660800 | tf_op jit(solution)/shard_map/dot_general | solution.py:187
  243.5 0.7 copy-done.7
  244.2 0.1 copy.126
  244.3 0.1 eq.56
  244.4 0.1 eq.52
  244.6 1.7 reduce-window.16
  246.4 0.1 copy.128
  246.5 0.2 reduce-window.17
  246.8 0.1 fusion.55
  246.9 0.1 reduce_sum.59
  247.1 0.1 fusion.52
  247.2 0.4 convolution_convert_fusion.2
  247.5 16.9 %all_to_all.10 = bf16[8,24,2048]{2,1,0:T(8,128)(2,1)S(1)} all-to-all(bf16[8,24,2048]{2,1,0:T(8,128)(2,1)S(1)} %bitcast.159), channel_id=1, replica_groups=mesh['ctx'=16,'exp'=8] {'exp'}, dimensions={0} | all-to-all | bytes 1572864 | tf_op jit(solution)/shard_map/all_to_all | solution.py:165
  264.5 5.6 %fusion.32 = f32[192,1408]{1,0:T(8,128)} fusion(bf16[192,2048]{1,0:T(8,128)(2,1)S(1)} %bitcast.162, bf16[1,2048,1408]{2,1,0:T(8,128)(2,1)} %param.30), kind=kOutput, calls=%fused_computation.51 | convolution fusion | flops 1107296256 | bytes 7634944 | tf_op jit(solution)/shard_map/dot_general | solution.py:93
  270.1 8.4 %fusion.40 = bf16[192,2048]{1,0:T(8,128)(2,1)} fusion(bf16[1,1408,2048]{2,1,0:T(8,128)(2,1)} %param.32, bf16[192,2048]{1,0:T(8,128)(2,1)S(1)} %bitcast.163, bf16[1,2048,1408]{2,1,0:T(8,128)(2,1)} %param.31, f32[192,1408]{1,0:T(8,128)} %fusion.32), kind=kOutput, calls=%fused_computation.57 | convolution fusion | flops 2216607744 | bytes 14188544 | tf_op jit(solution)/shard_map/dot_general | solution.py:171
  278.5 4.4 %all-to-all-start.1 = ((bf16[8,24,2048]{2,1,0:T(8,128)(2,1)}), bf16[8,24,2048]{2,1,0:T(8,128)(2,1)S(1)}, u32[]{:S(2)}, u32[]{:S(2)}) async-start(bf16[8,24,2048]{2,1,0:T(8,128)(2,1)} %bitcast.161), calls=%async_computation.3 | async-start | bytes 1572864 | tf_op jit(solution)/shard_map/all_to_all | solution.py:172
  282.9 1.3 fusion.48
  284.3 10.9 %all-to-all-done.1 = bf16[8,24,2048]{2,1,0:T(8,128)(2,1)S(1)} async-done(((bf16[8,24,2048]{2,1,0:T(8,128)(2,1)}), bf16[8,24,2048]{2,1,0:T(8,128)(2,1)S(1)}, u32[]{:S(2)}, u32[]{:S(2)}) %all-to-all-start.1) | async-done | bytes 786464 | tf_op jit(solution)/shard_map/all_to_all | solution.py:172
  295.2 32.0 %reduce-scatter.5.cloned.1.call-done = bf16[128,2048]{1,0:T(8,128)(2,1)} async-done(((bf16[2048,2048]{1,0:T(8,128)(2,1)}), bf16[128,2048]{1,0:T(8,128)(2,1)}) %reduce-scatter.5.cloned.1.call-update) | async-done | bytes 524304 | tf_op jit(solution)/shard_map/reduce_scatter | solution.py:186
  327.2 2.6 fusion.44
  (64 shorter events, 1.2 us)
Async XLA Ops:
  6.5 86.1 %copy-start = (bf16[256,2048]{1,0:T(8,128)(2,1)S(1)}, bf16[256,2048]{1,0:T(8,128)(2,1)}, u32[]{:S(2)}) copy-start(bf16[256,2048]{1,0:T(8,128)(2,1)} %param.26) | copy-start | bytes 3145732
  6.5 3.3 copy-start.5
  6.5 4.2 %copy-start.6 = (f32[2,1024]{1,0:T(2,128)S(1)}, f32[2,1024]{1,0:T(2,128)}, u32[]{:S(2)}) copy-start(f32[2,1024]{1,0:T(2,128)} %param.24) | copy-start | bytes 24580
  6.5 84.8 %all-gather.7.cloned.1.call-start = ((), (), s32[]{:S(2)}) async-start(), calls=%async_computation.7 | async-start | bytes 1114112 | tf_op jit(solution)/shard_map/all_gather | solution.py:16
  10.7 35.8 %copy-start.12 = (u32[128]{0:T(128)S(1)}, u32[128]{0:T(128)}, u32[]{:S(2)}) copy-start(u32[128]{0:T(128)} %constant.80) | copy-start | bytes 1540
  46.4 44.9 %copy-start.4 = (f32[2,512,2,128]{3,1,0,2:T(8,128)S(1)}, f32[2,512,2,128]{3,1,0,2:T(8,128)}, u32[]{:S(2)}) copy-start(f32[2,512,2,128]{3,1,0,2:T(8,128)} %get-tuple-element.111) | copy-start | bytes 3145732
  46.5 99.0 %reduce-scatter.3.cloned.1.call-start = ((), (), s32[]{:S(2)}) async-start(), calls=%async_computation.4 | async-start | bytes 4718592 | tf_op jit(solution)/shard_map/reduce_scatter | solution.py:129
  91.3 1.2 copy-start.9
  95.9 49.6 %copy-start.2 = (bf16[128,2048]{1,0:T(8,128)(2,1)S(1)}, bf16[128,2048]{1,0:T(8,128)(2,1)}, u32[]{:S(2)}) copy-start(bf16[128,2048]{1,0:T(8,128)(2,1)} %param.20) | copy-start | bytes 1572868
  95.9 50.9 %copy-start.8 = (f32[2048]{0:T(1024)S(1)}, f32[2048]{0:T(1024)}, u32[]{:S(2)}) copy-start(f32[2048]{0:T(1024)} %param.27) | copy-start | bytes 24580
  95.9 125.9 %copy-start.10 = (bf16[2048,176]{0,1:T(8,128)(2,1)S(1)}, bf16[2048,176]{0,1:T(8,128)(2,1)}, u32[]{:S(2)}) copy-start(bf16[2048,176]{0,1:T(8,128)(2,1)} %param.33) | copy-start | bytes 2162692
  95.9 125.9 %all-gather.5.cloned.1.call-start = ((), (), s32[]{:S(2)}) async-start(), calls=%async_computation.5 | async-start | bytes 8912896 | tf_op jit(solution)/shard_map/all_gather | solution.py:184
  148.9 80.4 %copy-start.11 = (bf16[176,2048]{1,0:T(8,128)(2,1)S(1)}, bf16[176,2048]{1,0:T(8,128)(2,1)}, u32[]{:S(2)}) copy-start(bf16[176,2048]{1,0:T(8,128)(2,1)} %param.35) | copy-start | bytes 2162692
  148.9 178.3 %reduce-scatter.5.cloned.1.call-start = ((), (), s32[]{:S(2)}) async-start(), calls=%async_computation.6 | async-start | bytes 8912896 | tf_op jit(solution)/shard_map/reduce_scatter | solution.py:186
  243.5 0.7 copy-start.7
  243.5 3.7 %copy-start.1 = (bf16[128,2048]{1,0:T(8,128)(2,1)S(1)}, bf16[128,2048]{1,0:T(8,128)(2,1)}, u32[]{:S(2)}) copy-start(bf16[128,2048]{1,0:T(8,128)(2,1)} %multiply_convert_fusion) | copy-start | bytes 1572868
  278.5 48.8 %copy-start.3 = (bf16[128,2048]{1,0:T(8,128)(2,1)S(1)}, bf16[128,2048]{1,0:T(8,128)(2,1)}, u32[]{:S(2)}) copy-start(bf16[128,2048]{1,0:T(8,128)(2,1)} %reduce-scatter.3.cloned.1.call-done) | copy-start | bytes 1572868
  278.5 16.7 %all-to-all-start.1 = ((bf16[8,24,2048]{2,1,0:T(8,128)(2,1)}), bf16[8,24,2048]{2,1,0:T(8,128)(2,1)S(1)}, u32[]{:S(2)}, u32[]{:S(2)}) async-start(bf16[8,24,2048]{2,1,0:T(8,128)(2,1)} %bitcast.161), calls=%async_computation.3 | async-start | bytes 1572864 | tf_op jit(solution)/shard_map/all_to_all | solution.py:172
Sparse Core Ops, SparseCore 0:
  46.6 44.6 all-gather.6
  96.1 49.4 reduce-scatter.2
  149.0 72.7 all-gather.4
  243.7 83.5 reduce-scatter.4
where the time goes:
time: 339 us; the launch traced here: 336 us
  waiting for transfers between devices  171 us (50%)
  blocking collectives  52.7 us (16%)
  matrix products  49.4 us (15%)
  local copies, waits for them, and re-layouts  34.4 us (10%)
  between operations  13.9 us (4%)
  other arithmetic  10.4 us (3%)
  starting transfers between devices  4.72 us (1%)
    all_gather x1, waiting for transfers between devices, on_device(): lax.all_gather(normed_ffn, 'ctx', axis=0, tiled=True)  72.7 us
    reduce_scatter x1, waiting for transfers between devices, on_device(): lax.psum_scatter(jnp.dot(normed, out_proj, preferred_element_type=jnp.flo...  49.5 us
    unnamed x1, blocking collectives  35.8 us
    reduce_scatter x1, waiting for transfers between devices, on_device(): lax.psum_scatter(jnp.dot(shared_mid, shared_down, preferred_element_type=...  32 us
    dynamic_update_slice x4, local copies, waits for them, and re-layouts, head_blocks(): lax.scan(advance, initial, (queries.reshape(block_shape), key_rows.reshap...  21.7 us
    all_to_all x1, blocking collectives, on_device(): lax.all_to_all(outgoing, 'exp', split_axis=0, concat_axis=0, tiled=True)  16.9 us
    dot_general x1, matrix products, on_device(): jnp.dot(shared_mid, shared_down, preferred_element_type=jnp.float32)  14.3 us
    dot_general x2, matrix products, swiglu(): gate_part = jnp.dot(rows_in, gate_w, preferred_element_type=jnp.float32)  13 us
  transfers between devices with their start and end apart: 5, of which 5 were waited for; matrix products, arithmetic and copies ran while one was open for 6% of the time, Pallas kernels for 0%

commit v1 on v0

v1 whole, which is shorter than its diff:
```python
import functools

import jax
import jax.numpy as jnp
from jax import lax
from jax.experimental import pallas as pl
from jax.experimental.pallas import tpu as pltpu
from jax.sharding import Mesh, PartitionSpec as P

BF = jnp.bfloat16
F32 = jnp.float32
CHUNK = 256
CHUNKS = 4
HD = 128
HEADS = 2
CAP = 24
SLOTS = 2 * CAP
T_DEV = 128
T_CHIP = 256
ROUTED = 64
TOPK = 6
D = 2048
FF = 1408
SH = 176
HALF = 96
SHIFT = SH - HALF
MSG = 272
FINEST = lax.Precision.HIGHEST
Z = ("zh", "zl")

VM = pl.BlockSpec(memory_space=pltpu.VMEM)
SM = pl.BlockSpec(memory_space=pltpu.SMEM)


def mm(a, b, dims=((1,), (0,))):
    return lax.dot_general(a, b, (dims, ((), ())), preferred_element_type=F32)


def lower_ones():
    t = lax.broadcasted_iota(jnp.int32, (CHUNK, CHUNK), 0)
    s = lax.broadcasted_iota(jnp.int32, (CHUNK, CHUNK), 1)
    return t, s


def chunk_rows(decay_ref, j, t, s):
    part = decay_ref[:, j * CHUNK : (j + 1) * CHUNK]
    upper = jnp.where(t <= s, 1.0, 0.0)
    return lax.dot_general(
        part, upper, (((1,), (0,)), ((), ())), precision=FINEST, preferred_element_type=F32
    )


def chunk_cols(decay_ref, j, t, s):
    part = decay_ref[:, j * CHUNK : (j + 1) * CHUNK]
    lower = jnp.where(s <= t, 1.0, 0.0)
    return lax.dot_general(
        lower, part, (((1,), (1,)), ((), ())), precision=FINEST, preferred_element_type=F32
    )


def rows_of(j):
    return slice(j * CHUNK, (j + 1) * CHUNK)


def cols_of(h):
    return slice(h * HD, (h + 1) * HD)


def three_parts(x):
    hi = x.astype(BF).astype(F32)
    mid = (x - hi).astype(BF).astype(F32)
    lo = x - hi - mid
    return hi, mid, lo


def write_message(message_ref, states, totals):
    row = lax.broadcasted_iota(jnp.int32, (16, HD), 0)
    tail = jnp.zeros((16, HD), F32)
    for h in range(HEADS):
        message_ref[h * HD : (h + 1) * HD, :] = states[h].astype(BF)
        for i, piece in enumerate(three_parts(totals[h])):
            tail = jnp.where(row == 3 * h + i, piece, tail)
    message_ref[HEADS * HD : MSG, :] = tail.astype(BF)


def read_message(message_ref):
    tail = message_ref[HEADS * HD : MSG, :].astype(F32)
    out = []
    for h in range(HEADS):
        total = tail[3 * h : 3 * h + 1] + tail[3 * h + 1 : 3 * h + 2] + tail[3 * h + 2 : 3 * h + 3]
        out.append((message_ref[h * HD : (h + 1) * HD, :].astype(F32), total))
    return out


def states_kernel(key_ref, value_ref, decay_ref, states_ref, message_ref):
    t, s = lower_ones()
    states = [jnp.zeros((HD, HD), F32) for _ in range(HEADS)]
    totals = [jnp.zeros((1, 1), F32) for _ in range(HEADS)]
    for j in range(CHUNKS):
        col = chunk_cols(decay_ref, j, t, s)
        for h in range(HEADS):
            states_ref[j, h] = states[h]
            within = col[:, h : h + 1]
            last = within[CHUNK - 1 : CHUNK, :]
            keys = (key_ref[rows_of(j), cols_of(h)].astype(F32) * jnp.exp(last - within)).astype(BF)
            states[h] = jnp.exp(last) * states[h] + mm(
                keys, value_ref[rows_of(j), cols_of(h)], ((0,), (0,))
            )
            totals[h] = totals[h] + last
    write_message(message_ref, states, totals)


def row_kernel(place_ref, own_ref, one_ref, two_ref, three_ref, prefix_ref, total_ref, message_ref):
    z = place_ref[0]
    parts = [read_message(r) for r in (own_ref, one_ref, two_ref, three_ref)]
    at = [lax.rem(z - d + 4, 4) for d in range(4)]
    sums, sum_totals = [], []
    for h in range(HEADS):
        whole = jnp.zeros((HD, HD), F32)
        before = jnp.zeros((HD, HD), F32)
        whole_total = jnp.zeros((1, HD), F32)
        before_total = jnp.zeros((1, HD), F32)
        for d in range(4):
            after = jnp.zeros((1, HD), F32)
            between = jnp.zeros((1, HD), F32)
            for e in range(4):
                if e == d:
                    continue
                later = at[e] > at[d]
                after = after + jnp.where(later, parts[e][h][1], 0.0)
                between = between + jnp.where(later & (at[e] < z), parts[e][h][1], 0.0)
            whole = whole + jnp.exp(after) * parts[d][h][0]
            whole_total = whole_total + parts[d][h][1]
            if d:
                earlier = at[d] < z
                before = before + jnp.where(earlier, jnp.exp(between), 0.0) * parts[d][h][0]
                before_total = before_total + jnp.where(earlier, parts[d][h][1], 0.0)
        prefix_ref[h] = before
        total_ref[h : h + 1, :] = before_total
        sums.append(whole)
        sum_totals.append(whole_total)
    write_message(message_ref, sums, sum_totals)


def inner_kernel(query_ref, key_ref, value_ref, decay_ref, out_ref):
    t, s = lower_ones()
    causal = s <= t
    for j in range(CHUNKS):
        col = chunk_cols(decay_ref, j, t, s)
        row = chunk_rows(decay_ref, j, t, s)
        for h in range(HEADS):
            scores = mm(
                query_ref[rows_of(j), cols_of(h)], key_ref[rows_of(j), cols_of(h)], ((1,), (1,))
            )
            spread = jnp.where(causal, col[:, h : h + 1] - row[h : h + 1, :], 0.0)
            near = jnp.where(causal, scores * jnp.exp(spread), 0.0).astype(BF)
            out_ref[rows_of(j), cols_of(h)] = mm(near, value_ref[rows_of(j), cols_of(h)])


def mix_kernel(
    place_ref,
    query_ref,
    decay_ref,
    inner_ref,
    states_ref,
    prefix_ref,
    total_ref,
    one_ref,
    two_ref,
    three_ref,
    gain_ref,
    out_ref,
):
    x = place_ref[1]
    t, s = lower_ones()
    earlier = [read_message(r) for r in (one_ref, two_ref, three_ref)]
    incoming = []
    for h in range(HEADS):
        far = earlier[2][h][0]
        far = earlier[1][h][0] + jnp.exp(earlier[1][h][1]) * far
        far = earlier[0][h][0] + jnp.exp(earlier[0][h][1]) * far
        incoming.append(prefix_ref[h] + jnp.exp(total_ref[h : h + 1, :]) * far)
    passed = [jnp.zeros((1, 1), F32) for _ in range(HEADS)]
    for j in range(CHUNKS):
        col = chunk_cols(decay_ref, j, t, s)
        place = lax.rem(j - x + 4, 4)
        for h in range(HEADS):
            within = col[:, h : h + 1]
            state = (states_ref[j, h] + jnp.exp(passed[h]) * incoming[h]).astype(BF)
            reach = (query_ref[rows_of(j), cols_of(h)].astype(F32) * jnp.exp(within)).astype(BF)
            mixed = inner_ref[rows_of(j), cols_of(h)] + mm(reach, state)
            scale = lax.rsqrt(jnp.mean(mixed * mixed, axis=1, keepdims=True) + 1e-06)
            out_ref[place, :, cols_of(h)] = (mixed * scale * gain_ref[:, cols_of(h)]).astype(BF)
            passed[h] = passed[h] + within[CHUNK - 1 : CHUNK, :]


def project_kernel(place_ref, one_ref, two_ref, three_ref, own_ref, weights_ref, part_ref, sent_ref):
    x = place_ref[1]
    for n in range(4):
        cols = slice(n * 512, (n + 1) * 512)
        total = mm(own_ref[...], weights_ref[x, :, cols])
        for d, rows_ref in ((1, one_ref), (2, two_ref), (3, three_ref)):
            total += mm(rows_ref[...], weights_ref[lax.rem(x - d + 4, 4), :, cols])
        part_ref[:, cols] = total
        sent_ref[:, cols] = total.astype(BF)


def route_kernel(place_ref, ids_ref, named_ref, selector_ref):
    x, core = place_ref[1], place_ref[2]
    lane = lax.broadcasted_iota(jnp.int32, (T_CHIP, ROUTED), 1)
    named = jnp.zeros((T_CHIP, ROUTED), F32)
    for k in range(TOPK):
        named = jnp.where(ids_ref[:, k : k + 1] == lane, 1.0, named)
    named_ref[...] = named
    t, s = lower_ones()
    before = jnp.where((s < t) & ((s < T_DEV) == (t < T_DEV)), 1.0, 0.0).astype(BF)
    ranks = mm(before, named.astype(BF))
    slot_lane = lax.broadcasted_iota(jnp.int32, (T_CHIP, 4 * SLOTS), 1)
    token = lax.broadcasted_iota(jnp.int32, (T_CHIP, 1), 0)
    wanted = jnp.full((T_CHIP, 4 * SLOTS), -1, jnp.int32)
    for d in range(4):
        mine = lane == 2 * lax.rem(x + d, 4) + core
        hit = jnp.sum(jnp.where(mine, named, 0.0), axis=1, keepdims=True) > 0.5
        rank = jnp.sum(jnp.where(mine, ranks, 0.0), axis=1, keepdims=True).astype(jnp.int32)
        slot = jnp.where(hit, rank + jnp.where(token < T_DEV, 0, CAP) + d * SLOTS, -1)
        inside = (slot_lane >= d * SLOTS) & (slot_lane < (d + 1) * SLOTS)
        wanted = jnp.where(inside, slot, wanted)
    selector_ref[...] = jnp.where(wanted == slot_lane, 1.0, 0.0).astype(BF)


def norm_kernel(
    place_ref,
    residual_ref,
    part_ref,
    other_ref,
    gain_ref,
    router_ref,
    named_ref,
    selector_ref,
    stream_ref,
    normed_ref,
    outgoing_ref,
    back_ref,
):
    x, core = place_ref[1], place_ref[2]
    stream = residual_ref[...].astype(F32) + part_ref[...] + other_ref[...].astype(F32)
    scale = lax.rsqrt(jnp.mean(stream * stream, axis=1, keepdims=True) + 1e-06)
    normed_ref[...] = (stream * scale * gain_ref[...]).astype(BF)
    outgoing_ref[...] = mm(selector_ref[...], normed_ref[...], ((0,), (0,))).astype(BF)
    stream_ref[...] = stream
    logits = mm(normed_ref[...], router_ref[...])
    affinity = named_ref[...] / (1.0 + jnp.exp(-logits))
    gates = affinity / jnp.sum(affinity, axis=1, keepdims=True)
    lane = lax.broadcasted_iota(jnp.int32, (T_CHIP, ROUTED), 1)
    slot_lane = lax.broadcasted_iota(jnp.int32, (T_CHIP, 4 * SLOTS), 1)
    back = selector_ref[...].astype(F32)
    weight = jnp.zeros((T_CHIP, 4 * SLOTS), F32)
    for d in range(4):
        mine = lane == 2 * lax.rem(x + d, 4) + core
        gate = jnp.sum(jnp.where(mine, gates, 0.0), axis=1, keepdims=True)
        inside = (slot_lane >= d * SLOTS) & (slot_lane < (d + 1) * SLOTS)
        weight = jnp.where(inside, gate, weight)
    back_ref[...] = back * weight


def expert_kernel(own_ref, one_ref, two_ref, three_ref, gate_ref, up_ref, down_ref, out_ref, rows_ref, hidden_ref):
    for d, ref in enumerate((own_ref, one_ref, two_ref, three_ref)):
        rows_ref[d * SLOTS : (d + 1) * SLOTS, :] = ref[...]
    for n in range(0, FF, 256):
        cols = slice(n, min(n + 256, FF))
        gate = mm(rows_ref[...], gate_ref[:, cols])
        up = mm(rows_ref[...], up_ref[:, cols])
        hidden_ref[:, cols] = (gate / (1.0 + jnp.exp(-gate)) * up).astype(BF)
    for n in range(4):
        cols = slice(n * 512, (n + 1) * 512)
        out_ref[:, cols] = mm(hidden_ref[...], down_ref[:, cols]).astype(BF)


def expert(pieces, gate_w, up_w, down_w):
    count = 4 * SLOTS
    return pl.pallas_call(
        expert_kernel,
        in_specs=[VM] * 7,
        out_specs=VM,
        out_shape=jax.ShapeDtypeStruct((count, D), BF),
        scratch_shapes=[pltpu.VMEM((count, D), BF), pltpu.VMEM((count, FF), BF)],
        compiler_params=pltpu.CompilerParams(vmem_limit_bytes=30 * 2**20),
        cost_estimate=pl.CostEstimate(
            flops=6 * count * D * FF, bytes_accessed=6 * D * FF, transcendentals=0
        ),
        name="expert",
    )(*pieces, gate_w, up_w, down_w)


def shared_kernel(*refs):
    rows_ref, pieces, (gate_ref, up_ref, down_ref) = refs[0], refs[1:8], refs[8:11]
    out_ref, hidden_ref, stack_ref = refs[11:]
    for i, piece in enumerate(pieces):
        rows = slice(i * HALF, (i + 1) * HALF)
        gate = mm(rows_ref[...], piece[:HALF, :], ((1,), (1,)))
        up = mm(rows_ref[...], piece[HALF : 2 * HALF, :], ((1,), (1,)))
        hidden_ref[:, rows] = (gate / (1.0 + jnp.exp(-gate)) * up).astype(BF)
        stack_ref[rows, :] = piece[2 * HALF :, :]
    rows = slice(7 * HALF, 8 * HALF)
    gate = mm(rows_ref[...], gate_ref[...], ((1,), (1,)))
    up = mm(rows_ref[...], up_ref[...], ((1,), (1,)))
    hidden_ref[:, rows] = (gate / (1.0 + jnp.exp(-gate)) * up).astype(BF)
    stack_ref[rows, :] = down_ref[...]
    for n in range(4):
        cols = slice(n * 512, (n + 1) * 512)
        out_ref[:, cols] = mm(hidden_ref[...], stack_ref[:, cols])


def shared(rows, weights):
    count = rows.shape[0]
    return pl.pallas_call(
        shared_kernel,
        in_specs=[VM] * 11,
        out_specs=VM,
        out_shape=jax.ShapeDtypeStruct((count, D), F32),
        scratch_shapes=[pltpu.VMEM((count, 8 * HALF), BF), pltpu.VMEM((8 * HALF, D), BF)],
        compiler_params=pltpu.CompilerParams(vmem_limit_bytes=30 * 2**20),
        cost_estimate=pl.CostEstimate(
            flops=2 * count * 24 * HALF * D, bytes_accessed=48 * HALF * D, transcendentals=0
        ),
        name="shared",
    )(rows, *weights)


def ring(step, count=4):
    return [(i, (i + step) % count) for i in range(count)]


def later(step, count=4):
    return [(i, i + step) for i in range(count - step)]


def swap_core(a):
    return lax.ppermute(a, "core", [(0, 1), (1, 0)])


def swap_pair(a):
    return lax.ppermute(a, "zl", [(0, 1), (1, 0)])


def swap_z(a):
    return lax.ppermute(a, Z, [(0, 3), (3, 0), (1, 2), (2, 1)])


def on_device(
    residual_in,
    queries,
    key_rows,
    values,
    log_decay,
    attn_gain,
    out_proj,
    ffn_gain,
    router,
    route_ids,
    w_gate,
    w_up,
    w_down,
    shared_gate,
    shared_up,
    shared_down,
):
    core = lax.axis_index("core")
    x = lax.axis_index("x")
    z = lax.axis_index(Z)
    place = jnp.stack([z, x, core]).astype(jnp.int32)

    def in_order(own, other):
        return jnp.where(
            core == 0, jnp.concatenate([own, other], 0), jnp.concatenate([other, own], 0)
        )

    def half_of(a, which):
        return lax.dynamic_slice_in_dim(a, which * T_DEV, T_DEV, 0)

    projection = lax.all_gather(out_proj, "x")

    first = core * SHIFT
    down_half = lax.dynamic_slice_in_dim(shared_down, first, HALF, 0)
    repeated = jnp.arange(HALF)[:, None] < jnp.where(core == 0, 0, 2 * HALF - SH)
    shared_own = jnp.concatenate(
        [
            lax.dynamic_slice_in_dim(shared_gate.T, first, HALF, 0),
            lax.dynamic_slice_in_dim(shared_up.T, first, HALF, 0),
            jnp.where(repeated, jnp.zeros_like(down_half), down_half),
        ],
        0,
    )
    near_low = lax.ppermute(shared_own, "y", ring(1))
    near_high = lax.ppermute(shared_own, "y", ring(3))
    pair_own = swap_pair(shared_own)

    states, message = pl.pallas_call(
        states_kernel,
        in_specs=[VM] * 3,
        out_specs=[VM] * 2,
        out_shape=[
            jax.ShapeDtypeStruct((CHUNKS, HEADS, HD, HD), F32),
            jax.ShapeDtypeStruct((MSG, HD), BF),
        ],
        name="states",
    )(key_rows, values, log_decay)
    along_z = [lax.ppermute(message, Z, ring(d)) for d in (1, 2, 3)]
    inner = pl.pallas_call(
        inner_kernel,
        in_specs=[VM] * 4,
        out_specs=VM,
        out_shape=jax.ShapeDtypeStruct((CHUNK * CHUNKS, HEADS * HD), F32),
        cost_estimate=pl.CostEstimate(flops=10**9, bytes_accessed=3 * 2**20, transcendentals=0),
        name="inner",
    )(queries, key_rows, values, log_decay)
    prefix, prefix_total, row_message = pl.pallas_call(
        row_kernel,
        in_specs=[SM] + [VM] * 4,
        out_specs=[VM] * 3,
        out_shape=[
            jax.ShapeDtypeStruct((HEADS, HD, HD), F32),
            jax.ShapeDtypeStruct((HEADS, HD), F32),
            jax.ShapeDtypeStruct((MSG, HD), BF),
        ],
        name="row_states",
    )(place, message, *along_z)
    low_there, high_there, pair_there, _ = lax.optimization_barrier(
        (near_low, near_high, pair_own, row_message)
    )
    pair_low = lax.ppermute(pair_there, "y", ring(1))
    far_own = lax.ppermute(high_there, "y", ring(3))
    pair_high = swap_pair(high_there)
    along_y = [lax.ppermute(row_message, "y", later(d)) for d in (1, 2, 3)]
    normed = pl.pallas_call(
        mix_kernel,
        in_specs=[SM] + [VM] * 10,
        out_specs=VM,
        out_shape=jax.ShapeDtypeStruct((4, T_CHIP, HEADS * HD), BF),
        name="mix",
    )(
        place,
        queries,
        log_decay,
        inner,
        states,
        prefix,
        prefix_total,
        *along_y,
        attn_gain.reshape(1, HEADS * HD),
    )

    pair_low_there, far_there, pair_high_there, _ = lax.optimization_barrier(
        (pair_low, far_own, pair_high, normed)
    )
    last_gate = swap_pair(far_there[:HALF])
    last_up = lax.ppermute(pair_low_there[HALF : 2 * HALF], "y", ring(1))
    last_down = lax.ppermute(pair_high_there[2 * HALF :], "y", ring(3))
    shared_weights = (
        shared_own,
        near_low,
        near_high,
        pair_own,
        pair_low,
        far_own,
        pair_high,
        last_gate,
        last_up,
        last_down,
    )

    ids = in_order(route_ids, swap_core(route_ids))
    named, selector = pl.pallas_call(
        route_kernel,
        in_specs=[SM, VM],
        out_specs=[VM] * 2,
        out_shape=[
            jax.ShapeDtypeStruct((T_CHIP, ROUTED), F32),
            jax.ShapeDtypeStruct((T_CHIP, 4 * SLOTS), BF),
        ],
        name="routes",
    )(place, ids)
    residual = in_order(residual_in, swap_core(residual_in))

    heads = [lax.ppermute(normed[d], "x", ring(d)) for d in (1, 2, 3)]
    part, part_sent = pl.pallas_call(
        project_kernel,
        in_specs=[SM] + [VM] * 5,
        out_specs=[VM] * 2,
        out_shape=[
            jax.ShapeDtypeStruct((T_CHIP, D), F32),
            jax.ShapeDtypeStruct((T_CHIP, D), BF),
        ],
        name="project",
    )(place, *heads, normed[0], projection)
    stream, normed_ffn, outgoing, weights_back = pl.pallas_call(
        norm_kernel,
        in_specs=[SM] + [VM] * 7,
        out_specs=[VM] * 4,
        out_shape=[
            jax.ShapeDtypeStruct((T_CHIP, D), F32),
            jax.ShapeDtypeStruct((T_CHIP, D), BF),
            jax.ShapeDtypeStruct((4 * SLOTS, D), BF),
            jax.ShapeDtypeStruct((T_CHIP, 4 * SLOTS), F32),
        ],
        name="norm",
    )(
        place,
        residual,
        part,
        swap_core(part_sent),
        ffn_gain.reshape(1, D),
        router,
        named,
        selector,
    )

    sent = [outgoing[d * SLOTS : (d + 1) * SLOTS] for d in range(4)]
    arrived = [sent[0]] + [lax.ppermute(sent[d], "x", ring(d)) for d in (1, 2, 3)]

    partner_own = swap_z(half_of(normed_ffn, core))
    partner_rows = in_order(partner_own, swap_core(partner_own))

    result = expert(arrived, w_gate[0], w_up[0], w_down[0])
    returned = [result[:SLOTS]] + [
        lax.ppermute(result[d * SLOTS : (d + 1) * SLOTS], "x", ring(4 - d)) for d in (1, 2, 3)
    ]

    partner_part = shared(partner_rows, shared_weights)
    partner_sum = half_of(partner_part, core) + swap_core(
        half_of(partner_part, 1 - core).astype(BF)
    ).astype(F32)
    from_partner = swap_z(partner_sum.astype(BF)).astype(F32)
    own_part = shared(normed_ffn, shared_weights)

    high = weights_back.astype(BF)
    low = (weights_back - high.astype(F32)).astype(BF)
    back = jnp.concatenate(returned, 0)
    both = own_part + mm(high, back) + mm(low, back)
    other = swap_core(half_of(both, 1 - core).astype(BF)).astype(F32)
    return (half_of(stream, core) + half_of(both, core) + other + from_partner).astype(BF)


def solution(mesh):
    fine = Mesh(mesh.devices.reshape(4, 2, 2, 4, 2), ("y", "zh", "zl", "x", "core"))
    ctx = ("y", "zh", "zl")
    exp = ("x", "core")
    return jax.shard_map(
        on_device,
        mesh=fine,
        in_specs=(
            P(ctx + exp, None),
            P(ctx, exp),
            P(ctx, exp),
            P(ctx, exp),
            P(exp, ctx),
            P(exp),
            P(exp, None),
            P(),
            P(),
            P(ctx + exp, None),
            P(exp, None, None),
            P(exp, None, None),
            P(exp, None, None),
            P(None, ctx),
            P(None, ctx),
            P(ctx, None),
        ),
        out_specs=P(ctx + exp, None),
        check_vma=False,
    )
```

time: 339 us -> 199 us (0.59)
  waiting for transfers between devices: 171 us -> 54.3 us
  blocking collectives: 52.7 us -> 0 us
  Pallas kernels: 0 us -> 49.1 us
  matrix products: 49.4 us -> 0.86 us
  starting transfers between devices: 4.72 us -> 49.4 us
  local copies, waits for them, and re-layouts: 34.4 us -> 22 us
    reduce_scatter x2 -> x0, waiting for transfers between devices: 81.5 us -> none  [the longest x1 49.5 us: on_device(): lax.psum_scatter(jnp.dot(normed, out_proj, preferred_element_type=jnp.flo...]
    all_gather x2 -> x1, waiting for transfers between devices: 78 us -> 0.01 us  [on_device(): projection = lax.all_gather(out_proj, 'x')]
    ppermute x0 -> x32, waiting for transfers between devices: none -> 53.6 us  [the longest x3 14 us: on_device(): along_y = [lax.ppermute(row_message, 'y', later(d)) for d in (1, 2, 3)]]
    ppermute x0 -> x32, starting transfers between devices: none -> 49.3 us  [the longest x6 9.99 us: swap_core(): return lax.ppermute(a, 'core', [(0, 1), (1, 0)])]
    pallas_call x0 -> x10, Pallas kernels: none -> 49.1 us  [the longest x2 13.9 us: shared(): pl.pallas_call(shared_kernel, in_specs=[VM] * 11, out_specs=VM, out_shape...]
    dot_general x15 -> x2, matrix products: 49.4 us -> 0.86 us  [mm(): return lax.dot_general(a, b, (dims, ((), ())), preferred_element_type=F32)]
    unnamed x1 -> x0, blocking collectives: 35.8 us -> none
    dynamic_update_slice x4 -> x0, local copies, waits for them, and re-layouts: 21.7 us -> none  [head_blocks(): lax.scan(advance, initial, (queries.reshape(block_shape), key_rows.reshap...]
  transfers between devices with their start and end apart: 5 -> 33, of which waited for: 5 -> 14; matrix products, arithmetic and copies ran while one was open for 6% -> 9% of each run, Pallas kernels for 0% -> 21%
where the time goes in v1:
time: 199 us; the launch traced here: 198 us
  waiting for transfers between devices  54.3 us (27%)
  starting transfers between devices  49.4 us (25%)
  Pallas kernels  49.1 us (25%)
  local copies, waits for them, and re-layouts  22 us (11%)
  between operations  13.7 us (7%)
  other arithmetic  8.98 us (5%)
    ppermute x3, waiting for transfers between devices, on_device(): along_y = [lax.ppermute(row_message, 'y', later(d)) for d in (1, 2, 3)]  14 us
    pallas_call x2, Pallas kernels, shared(): pl.pallas_call(shared_kernel, in_specs=[VM] * 11, out_specs=VM, out_shape...  13.9 us
    unnamed x39, local copies, waits for them, and re-layouts  13.3 us
    ppermute x2, waiting for transfers between devices, swap_z(): return lax.ppermute(a, Z, [(0, 3), (3, 0), (1, 2), (2, 1)])  12.5 us
    ppermute x1, waiting for transfers between devices, on_device(): pair_low = lax.ppermute(pair_there, 'y', ring(1))  10.5 us
    ppermute x6, starting transfers between devices, swap_core(): return lax.ppermute(a, 'core', [(0, 1), (1, 0)])  9.99 us
    ppermute x3, starting transfers between devices, on_device(): along_y = [lax.ppermute(row_message, 'y', later(d)) for d in (1, 2, 3)]  9.05 us
    ppermute x3, starting transfers between devices, on_device(): along_z = [lax.ppermute(message, Z, ring(d)) for d in (1, 2, 3)]  6.5 us
  transfers between devices with their start and end apart: 33, of which 14 were waited for; matrix products, arithmetic and copies ran while one was open for 9% of the time, Pallas kernels for 21%

profile of v1, /device:TPU:1, one launch (start us, length us, event | category | flops | bytes accessed | tf_op | source)
XLA Modules:
  0.0 198.2 jit_solution(3763418904387555382)
XLA Ops:
  6.5 0.7 all-gather.3.cloned.1.call-update
  7.3 5.0 %states.1 = (f32[4,2,128,128]{3,2,1,0:T(8,128)}, bf16[272,128]{1,0:T(8,128)(2,1)}) custom-call(bf16[1024,256]{1,0:T(8,128)(2,1)} %key_ref.3, bf16[1024,256]{1,0:T(8,128)(2,1)} %value_ref.3, f32[2,1024]{1,0:T(2,128)} %decay_ref.5), custom_call_target="tpu_custom_call" | custom-call | tf_op jit(solution)/shard_map/states/pallas_call | solution.py:398
  12.3 2.5 %collective-permute-start.1 = (bf16[272,128]{1,0:T(8,128)(2,1)}, bf16[272,128]{1,0:T(8,128)(2,1)S(1)}, u32[]{:S(2)}, u32[]{:S(2)}) collective-permute-start(bf16[272,128]{1,0:T(8,128)(2,1)} %get-tuple-element.24.own_ref), channel_id=1, source_target_pairs={{0,8},{8,16},{16,24},{24,0},{1,9},{9,17},{17,25},{25,1},{2,10},{10... | collective-permute-start | bytes 208904 | tf_op jit(solution)/shard_map/ppermute | solution.py:408
  14.8 3.3 %collective-permute-start.2 = (bf16[272,128]{1,0:T(8,128)(2,1)}, bf16[272,128]{1,0:T(8,128)(2,1)S(1)}, u32[]{:S(2)}, u32[]{:S(2)}) collective-permute-start(bf16[272,128]{1,0:T(8,128)(2,1)} %get-tuple-element.24.own_ref), channel_id=1, source_target_pairs={{0,16},{8,24},{16,0},{24,8},{1,17},{9,25},{17,1},{25,9},{2,18},{10... | collective-permute-start | bytes 208904 | tf_op jit(solution)/shard_map/ppermute | solution.py:408
  18.1 0.7 collective-permute-start.3
  19.0 0.7 pad_add_fusion.2.place_ref
  19.7 1.3 collective-permute-done.2.two_ref
  22.4 1.8 row_states.1
  24.2 3.8 %collective-permute-start.4 = (bf16[272,128]{1,0:T(8,128)(2,1)}, bf16[272,128]{1,0:T(8,128)(2,1)}, u32[]{:S(2)}, u32[]{:S(2)}) collective-permute-start(bf16[272,128]{1,0:T(8,128)(2,1)} %get-tuple-element.27), channel_id=1, source_target_pairs={{0,32},{32,64},{64,96},{1,33},{33,65},{65,97},{2,34},{34,66},{66,9... | collective-permute-start | bytes 208904 | tf_op jit(solution)/shard_map/ppermute | solution.py:434
  28.1 0.8 collective-permute-start.12
  28.8 2.0 %collective-permute-start.13 = (bf16[288,2048]{1,0:T(8,128)(2,1)S(1)}, bf16[288,2048]{1,0:T(8,128)(2,1)}, u32[]{:S(2)}, u32[]{:S(2)}) collective-permute-start(bf16[288,2048]{1,0:T(8,128)(2,1)S(1)} %pad_maximum_fusion.refs_1_), channel_id=1, source_target_pairs={{0,96},{32,0},{64,32},{96,64},{1,97},{33,1},{65,33},{97,65},{2,98}... | collective-permute-start | bytes 3538952 | tf_op jit(solution)/shard_map/ppermute | solution.py:395
  31.1 3.3 %collective-permute-start.5 = (bf16[272,128]{1,0:T(8,128)(2,1)}, bf16[272,128]{1,0:T(8,128)(2,1)}, u32[]{:S(2)}, u32[]{:S(2)}) collective-permute-start(bf16[272,128]{1,0:T(8,128)(2,1)} %get-tuple-element.27), channel_id=1, source_target_pairs={{0,64},{32,96},{1,65},{33,97},{2,66},{34,98},{3,67},{35,99},{4,68}... | collective-permute-start | bytes 208904 | tf_op jit(solution)/shard_map/ppermute | solution.py:434
  34.4 1.9 collective-permute-start.6
  36.3 5.4 %inner.1.inner_ref = f32[1024,256]{1,0:T(8,128)} custom-call(bf16[1024,256]{1,0:T(8,128)(2,1)} %query_ref.3, bf16[1024,256]{1,0:T(8,128)(2,1)} %key_ref.3, bf16[1024,256]{1,0:T(8,128)(2,1)} %value_ref.3, f32[2,1024]{1,0:T(2,128)} %decay_ref.5), custom_call_target="tpu_custom_call" | custom-call | flops 1000000000 | bytes 3145728 | tf_op jit(solution)/shard_map/inner/pallas_call | solution.py:409
  41.7 13.1 %collective-permute-done.5.two_ref = bf16[272,128]{1,0:T(8,128)(2,1)} collective-permute-done((bf16[272,128]{1,0:T(8,128)(2,1)}, bf16[272,128]{1,0:T(8,128)(2,1)}, u32[]{:S(2)}, u32[]{:S(2)}) %collective-permute-start.5) | collective-permute-done | bytes 69664 | tf_op jit(solution)/shard_map/ppermute | solution.py:434
  54.8 1.0 collective-permute-done.6.three_ref
  55.8 5.2 %mix.1 = bf16[4,256,256]{2,1,0:T(8,128)(2,1)} custom-call(s32[3]{0:T(128)} %pad_add_fusion.2.place_ref, bf16[1024,256]{1,0:T(8,128)(2,1)} %query_ref.3, f32[2,1024]{1,0:T(2,128)} %decay_ref.5, f32[1024,256]{1,0:T(8,128)} %inner.1.inner_ref, f32[4,2,128,128]{3,2,1,0:T(8,128)} %get-tuple-element.23.states_ref, f32[2,128,128]{2,1,0:T(8,128)} %get-tuple-element.25.prefix_ref, ...), custom_call_target="tpu_custom_call" | custom-call | tf_op jit(solution)/shard_map/mix/pallas_call | solution.py:435
  61.0 1.8 slice_bitcast_fusion
  62.8 1.2 collective-permute-start.7
  64.0 2.4 %collective-permute-start.8 = (bf16[256,256]{1,0:T(8,128)(2,1)S(1)}, bf16[256,256]{1,0:T(8,128)(2,1)}, u32[]{:S(2)}, u32[]{:S(2)}) collective-permute-start(bf16[256,256]{1,0:T(8,128)(2,1)S(1)} %get-tuple-element.51), channel_id=1, source_target_pairs={{0,4},{2,6},{4,0},{6,2},{1,5},{3,7},{5,1},{7,3},{8,12},{10,14},{12... | collective-permute-start | bytes 393224 | tf_op jit(solution)/shard_map/ppermute | solution.py:485
  66.4 1.5 collective-permute-done.7.one_ref
  67.9 1.3 collective-permute-start.9
  69.2 1.1 collective-permute-done.8.two_ref
  70.3 1.8 collective-permute-done.9.three_ref
  72.1 5.4 %project.1 = (f32[256,2048]{1,0:T(8,128)}, bf16[256,2048]{1,0:T(8,128)(2,1)}) custom-call(s32[3]{0:T(128)} %pad_add_fusion.2.place_ref, bf16[256,256]{1,0:T(8,128)(2,1)} %collective-permute-done.7.one_ref, bf16[256,256]{1,0:T(8,128)(2,1)} %collective-permute-done.8.two_ref, bf16[256,256]{1,0:T(8,128)(2,1)} %collective-permute-done.9.three_ref, ...), custom_call_target="tpu_custom_call" | custom-call | tf_op jit(solution)/shard_map/project/pallas_call | solution.py:486
  77.6 6.3 %collective-permute-start.10 = (bf16[256,2048]{1,0:T(8,128)(2,1)}, bf16[256,2048]{1,0:T(8,128)(2,1)}, u32[]{:S(2)}, u32[]{:S(2)}) collective-permute-start(bf16[256,2048]{1,0:T(8,128)(2,1)} %get-tuple-element.29), channel_id=1, source_target_pairs={{0,1},{1,0},{2,3},{3,2},{4,5},{5,4},{6,7},{7,6},{8,9},{9,8},{10,11... | collective-permute-start | bytes 3145736 | tf_op jit(solution)/shard_map/ppermute | solution.py:339
  84.0 2.1 %collective-permute-done.11 = s32[128,6]{0,1:T(8,128)S(1)} collective-permute-done((s32[128,6]{0,1:T(8,128)S(1)}, s32[128,6]{0,1:T(8,128)S(1)}, u32[]{:S(2)}, u32[]{:S(2)}) %collective-permute-start.11) | collective-permute-done | bytes 3104 | tf_op jit(solution)/shard_map/ppermute | solution.py:339
  86.8 2.0 copy.23.router_ref
  88.7 0.8 pad_add_fusion.1
  89.5 0.8 copy.21
  90.3 0.8 copy.22
  91.1 1.1 copy-done.3
  92.2 1.0 copy-done.5
  93.3 3.4 %collective-permute-start.16 = (bf16[288,2048]{1,0:T(8,128)(2,1)}, bf16[288,2048]{1,0:T(8,128)(2,1)S(1)}, u32[]{:S(2)}, u32[]{:S(2)}) collective-permute-start(bf16[288,2048]{1,0:T(8,128)(2,1)} %collective-permute-done.13.refs_3_), channel_id=1, source_target_pairs={{0,96},{32,0},{64,32},{96,64},{1,97},{33,1},{65,33},{97,65},{2,98}... | collective-permute-start | bytes 3538952 | tf_op jit(solution)/shard_map/ppermute | solution.py:432
  96.9 1.6 broadcast_select_fusion.ids_ref
  98.5 2.3 %routes.1 = (f32[256,64]{1,0:T(8,128)}, bf16[256,192]{1,0:T(8,128)(2,1)}) custom-call(s32[3]{0:T(128)} %pad_add_fusion.2.place_ref, s32[256,6]{1,0:T(8,128)} %broadcast_select_fusion.ids_ref), custom_call_target="tpu_custom_call" | custom-call | tf_op jit(solution)/shard_map/routes/pallas_call | solution.py:473
  100.8 3.0 %maximum_select_fusion.residual_ref = bf16[256,2048]{1,0:T(8,128)(2,1)} fusion(bf16[128,2048]{1,0:T(8,128)(2,1)} %collective-permute-done, bf16[128,2048]{1,0:T(8,128)(2,1)} %param.16, pred[]{:T(512)S(6)} %eq.2), kind=kLoop, calls=%fused_computation.2 | loop fusion | flops 4718592 | bytes 2097153 | tf_op jit(solution)/shard_map/jit(_where)/select_n | solution.py:374
  103.8 4.9 %norm.1 = (f32[256,2048]{1,0:T(8,128)}, bf16[256,2048]{1,0:T(8,128)(2,1)}, bf16[192,2048]{1,0:T(8,128)(2,1)}, f32[256,192]{1,0:T(8,128)}) custom-call(s32[3]{0:T(128)} %pad_add_fusion.2.place_ref, bf16[256,2048]{1,0:T(8,128)(2,1)} %maximum_select_fusion.residual_ref, f32[256,2048]{1,0:T(8,128)} %get-tuple-element.28.part_ref, ...), custom_call_target="tpu_custom_call" | custom-call | tf_op jit(solution)/shard_map/norm/pallas_call | solution.py:496
  108.7 1.9 constant_dynamic-slice_fusion
  110.6 1.8 collective-permute-start.28
  112.4 2.1 %fusion.7 = (bf16[48,2048]{1,0:T(8,128)(2,1)}, bf16[48,2048]{1,0:T(8,128)(2,1)}, bf16[48,2048]{1,0:T(8,128)(2,1)}, bf16[48,2048]{1,0:T(8,128)(2,1)}) fusion(bf16[192,2048]{1,0:T(8,128)(2,1)} %get-tuple-element.40), kind=kLoop, calls=%fused_computation.30 | loop fusion | bytes 1572864 | tf_op jit(solution)/shard_map/slice | solution.py:518
  114.5 10.5 %collective-permute-done.15.refs_5_ = bf16[288,2048]{1,0:T(8,128)(2,1)} collective-permute-done((bf16[288,2048]{1,0:T(8,128)(2,1)}, bf16[288,2048]{1,0:T(8,128)(2,1)}, u32[]{:S(2)}, u32[]{:S(2)}) %collective-permute-start.15) | collective-permute-done | bytes 1179680 | tf_op jit(solution)/shard_map/ppermute | solution.py:431
  125.0 1.5 collective-permute-start.22
  126.5 1.0 collective-permute-start.23
  127.5 1.3 collective-permute-start.18
  128.8 1.0 slice.50
  130.0 1.4 collective-permute-done.22.two_ref
  131.3 1.3 collective-permute-start.20
  132.6 3.5 %collective-permute-done.23.three_ref = bf16[48,2048]{1,0:T(8,128)(2,1)} collective-permute-done((bf16[48,2048]{1,0:T(8,128)(2,1)}, bf16[48,2048]{1,0:T(8,128)(2,1)}, u32[]{:S(2)}, u32[]{:S(2)}) %collective-permute-start.23) | collective-permute-done | bytes 196640 | tf_op jit(solution)/shard_map/ppermute | solution.py:519
  136.1 2.6 %copy-done = bf16[1,2048,1408]{2,1,0:T(8,128)(2,1)S(1)} copy-done((bf16[1,2048,1408]{2,1,0:T(8,128)(2,1)S(1)}, bf16[1,2048,1408]{2,1,0:T(8,128)(2,1)}, u32[]{:S(2)}) %copy-start) | copy-done | bytes 5767192
  138.8 2.6 %copy-done.1 = bf16[1,2048,1408]{2,1,0:T(8,128)(2,1)S(1)} copy-done((bf16[1,2048,1408]{2,1,0:T(8,128)(2,1)S(1)}, bf16[1,2048,1408]{2,1,0:T(8,128)(2,1)}, u32[]{:S(2)}) %copy-start.1) | copy-done | bytes 5767192
  141.4 2.6 %copy-done.2 = bf16[1,1408,2048]{2,1,0:T(8,128)(2,1)S(1)} copy-done((bf16[1,1408,2048]{2,1,0:T(8,128)(2,1)S(1)}, bf16[1,1408,2048]{2,1,0:T(8,128)(2,1)}, u32[]{:S(2)}) %copy-start.2) | copy-done | bytes 5767192
  144.0 5.1 %expert.1 = bf16[192,2048]{1,0:T(8,128)(2,1)S(1)} custom-call(bf16[48,2048]{1,0:T(8,128)(2,1)S(1)} %copy-done.8, bf16[48,2048]{1,0:T(8,128)(2,1)} %collective-permute-done.21.one_ref, bf16[48,2048]{1,0:T(8,128)(2,1)} %collective-permute-done.22.two_ref, bf16[48,2048]{1,0:T(8,128)(2,1)} %collective-permute-done.23.three_ref, bf16[2048,1408]{1,0:T(8,128)(2,1)S(1)} %bitcast.21, ...), custom_call_target="tpu_custom_call" | custom-call | flops 3321888768 | bytes 17301504 | tf_op jit(solution)/shard_map/expert/pallas_call | solution.py:281
  149.2 2.4 %collective-permute-start.29 = (bf16[128,2048]{1,0:T(8,128)(2,1)}, bf16[128,2048]{1,0:T(8,128)(2,1)S(1)}, u32[]{:S(2)}, u32[]{:S(2)}) collective-permute-start(bf16[128,2048]{1,0:T(8,128)(2,1)} %collective-permute-done.28), channel_id=1, source_target_pairs={{0,1},{1,0},{2,3},{3,2},{4,5},{5,4},{6,7},{7,6},{8,9},{9,8},{10,11... | collective-permute-start | bytes 1572872 | tf_op jit(solution)/shard_map/ppermute | solution.py:339
  151.8 3.2 %collective-permute-start.25 = (bf16[48,2048]{1,0:T(8,128)(2,1)S(1)}, bf16[48,2048]{1,0:T(8,128)(2,1)S(1)}, u32[]{:S(2)}, u32[]{:S(2)}) collective-permute-start(bf16[48,2048]{1,0:T(8,128)(2,1)S(1)} %get-tuple-element.43), channel_id=1, source_target_pairs={{0,4},{2,6},{4,0},{6,2},{1,5},{3,7},{5,1},{7,3},{8,12},{10,14},{12... | collective-permute-start | bytes 589832 | tf_op jit(solution)/shard_map/ppermute | solution.py:526
  155.0 7.0 %shared.2 = f32[256,2048]{1,0:T(8,128)S(1)} custom-call(bf16[256,2048]{1,0:T(8,128)(2,1)S(1)} %copy-done.7, bf16[288,2048]{1,0:T(8,128)(2,1)S(1)} %pad_maximum_fusion.refs_1_, bf16[288,2048]{1,0:T(8,128)(2,1)S(1)} %copy-done.4, bf16[288,2048]{1,0:T(8,128)(2,1)} %collective-permute-done.13.refs_3_, bf16[288,2048]{1,0:T(8,128)(2,1)S(1)} %copy-done.6, ...), custom_call_target="tpu_custom_call" | custom-call | flops 2415919104 | bytes 9437184 | tf_op jit(solution)/shard_map/shared/pallas_call | solution.py:316
  162.0 2.2 %collective-permute-done.25 = bf16[48,2048]{1,0:T(8,128)(2,1)S(1)} collective-permute-done((bf16[48,2048]{1,0:T(8,128)(2,1)S(1)}, bf16[48,2048]{1,0:T(8,128)(2,1)S(1)}, u32[]{:S(2)}, u32[]{:S(2)}) %collective-permute-start.25) | collective-permute-done | bytes 196640 | tf_op jit(solution)/shard_map/ppermute | solution.py:526
  164.7 1.5 maximum_select_fusion.1.refs_0_
  166.3 6.9 %shared.3 = f32[256,2048]{1,0:T(8,128)S(1)} custom-call(bf16[256,2048]{1,0:T(8,128)(2,1)S(1)} %maximum_select_fusion.1.refs_0_, bf16[288,2048]{1,0:T(8,128)(2,1)S(1)} %pad_maximum_fusion.refs_1_, bf16[288,2048]{1,0:T(8,128)(2,1)S(1)} %copy-done.4, bf16[288,2048]{1,0:T(8,128)(2,1)} %collective-permute-done.13.refs_3_, bf16[288,2048]{1,0:T(8,128)(2,1)S(1)} %copy-done.6, ...), custom_call_target="tpu_custom_call" | custom-call | flops 2415919104 | bytes 9437184 | tf_op jit(solution)/shard_map/shared/pallas_call | solution.py:316
  173.3 0.9 collective-permute-start.30
  174.8 0.9 collective-permute-done.30
  175.9 1.9 collective-permute-start.31
  177.8 12.5 %collective-permute-done.31 = bf16[128,2048]{1,0:T(8,128)(2,1)S(1)} collective-permute-done((bf16[128,2048]{1,0:T(8,128)(2,1)S(1)}, bf16[128,2048]{1,0:T(8,128)(2,1)S(1)}, u32[]{:S(2)}, u32[]{:S(2)}) %collective-permute-start.31) | collective-permute-done | bytes 524320 | tf_op jit(solution)/shard_map/ppermute | solution.py:347
  190.3 1.1 add_convert_fusion
  (76 shorter events, 4.5 us)
Async XLA Ops:
  6.5 12.3 %copy-start.12 = (bf16[2048,176]{0,1:T(8,128)(2,1)S(1)}, bf16[2048,176]{0,1:T(8,128)(2,1)}, u32[]{:S(2)}) copy-start(bf16[2048,176]{0,1:T(8,128)(2,1)} %param.30) | copy-start | bytes 2162692
  6.5 12.3 %copy-start.13 = (bf16[2048,176]{0,1:T(8,128)(2,1)S(1)}, bf16[2048,176]{0,1:T(8,128)(2,1)}, u32[]{:S(2)}) copy-start(bf16[2048,176]{0,1:T(8,128)(2,1)} %param.29) | copy-start | bytes 2162692
  6.5 12.4 %copy-start.11 = (bf16[176,2048]{1,0:T(8,128)(2,1)S(1)}, bf16[176,2048]{1,0:T(8,128)(2,1)}, u32[]{:S(2)}) copy-start(bf16[176,2048]{1,0:T(8,128)(2,1)} %param.31) | copy-start | bytes 2162692
  6.5 65.6 %all-gather.3.cloned.1.call-start = ((), (), s32[]{:S(2)}) async-start(), calls=%async_computation | async-start | bytes 5242880 | tf_op jit(solution)/shard_map/all_gather | solution.py:381
  12.3 7.4 %collective-permute-start.1 = (bf16[272,128]{1,0:T(8,128)(2,1)}, bf16[272,128]{1,0:T(8,128)(2,1)S(1)}, u32[]{:S(2)}, u32[]{:S(2)}) collective-permute-start(bf16[272,128]{1,0:T(8,128)(2,1)} %get-tuple-element.24.own_ref), channel_id=1, source_target_pairs={{0,8},{8,16},{16,24},{24,0},{1,9},{9,17},{17,25},{25,1},{2,10},{10... | collective-permute-start | bytes 208904 | tf_op jit(solution)/shard_map/ppermute | solution.py:408
  14.8 6.3 %collective-permute-start.2 = (bf16[272,128]{1,0:T(8,128)(2,1)}, bf16[272,128]{1,0:T(8,128)(2,1)S(1)}, u32[]{:S(2)}, u32[]{:S(2)}) collective-permute-start(bf16[272,128]{1,0:T(8,128)(2,1)} %get-tuple-element.24.own_ref), channel_id=1, source_target_pairs={{0,16},{8,24},{16,0},{24,8},{1,17},{9,25},{17,1},{25,9},{2,18},{10... | collective-permute-start | bytes 208904 | tf_op jit(solution)/shard_map/ppermute | solution.py:408
  18.1 3.7 %collective-permute-start.3 = (bf16[272,128]{1,0:T(8,128)(2,1)}, bf16[272,128]{1,0:T(8,128)(2,1)S(1)}, u32[]{:S(2)}, u32[]{:S(2)}) collective-permute-start(bf16[272,128]{1,0:T(8,128)(2,1)} %get-tuple-element.24.own_ref), channel_id=1, source_target_pairs={{0,24},{8,0},{16,8},{24,16},{1,25},{9,1},{17,9},{25,17},{2,26},{10... | collective-permute-start | bytes 208904 | tf_op jit(solution)/shard_map/ppermute | solution.py:408
  19.7 2.0 %copy-start.14 = (bf16[272,128]{1,0:T(8,128)(2,1)}, bf16[272,128]{1,0:T(8,128)(2,1)S(1)}, u32[]{:S(2)}) copy-start(bf16[272,128]{1,0:T(8,128)(2,1)S(1)} %collective-permute-done.1.one_ref) | copy-start | bytes 208900
  21.1 0.7 copy-start.15
  21.7 0.6 copy-start.16
  24.2 10.2 %collective-permute-start.4 = (bf16[272,128]{1,0:T(8,128)(2,1)}, bf16[272,128]{1,0:T(8,128)(2,1)}, u32[]{:S(2)}, u32[]{:S(2)}) collective-permute-start(bf16[272,128]{1,0:T(8,128)(2,1)} %get-tuple-element.27), channel_id=1, source_target_pairs={{0,32},{32,64},{64,96},{1,33},{33,65},{65,97},{2,34},{34,66},{66,9... | collective-permute-start | bytes 208904 | tf_op jit(solution)/shard_map/ppermute | solution.py:434
  28.1 63.0 %collective-permute-start.12 = (bf16[288,2048]{1,0:T(8,128)(2,1)S(1)}, bf16[288,2048]{1,0:T(8,128)(2,1)S(1)}, u32[]{:S(2)}, u32[]{:S(2)}) collective-permute-start(bf16[288,2048]{1,0:T(8,128)(2,1)S(1)} %pad_maximum_fusion.refs_1_), channel_id=1, source_target_pairs={{0,32},{32,64},{64,96},{96,0},{1,33},{33,65},{65,97},{97,1},{2,34}... | collective-permute-start | bytes 3538952 | tf_op jit(solution)/shard_map/ppermute | solution.py:394
  28.8 63.4 %collective-permute-start.13 = (bf16[288,2048]{1,0:T(8,128)(2,1)S(1)}, bf16[288,2048]{1,0:T(8,128)(2,1)}, u32[]{:S(2)}, u32[]{:S(2)}) collective-permute-start(bf16[288,2048]{1,0:T(8,128)(2,1)S(1)} %pad_maximum_fusion.refs_1_), channel_id=1, source_target_pairs={{0,96},{32,0},{64,32},{96,64},{1,97},{33,1},{65,33},{97,65},{2,98}... | collective-permute-start | bytes 3538952 | tf_op jit(solution)/shard_map/ppermute | solution.py:395
  30.8 61.4 %collective-permute-start.14 = (bf16[288,2048]{1,0:T(8,128)(2,1)S(1)}, bf16[288,2048]{1,0:T(8,128)(2,1)S(1)}, u32[]{:S(2)}, u32[]{:S(2)}) collective-permute-start(bf16[288,2048]{1,0:T(8,128)(2,1)S(1)} %pad_maximum_fusion.refs_1_), channel_id=1, source_target_pairs={{0,8},{8,0},{1,9},{9,1},{2,10},{10,2},{3,11},{11,3},{4,12},{12,4},... | collective-permute-start | bytes 3538952 | tf_op jit(solution)/shard_map/ppermute | solution.py:343
  31.1 23.7 %collective-permute-start.5 = (bf16[272,128]{1,0:T(8,128)(2,1)}, bf16[272,128]{1,0:T(8,128)(2,1)}, u32[]{:S(2)}, u32[]{:S(2)}) collective-permute-start(bf16[272,128]{1,0:T(8,128)(2,1)} %get-tuple-element.27), channel_id=1, source_target_pairs={{0,64},{32,96},{1,65},{33,97},{2,66},{34,98},{3,67},{35,99},{4,68}... | collective-permute-start | bytes 208904 | tf_op jit(solution)/shard_map/ppermute | solution.py:434
  34.4 21.4 %collective-permute-start.6 = (bf16[272,128]{1,0:T(8,128)(2,1)}, bf16[272,128]{1,0:T(8,128)(2,1)}, u32[]{:S(2)}, u32[]{:S(2)}) collective-permute-start(bf16[272,128]{1,0:T(8,128)(2,1)} %get-tuple-element.27), channel_id=1, source_target_pairs={{0,96},{1,97},{2,98},{3,99},{4,100},{5,101},{6,102},{7,103},{8,104... | collective-permute-start | bytes 208904 | tf_op jit(solution)/shard_map/ppermute | solution.py:434
  62.8 5.1 %collective-permute-start.7 = (bf16[256,256]{1,0:T(8,128)(2,1)S(1)}, bf16[256,256]{1,0:T(8,128)(2,1)}, u32[]{:S(2)}, u32[]{:S(2)}) collective-permute-start(bf16[256,256]{1,0:T(8,128)(2,1)S(1)} %get-tuple-element.52), channel_id=1, source_target_pairs={{0,2},{2,4},{4,6},{6,0},{1,3},{3,5},{5,7},{7,1},{8,10},{10,12},{12... | collective-permute-start | bytes 393224 | tf_op jit(solution)/shard_map/ppermute | solution.py:485
  64.0 6.3 %collective-permute-start.8 = (bf16[256,256]{1,0:T(8,128)(2,1)S(1)}, bf16[256,256]{1,0:T(8,128)(2,1)}, u32[]{:S(2)}, u32[]{:S(2)}) collective-permute-start(bf16[256,256]{1,0:T(8,128)(2,1)S(1)} %get-tuple-element.51), channel_id=1, source_target_pairs={{0,4},{2,6},{4,0},{6,2},{1,5},{3,7},{5,1},{7,3},{8,12},{10,14},{12... | collective-permute-start | bytes 393224 | tf_op jit(solution)/shard_map/ppermute | solution.py:485
  67.9 4.2 %collective-permute-start.9 = (bf16[256,256]{1,0:T(8,128)(2,1)S(1)}, bf16[256,256]{1,0:T(8,128)(2,1)}, u32[]{:S(2)}, u32[]{:S(2)}) collective-permute-start(bf16[256,256]{1,0:T(8,128)(2,1)S(1)} %get-tuple-element.50), channel_id=1, source_target_pairs={{0,6},{2,0},{4,2},{6,4},{1,7},{3,1},{5,3},{7,5},{8,14},{10,8},{12,... | collective-permute-start | bytes 393224 | tf_op jit(solution)/shard_map/ppermute | solution.py:485
  72.1 11.8 %copy-start.17 = (s32[128,6]{0,1:T(8,128)S(1)}, s32[128,6]{0,1:T(8,128)}, u32[]{:S(2)}) copy-start(s32[128,6]{0,1:T(8,128)} %param.25) | copy-start | bytes 9220
  77.6 26.2 %collective-permute-start.10 = (bf16[256,2048]{1,0:T(8,128)(2,1)}, bf16[256,2048]{1,0:T(8,128)(2,1)}, u32[]{:S(2)}, u32[]{:S(2)}) collective-permute-start(bf16[256,2048]{1,0:T(8,128)(2,1)} %get-tuple-element.29), channel_id=1, source_target_pairs={{0,1},{1,0},{2,3},{3,2},{4,5},{5,4},{6,7},{7,6},{8,9},{9,8},{10,11... | collective-permute-start | bytes 3145736 | tf_op jit(solution)/shard_map/ppermute | solution.py:339
  83.9 2.2 %collective-permute-start.11 = (s32[128,6]{0,1:T(8,128)S(1)}, s32[128,6]{0,1:T(8,128)S(1)}, u32[]{:S(2)}, u32[]{:S(2)}) collective-permute-start(s32[128,6]{0,1:T(8,128)S(1)} %copy-done.17), channel_id=1, source_target_pairs={{0,1},{1,0},{2,3},{3,2},{4,5},{5,4},{6,7},{7,6},{8,9},{9,8},{10,11... | collective-permute-start | bytes 9224 | tf_op jit(solution)/shard_map/ppermute | solution.py:339
  86.1 0.6 copy-start.18
  86.6 14.2 %collective-permute-start = (bf16[128,2048]{1,0:T(8,128)(2,1)}, bf16[128,2048]{1,0:T(8,128)(2,1)}, u32[]{:S(2)}, u32[]{:S(2)}) collective-permute-start(bf16[128,2048]{1,0:T(8,128)(2,1)} %param.16), channel_id=1, source_target_pairs={{0,1},{1,0},{2,3},{3,2},{4,5},{5,4},{6,7},{7,6},{8,9},{9,8},{10,11... | collective-permute-start | bytes 1572872 | tf_op jit(solution)/shard_map/ppermute | solution.py:339
  91.1 1.1 copy-start.3
  92.2 1.0 copy-start.5
  93.3 33.3 %collective-permute-start.16 = (bf16[288,2048]{1,0:T(8,128)(2,1)}, bf16[288,2048]{1,0:T(8,128)(2,1)S(1)}, u32[]{:S(2)}, u32[]{:S(2)}) collective-permute-start(bf16[288,2048]{1,0:T(8,128)(2,1)} %collective-permute-done.13.refs_3_), channel_id=1, source_target_pairs={{0,96},{32,0},{64,32},{96,64},{1,97},{33,1},{65,33},{97,65},{2,98}... | collective-permute-start | bytes 3538952 | tf_op jit(solution)/shard_map/ppermute | solution.py:432
  96.7 30.8 %collective-permute-start.17 = (bf16[288,2048]{1,0:T(8,128)(2,1)}, bf16[288,2048]{1,0:T(8,128)(2,1)S(1)}, u32[]{:S(2)}, u32[]{:S(2)}) collective-permute-start(bf16[288,2048]{1,0:T(8,128)(2,1)} %collective-permute-done.13.refs_3_), channel_id=1, source_target_pairs={{0,8},{8,0},{1,9},{9,1},{2,10},{10,2},{3,11},{11,3},{4,12},{12,4},... | collective-permute-start | bytes 3538952 | tf_op jit(solution)/shard_map/ppermute | solution.py:343
  96.9 28.1 %collective-permute-start.15 = (bf16[288,2048]{1,0:T(8,128)(2,1)}, bf16[288,2048]{1,0:T(8,128)(2,1)}, u32[]{:S(2)}, u32[]{:S(2)}) collective-permute-start(bf16[288,2048]{1,0:T(8,128)(2,1)} %copy-done.5), channel_id=1, source_target_pairs={{0,32},{32,64},{64,96},{96,0},{1,33},{33,65},{65,97},{97,1},{2,34}... | collective-permute-start | bytes 3538952 | tf_op jit(solution)/shard_map/ppermute | solution.py:431
  110.6 38.6 %collective-permute-start.28 = (bf16[128,2048]{1,0:T(8,128)(2,1)}, bf16[128,2048]{1,0:T(8,128)(2,1)}, u32[]{:S(2)}, u32[]{:S(2)}) collective-permute-start(bf16[128,2048]{1,0:T(8,128)(2,1)} %constant_dynamic-slice_fusion), channel_id=1, source_target_pairs={{0,24},{24,0},{8,16},{16,8},{1,25},{25,1},{9,17},{17,9},{2,26},{26... | collective-permute-start | bytes 1572872 | tf_op jit(solution)/shard_map/ppermute | solution.py:347
  114.5 15.3 %collective-permute-start.21 = (bf16[48,2048]{1,0:T(8,128)(2,1)}, bf16[48,2048]{1,0:T(8,128)(2,1)}, u32[]{:S(2)}, u32[]{:S(2)}) collective-permute-start(bf16[48,2048]{1,0:T(8,128)(2,1)} %get-tuple-element.47), channel_id=1, source_target_pairs={{0,2},{2,4},{4,6},{6,0},{1,3},{3,5},{5,7},{7,1},{8,10},{10,12},{12... | collective-permute-start | bytes 589832 | tf_op jit(solution)/shard_map/ppermute | solution.py:519
  125.0 6.3 %collective-permute-start.22 = (bf16[48,2048]{1,0:T(8,128)(2,1)}, bf16[48,2048]{1,0:T(8,128)(2,1)}, u32[]{:S(2)}, u32[]{:S(2)}) collective-permute-start(bf16[48,2048]{1,0:T(8,128)(2,1)} %get-tuple-element.46), channel_id=1, source_target_pairs={{0,4},{2,6},{4,0},{6,2},{1,5},{3,7},{5,1},{7,3},{8,12},{10,14},{12... | collective-permute-start | bytes 589832 | tf_op jit(solution)/shard_map/ppermute | solution.py:519
  126.5 9.6 %collective-permute-start.23 = (bf16[48,2048]{1,0:T(8,128)(2,1)}, bf16[48,2048]{1,0:T(8,128)(2,1)}, u32[]{:S(2)}, u32[]{:S(2)}) collective-permute-start(bf16[48,2048]{1,0:T(8,128)(2,1)} %get-tuple-element.45), channel_id=1, source_target_pairs={{0,6},{2,0},{4,2},{6,4},{1,7},{3,1},{5,3},{7,5},{8,14},{10,8},{12,... | collective-permute-start | bytes 589832 | tf_op jit(solution)/shard_map/ppermute | solution.py:519
  127.5 8.6 %copy-start.8 = (bf16[48,2048]{1,0:T(8,128)(2,1)S(1)}, bf16[48,2048]{1,0:T(8,128)(2,1)}, u32[]{:S(2)}) copy-start(bf16[48,2048]{1,0:T(8,128)(2,1)} %get-tuple-element.48.own_ref) | copy-start | bytes 589828
  127.5 24.3 %collective-permute-start.18 = (bf16[96,2048]{1,0:T(8,128)(2,1)S(1)}, bf16[96,2048]{1,0:T(8,128)(2,1)S(1)}, u32[]{:S(2)}, u32[]{:S(2)}) collective-permute-start(bf16[96,2048]{1,0:T(8,128)(2,1)S(1)} %slice.49), channel_id=1, source_target_pairs={{0,8},{8,0},{1,9},{9,1},{2,10},{10,2},{3,11},{11,3},{4,12},{12,4},... | collective-permute-start | bytes 1179656 | tf_op jit(solution)/shard_map/ppermute | solution.py:343
  129.9 25.1 %collective-permute-start.19 = (bf16[96,2048]{1,0:T(8,128)(2,1)S(1)}, bf16[96,2048]{1,0:T(8,128)(2,1)S(1)}, u32[]{:S(2)}, u32[]{:S(2)}) collective-permute-start(bf16[96,2048]{1,0:T(8,128)(2,1)S(1)} %slice.50), channel_id=1, source_target_pairs={{0,32},{32,64},{64,96},{96,0},{1,33},{33,65},{65,97},{97,1},{2,34}... | collective-permute-start | bytes 1179656 | tf_op jit(solution)/shard_map/ppermute | solution.py:457
  131.3 23.7 %collective-permute-start.20 = (bf16[96,2048]{1,0:T(8,128)(2,1)S(1)}, bf16[96,2048]{1,0:T(8,128)(2,1)S(1)}, u32[]{:S(2)}, u32[]{:S(2)}) collective-permute-start(bf16[96,2048]{1,0:T(8,128)(2,1)S(1)} %slice.51), channel_id=1, source_target_pairs={{0,96},{32,0},{64,32},{96,64},{1,97},{33,1},{65,33},{97,65},{2,98}... | collective-permute-start | bytes 1179656 | tf_op jit(solution)/shard_map/ppermute | solution.py:458
  136.1 2.6 %copy-start = (bf16[1,2048,1408]{2,1,0:T(8,128)(2,1)S(1)}, bf16[1,2048,1408]{2,1,0:T(8,128)(2,1)}, u32[]{:S(2)}) copy-start(bf16[1,2048,1408]{2,1,0:T(8,128)(2,1)} %param.26) | copy-start | bytes 17301508
  138.8 2.6 %copy-start.1 = (bf16[1,2048,1408]{2,1,0:T(8,128)(2,1)S(1)}, bf16[1,2048,1408]{2,1,0:T(8,128)(2,1)}, u32[]{:S(2)}) copy-start(bf16[1,2048,1408]{2,1,0:T(8,128)(2,1)} %param.27) | copy-start | bytes 17301508
  141.4 2.6 %copy-start.2 = (bf16[1,1408,2048]{2,1,0:T(8,128)(2,1)S(1)}, bf16[1,1408,2048]{2,1,0:T(8,128)(2,1)}, u32[]{:S(2)}) copy-start(bf16[1,1408,2048]{2,1,0:T(8,128)(2,1)} %param.28) | copy-start | bytes 17301508
  144.0 11.0 %copy-start.6 = (bf16[288,2048]{1,0:T(8,128)(2,1)S(1)}, bf16[288,2048]{1,0:T(8,128)(2,1)}, u32[]{:S(2)}) copy-start(bf16[288,2048]{1,0:T(8,128)(2,1)} %copy-done.5) | copy-start | bytes 3538948
  144.0 11.0 %copy-start.7 = (bf16[256,2048]{1,0:T(8,128)(2,1)S(1)}, bf16[256,2048]{1,0:T(8,128)(2,1)}, u32[]{:S(2)}) copy-start(bf16[256,2048]{1,0:T(8,128)(2,1)} %get-tuple-element.33.refs_0_) | copy-start | bytes 3145732
  149.2 5.9 %copy-start.4 = (bf16[288,2048]{1,0:T(8,128)(2,1)S(1)}, bf16[288,2048]{1,0:T(8,128)(2,1)}, u32[]{:S(2)}) copy-start(bf16[288,2048]{1,0:T(8,128)(2,1)} %copy-done.3) | copy-start | bytes 3538948
  149.2 15.5 %collective-permute-start.29 = (bf16[128,2048]{1,0:T(8,128)(2,1)}, bf16[128,2048]{1,0:T(8,128)(2,1)S(1)}, u32[]{:S(2)}, u32[]{:S(2)}) collective-permute-start(bf16[128,2048]{1,0:T(8,128)(2,1)} %collective-permute-done.28), channel_id=1, source_target_pairs={{0,1},{1,0},{2,3},{3,2},{4,5},{5,4},{6,7},{7,6},{8,9},{9,8},{10,11... | collective-permute-start | bytes 1572872 | tf_op jit(solution)/shard_map/ppermute | solution.py:339
  151.7 10.4 %collective-permute-start.26 = (bf16[48,2048]{1,0:T(8,128)(2,1)S(1)}, bf16[48,2048]{1,0:T(8,128)(2,1)S(1)}, u32[]{:S(2)}, u32[]{:S(2)}) collective-permute-start(bf16[48,2048]{1,0:T(8,128)(2,1)S(1)} %get-tuple-element.42), channel_id=1, source_target_pairs={{0,2},{2,4},{4,6},{6,0},{1,3},{3,5},{5,7},{7,1},{8,10},{10,12},{12... | collective-permute-start | bytes 589832 | tf_op jit(solution)/shard_map/ppermute | solution.py:526
  151.8 12.5 %collective-permute-start.25 = (bf16[48,2048]{1,0:T(8,128)(2,1)S(1)}, bf16[48,2048]{1,0:T(8,128)(2,1)S(1)}, u32[]{:S(2)}, u32[]{:S(2)}) collective-permute-start(bf16[48,2048]{1,0:T(8,128)(2,1)S(1)} %get-tuple-element.43), channel_id=1, source_target_pairs={{0,4},{2,6},{4,0},{6,2},{1,5},{3,7},{5,1},{7,3},{8,12},{10,14},{12... | collective-permute-start | bytes 589832 | tf_op jit(solution)/shard_map/ppermute | solution.py:526
  155.0 9.3 %copy-start.9 = (f32[256,192]{1,0:T(8,128)S(1)}, f32[256,192]{1,0:T(8,128)}, u32[]{:S(2)}) copy-start(f32[256,192]{1,0:T(8,128)} %get-tuple-element.39) | copy-start | bytes 589828
  155.0 9.3 %collective-permute-start.24 = (bf16[48,2048]{1,0:T(8,128)(2,1)S(1)}, bf16[48,2048]{1,0:T(8,128)(2,1)S(1)}, u32[]{:S(2)}, u32[]{:S(2)}) collective-permute-start(bf16[48,2048]{1,0:T(8,128)(2,1)S(1)} %get-tuple-element.44), channel_id=1, source_target_pairs={{0,6},{2,0},{4,2},{6,4},{1,7},{3,1},{5,3},{7,5},{8,14},{10,8},{12,... | collective-permute-start | bytes 589832 | tf_op jit(solution)/shard_map/ppermute | solution.py:526
  173.3 2.5 %collective-permute-start.30 = (bf16[128,2048]{1,0:T(8,128)(2,1)S(1)}, bf16[128,2048]{1,0:T(8,128)(2,1)S(1)}, u32[]{:S(2)}, u32[]{:S(2)}) collective-permute-start(bf16[128,2048]{1,0:T(8,128)(2,1)S(1)} %dynamic-slice_convert_fusion), channel_id=1, source_target_pairs={{0,1},{1,0},{2,3},{3,2},{4,5},{5,4},{6,7},{7,6},{8,9},{9,8},{10,11... | collective-permute-start | bytes 1572872 | tf_op jit(solution)/shard_map/ppermute | solution.py:339
  174.7 15.6 %copy-start.10 = (f32[256,2048]{1,0:T(8,128)S(1)}, f32[256,2048]{1,0:T(8,128)}, u32[]{:S(2)}) copy-start(f32[256,2048]{1,0:T(8,128)} %get-tuple-element.32) | copy-start | bytes 6291460
  174.7 3.1 %collective-permute-start.27 = (bf16[128,2048]{1,0:T(8,128)(2,1)S(1)}, bf16[128,2048]{1,0:T(8,128)(2,1)S(1)}, u32[]{:S(2)}, u32[]{:S(2)}) collective-permute-start(bf16[128,2048]{1,0:T(8,128)(2,1)S(1)} %dynamic-slice_convert_fusion.1), channel_id=1, source_target_pairs={{0,1},{1,0},{2,3},{3,2},{4,5},{5,4},{6,7},{7,6},{8,9},{9,8},{10,11... | collective-permute-start | bytes 1572872 | tf_op jit(solution)/shard_map/ppermute | solution.py:339
  175.9 14.4 %collective-permute-start.31 = (bf16[128,2048]{1,0:T(8,128)(2,1)S(1)}, bf16[128,2048]{1,0:T(8,128)(2,1)S(1)}, u32[]{:S(2)}, u32[]{:S(2)}) collective-permute-start(bf16[128,2048]{1,0:T(8,128)(2,1)S(1)} %add_convert_fusion.1), channel_id=1, source_target_pairs={{0,24},{24,0},{8,16},{16,8},{1,25},{25,1},{9,17},{17,9},{2,26},{26... | collective-permute-start | bytes 1572872 | tf_op jit(solution)/shard_map/ppermute | solution.py:347
Sparse Core Ops, SparseCore 0:
  9.0 51.4 all-gather.2

commit v2 on v1

v2 whole, which is shorter than its diff:
```python
import functools
import math

import jax
import jax.numpy as jnp
from jax import lax
from jax.experimental import pallas as pl
from jax.experimental.pallas import tpu as pltpu
from jax.sharding import Mesh, PartitionSpec as P

BF = jnp.bfloat16
F32 = jnp.float32
CHUNK = 256
CHUNKS = 4
HD = 128
HEADS = 2
CAP = 24
SLOTS = 2 * CAP
T_DEV = 128
T_CHIP = 256
ROUTED = 64
TOPK = 6
D = 2048
FF = 1408
SH = 176
PART = 48
LAST = SH - PART
N_CTX = 16
MSG = 272
FINEST = lax.Precision.HIGHEST

VM = pl.BlockSpec(memory_space=pltpu.VMEM)
HBM = pl.BlockSpec(memory_space=pltpu.HBM)
SM = pl.BlockSpec(memory_space=pltpu.SMEM)


def mm(a, b, dims=((1,), (0,))):
    return lax.dot_general(a, b, (dims, ((), ())), preferred_element_type=F32)


def places():
    t = lax.broadcasted_iota(jnp.int32, (CHUNK, CHUNK), 0)
    s = lax.broadcasted_iota(jnp.int32, (CHUNK, CHUNK), 1)
    return t, s


def split_decay(decay_ref):
    rows = jnp.concatenate(
        [decay_ref[:, j * CHUNK : (j + 1) * CHUNK] for j in range(CHUNKS)], axis=0
    )
    return jnp.concatenate(three_parts(rows), axis=0).astype(BF)


def chunk_cols(decay_ref, t, s):
    lower = jnp.where(s <= t, 1.0, 0.0).astype(BF)
    out = mm(lower, split_decay(decay_ref), ((1,), (1,)))
    n = CHUNKS * HEADS
    return out[:, :n] + out[:, n : 2 * n] + out[:, 2 * n :]


def chunk_rows(decay_ref, t, s):
    upper = jnp.where(t <= s, 1.0, 0.0).astype(BF)
    out = mm(split_decay(decay_ref), upper)
    n = CHUNKS * HEADS
    return out[:n] + out[n : 2 * n] + out[2 * n :]


def rows_of(j):
    return slice(j * CHUNK, (j + 1) * CHUNK)


def cols_of(h):
    return slice(h * HD, (h + 1) * HD)


def three_parts(x):
    hi = x.astype(BF).astype(F32)
    mid = (x - hi).astype(BF).astype(F32)
    lo = x - hi - mid
    return hi, mid, lo


def write_message(message_ref, states, totals):
    row = lax.broadcasted_iota(jnp.int32, (16, HD), 0)
    tail = jnp.zeros((16, HD), F32)
    for h in range(HEADS):
        message_ref[h * HD : (h + 1) * HD, :] = states[h].astype(BF)
        for i, piece in enumerate(three_parts(totals[h])):
            tail = jnp.where(row == 3 * h + i, piece, tail)
    message_ref[HEADS * HD : MSG, :] = tail.astype(BF)


def read_message(message_ref):
    tail = message_ref[HEADS * HD : MSG, :].astype(F32)
    out = []
    for h in range(HEADS):
        total = tail[3 * h : 3 * h + 1] + tail[3 * h + 1 : 3 * h + 2] + tail[3 * h + 2 : 3 * h + 3]
        out.append((message_ref[h * HD : (h + 1) * HD, :].astype(F32), total))
    return out


def states_kernel(
    place_ref, decay_ref, key_ref, value_ref, gate_ref, up_ref, down_ref,
    states_ref, passed_ref, message_ref, slab_ref, keys_ref, values_ref, sems
):
    loads = [
        [
            pltpu.make_async_copy(ref.at[rows_of(j)], buffer.at[rows_of(j)], sems.at[k, j])
            for k, (ref, buffer) in enumerate(((key_ref, keys_ref), (value_ref, values_ref)))
        ]
        for j in range(CHUNKS)
    ]
    first = pl.ds(pl.multiple_of(place_ref[6], 16), PART)
    cuts = [
        pltpu.make_async_copy(ref.at[first], slab_ref.at[i], sems.at[2, i])
        for i, ref in enumerate((gate_ref, up_ref, down_ref))
    ]
    for pair in loads:
        for copy in pair:
            copy.start()
    for copy in cuts:
        copy.start()
    t, s = places()
    within = chunk_cols(decay_ref, t, s)
    last = within[CHUNK - 1 : CHUNK, :]
    rest = jnp.exp(last - within)
    states = [jnp.zeros((HD, HD), F32) for _ in range(HEADS)]
    totals = [jnp.zeros((1, HD), F32) for _ in range(HEADS)]
    for j in range(CHUNKS):
        for copy in loads[j]:
            copy.wait()
        for h in range(HEADS):
            states_ref[j, h] = states[h]
            passed_ref[j, h : h + 1, :] = jnp.exp(totals[h])
            at = HEADS * j + h
            ending = jnp.broadcast_to(last[:, at : at + 1], (1, HD))
            keys = (keys_ref[rows_of(j), cols_of(h)].astype(F32) * rest[:, at : at + 1]).astype(BF)
            states[h] = jnp.exp(ending) * states[h] + mm(
                keys, values_ref[rows_of(j), cols_of(h)], ((0,), (0,))
            )
            totals[h] = totals[h] + ending
    write_message(message_ref, states, totals)
    for copy in cuts:
        copy.wait()


def step_kernel(bit, place_ref, own_ref, other_ref, *rest):
    before, (prefix_ref, total_ref, message_ref) = rest[:-3], rest[-3:]
    upper = place_ref[bit] == 1
    own, other = read_message(own_ref), read_message(other_ref)
    states, totals = [], []
    for h in range(HEADS):
        (mine, mine_total), (theirs, theirs_total) = own[h], other[h]
        if before:
            prefix, total = before[0][h], before[1][h : h + 1, :]
            prefix_ref[h] = jnp.where(upper, jnp.exp(total) * theirs + prefix, prefix)
            total_ref[h : h + 1, :] = jnp.where(upper, theirs_total + total, total)
        else:
            prefix_ref[h] = jnp.where(upper, theirs, 0.0)
            total_ref[h : h + 1, :] = jnp.where(upper, theirs_total, 0.0)
        first = jnp.where(upper, theirs, mine)
        second = jnp.where(upper, mine, theirs)
        states.append(jnp.exp(jnp.where(upper, mine_total, theirs_total)) * first + second)
        totals.append(mine_total + theirs_total)
    write_message(message_ref, states, totals)


def inner_kernel(query_ref, key_ref, value_ref, decay_ref, out_ref):
    t, s = places()
    causal = s <= t
    cols = chunk_cols(decay_ref, t, s)
    rows = chunk_rows(decay_ref, t, s)
    for j in range(CHUNKS):
        for h in range(HEADS):
            at = HEADS * j + h
            scores = mm(
                query_ref[rows_of(j), cols_of(h)], key_ref[rows_of(j), cols_of(h)], ((1,), (1,))
            )
            spread = jnp.where(causal, cols[:, at : at + 1] - rows[at : at + 1, :], -1e30)
            near = (scores * jnp.exp(spread)).astype(BF)
            out_ref[rows_of(j), cols_of(h)] = mm(near, value_ref[rows_of(j), cols_of(h)])


def mix_kernel(
    place_ref,
    query_ref,
    decay_ref,
    inner_ref,
    states_ref,
    passed_ref,
    prefix_ref,
    total_ref,
    other_ref,
    gain_ref,
    *outs,
):
    x = place_ref[4]
    t, s = places()
    other = read_message(other_ref)
    incoming = []
    for h in range(HEADS):
        far = jnp.exp(total_ref[h : h + 1, :]) * other[h][0] + prefix_ref[h]
        incoming.append(jnp.where(place_ref[3] == 1, far, prefix_ref[h]))
    lower = jnp.where(s <= t, 1.0, 0.0).astype(BF)
    for d in range(CHUNKS):
        j = lax.rem(x + d, 4)
        rows = pl.ds(pl.multiple_of(j * CHUNK, CHUNK), CHUNK)
        parts = jnp.concatenate(three_parts(decay_ref[:, rows]), axis=0).astype(BF)
        summed = mm(lower, parts, ((1,), (1,)))
        reach = jnp.exp(summed[:, :HEADS] + summed[:, HEADS : 2 * HEADS] + summed[:, 2 * HEADS :])
        for h in range(HEADS):
            state = (states_ref[j, h] + passed_ref[j, h : h + 1, :] * incoming[h]).astype(BF)
            query = (query_ref[rows, cols_of(h)].astype(F32) * reach[:, h : h + 1]).astype(BF)
            mixed = inner_ref[rows, cols_of(h)] + mm(query, state)
            scale = lax.rsqrt(jnp.mean(mixed * mixed, axis=1, keepdims=True) + 1e-06)
            outs[d][:, cols_of(h)] = (mixed * scale * gain_ref[:, cols_of(h)]).astype(BF)


def project_kernel(
    place_ref, own_ref, one_ref, two_ref, three_ref, residual_ref, w0_ref, w1_ref, w2a_ref, w2b_ref, w3_ref,
    part_ref, sent_ref, rows_ref
):
    core = place_ref[5]
    mine = pl.ds(pl.multiple_of(core * T_DEV, T_DEV), T_DEV)
    theirs = pl.ds(pl.multiple_of((1 - core) * T_DEV, T_DEV), T_DEV)
    for d, ref in enumerate((own_ref, one_ref, two_ref, three_ref)):
        cols = slice(d * CHUNK, (d + 1) * CHUNK)
        rows_ref[:T_DEV, cols] = ref[mine, :]
        rows_ref[T_DEV:, cols] = ref[theirs, :]
    for n in range(4):
        cols = slice(n * 512, (n + 1) * 512)
        total = jnp.zeros((T_CHIP, 512), F32)
        at = 0
        for ref in (w0_ref, w1_ref, w2a_ref, w2b_ref, w3_ref):
            total += mm(rows_ref[:, at : at + ref.shape[0]], ref[:, cols])
            at += ref.shape[0]
        own = total[:T_DEV] + residual_ref[:, cols].astype(F32)
        part_ref[:T_DEV, cols] = own
        part_ref[T_DEV:, cols] = total[T_DEV:]
        sent_ref[:T_DEV, cols] = total[T_DEV:].astype(BF)
        sent_ref[T_DEV:, cols] = own.astype(BF)


def route_kernel(place_ref, own_ref, other_ref, named_ref, selector_ref):
    x, core = place_ref[4], place_ref[5]
    lane = lax.broadcasted_iota(jnp.int32, (T_CHIP, ROUTED), 1)
    ids = jnp.concatenate([own_ref[...], other_ref[...]], axis=0)
    named = jnp.zeros((T_CHIP, ROUTED), F32)
    for k in range(TOPK):
        named = jnp.where(ids[:, k : k + 1] == lane, 1.0, named)
    named_ref[...] = named
    t, s = places()
    before = jnp.where((s < t) & ((s < T_DEV) == (t < T_DEV)), 1.0, 0.0).astype(BF)
    ranks = mm(before, named.astype(BF))
    slot_lane = lax.broadcasted_iota(jnp.int32, (T_CHIP, 4 * SLOTS), 1)
    token = lax.broadcasted_iota(jnp.int32, (T_CHIP, 1), 0)
    wanted = jnp.full((T_CHIP, 4 * SLOTS), -1, jnp.int32)
    for d in range(4):
        mine = lane == 2 * lax.rem(x + d, 4) + core
        hit = jnp.sum(jnp.where(mine, named, 0.0), axis=1, keepdims=True) > 0.5
        rank = jnp.sum(jnp.where(mine, ranks, 0.0), axis=1, keepdims=True).astype(jnp.int32)
        slot = jnp.where(hit, rank + jnp.where(token < T_DEV, 0, CAP) + d * SLOTS, -1)
        inside = (slot_lane >= d * SLOTS) & (slot_lane < (d + 1) * SLOTS)
        wanted = jnp.where(inside, slot, wanted)
    selector_ref[...] = jnp.where(wanted == slot_lane, 1.0, 0.0).astype(BF)


def norm_kernel(
    place_ref,
    part_ref,
    other_ref,
    gain_ref,
    router_ref,
    named_ref,
    selector_ref,
    stream_ref,
    mine_ref,
    theirs_ref,
    out0_ref,
    out1_ref,
    out2_ref,
    out3_ref,
    back_ref,
    normed_ref,
):
    x, core = place_ref[4], place_ref[5]
    for half, out in ((0, mine_ref), (1, theirs_ref)):
        rows = slice(half * T_DEV, (half + 1) * T_DEV)
        stream = part_ref[rows, :] + other_ref[rows, :].astype(F32)
        if half == 0:
            stream_ref[...] = stream
        scale = lax.rsqrt(jnp.mean(stream * stream, axis=1, keepdims=True) + 1e-06)
        normed = (stream * scale * gain_ref[...]).astype(BF)
        normed_ref[rows, :] = normed
        out[...] = normed
    sent = mm(selector_ref[...], normed_ref[...], ((0,), (0,))).astype(BF)
    for d, ref in enumerate((out0_ref, out1_ref, out2_ref, out3_ref)):
        ref[...] = sent[d * SLOTS : (d + 1) * SLOTS]
    logits = mm(normed_ref[...], router_ref[...], ((1,), (1,)))
    affinity = named_ref[...] / (1.0 + jnp.exp(-logits))
    gates = affinity / jnp.sum(affinity, axis=1, keepdims=True)
    lane = lax.broadcasted_iota(jnp.int32, (T_CHIP, ROUTED), 1)
    slot_lane = lax.broadcasted_iota(jnp.int32, (T_CHIP, 4 * SLOTS), 1)
    weight = jnp.zeros((T_CHIP, 4 * SLOTS), F32)
    for d in range(4):
        mine = lane == 2 * lax.rem(x + d, 4) + core
        gate = jnp.sum(jnp.where(mine, gates, 0.0), axis=1, keepdims=True)
        inside = (slot_lane >= d * SLOTS) & (slot_lane < (d + 1) * SLOTS)
        weight = jnp.where(inside, gate, weight)
    weight = selector_ref[...].astype(F32) * weight
    high = weight.astype(BF)
    back_ref[:, : 4 * SLOTS] = high
    back_ref[:, 4 * SLOTS :] = (weight - high.astype(F32)).astype(BF)


def load_kernel(*refs):
    count = len(refs) // 2
    copies = [
        pltpu.make_async_copy(refs[i], refs[count + i], refs[-1].at[i]) for i in range(count)
    ]
    for copy in copies:
        copy.start()
    for copy in copies:
        copy.wait()


def expert_kernel(
    own_ref, one_ref, two_ref, three_ref, gate_ref, up_ref, down_ref, *rest
):
    outs, (rows_ref, hidden_ref) = rest[:4], rest[4:]
    for d, ref in enumerate((own_ref, one_ref, two_ref, three_ref)):
        rows_ref[d * SLOTS : (d + 1) * SLOTS, :] = ref[...]
    for n in range(0, FF, 256):
        cols = slice(n, min(n + 256, FF))
        gate = mm(rows_ref[...], gate_ref[:, cols])
        up = mm(rows_ref[...], up_ref[:, cols])
        hidden_ref[:, cols] = (gate / (1.0 + jnp.exp(-gate)) * up).astype(BF)
    for n in range(4):
        cols = slice(n * 512, (n + 1) * 512)
        out = mm(hidden_ref[...], down_ref[:, cols]).astype(BF)
        for d, ref in enumerate(outs):
            ref[:, cols] = out[d * SLOTS : (d + 1) * SLOTS]


def shared_kernel(place_ref, own_ref, other_ref, weights_ref, mine_ref, theirs_ref, rows_ref, side_ref):
    rows_ref[:, :T_DEV] = own_ref[...].T
    rows_ref[:, T_DEV:] = other_ref[...].T

    def side(k):
        return weights_ref[:, k].reshape(N_CTX * PART, D)

    gate = mm(side(0), rows_ref[...])
    up = mm(side(1), rows_ref[...])
    unit = lax.rem(lax.broadcasted_iota(jnp.int32, (N_CTX * PART, T_CHIP), 0), PART)
    kept = unit >= jnp.where(place_ref[6] == LAST, 4 * PART - SH, 0)
    side_ref[...] = jnp.where(kept, gate / (1.0 + jnp.exp(-gate)) * up, 0.0).astype(BF)
    hidden = side_ref[...].T
    for n in range(4):
        cols = slice(n * 512, (n + 1) * 512)
        out = mm(hidden, weights_ref[:, 2, :, cols].reshape(N_CTX * PART, 512))
        mine_ref[:, cols] = out[:T_DEV]
        theirs_ref[:, cols] = out[T_DEV:].astype(BF)


def combine_kernel(mine_ref, theirs_ref, back_ref, one_ref, two_ref, three_ref, four_ref, out_ref, sent_ref, rows_ref):
    for d, ref in enumerate((one_ref, two_ref, three_ref, four_ref)):
        rows_ref[d * SLOTS : (d + 1) * SLOTS, :] = ref[...]
    for n in range(4):
        cols = slice(n * 512, (n + 1) * 512)
        routed = mm(back_ref[:, : 4 * SLOTS], rows_ref[:, cols]) + mm(
            back_ref[:, 4 * SLOTS :], rows_ref[:, cols]
        )
        out_ref[:, cols] = mine_ref[:, cols] + routed[:T_DEV]
        sent_ref[:, cols] = (theirs_ref[:, cols].astype(F32) + routed[T_DEV:]).astype(BF)


def call(kernel, outs, *args, scratch=(), scalars=0, loose=0, sems=None, limit=12, name=None, flops=10**9):
    size = sum(a.size * a.dtype.itemsize for a in args)
    size += sum(math.prod(shape) * jnp.dtype(kind).itemsize for shape, kind in outs)
    if not flops:
        size = 0
    sems = [] if sems is None else [pltpu.SemaphoreType.DMA(sems)]
    return pl.pallas_call(
        kernel,
        in_specs=[SM] * scalars + [VM] * (len(args) - scalars - loose) + [HBM] * loose,
        out_specs=[VM] * len(outs),
        out_shape=[jax.ShapeDtypeStruct(shape, kind) for shape, kind in outs],
        scratch_shapes=[pltpu.VMEM(shape, kind) for shape, kind in scratch] + sems,
        compiler_params=pltpu.CompilerParams(vmem_limit_bytes=limit * 2**20),
        cost_estimate=pl.CostEstimate(flops=flops, bytes_accessed=size, transcendentals=0),
        name=name or kernel.__name__.replace("_kernel", ""),
    )(*args)


def group(*values):
    return lax.optimization_barrier(values)


def after(value, *others):
    return lax.optimization_barrier((value,) + others)[0]


def ring(step, count=4):
    return [(i, (i + step) % count) for i in range(count)]


def swap_core(a):
    return lax.ppermute(a, "core", [(0, 1), (1, 0)])


def swap(a, axis, bit):
    count = 4 if axis == "y" or axis == "x" else 2
    return lax.ppermute(a, axis, [(i, i ^ bit) for i in range(count)])


def on_device(
    residual_in,
    queries,
    key_rows,
    values,
    log_decay,
    attn_gain,
    out_proj,
    ffn_gain,
    router,
    route_ids,
    w_gate,
    w_up,
    w_down,
    shared_gate,
    shared_up,
    shared_down,
):
    core = lax.axis_index("core")
    x = lax.axis_index("x")
    y = lax.axis_index("y")
    first = jnp.minimum((2 * lax.rem(x, 2) + core) * PART, LAST)
    place = jnp.stack(
        [lax.axis_index("zl"), lax.axis_index("zh"), lax.rem(y, 2), y // 2, x, core, first]
    ).astype(jnp.int32)
    token_rows = ((T_DEV, D), BF)

    proj_low = lax.ppermute(out_proj, "x", ring(1))
    proj_high = lax.ppermute(out_proj, "x", ring(3))

    states, passed, message, slab = call(
        states_kernel,
        [
            ((CHUNKS, HEADS, HD, HD), F32),
            ((CHUNKS, HEADS, HD), F32),
            ((MSG, HD), BF),
            ((3, PART, D), BF),
        ],
        place,
        log_decay,
        key_rows,
        values,
        shared_gate.T,
        shared_up.T,
        shared_down,
        scratch=[((CHUNK * CHUNKS, HEADS * HD), BF)] * 2,
        scalars=1,
        loose=5,
        sems=(3, 4),
        limit=60,
    )
    shared_weights = lax.all_gather(slab, ("y", "zh", "zl"))
    prefix = ()
    for bit, (axis, step) in enumerate((("zl", 1), ("zh", 1), ("y", 1))):
        other = swap(message, axis, step)
        *prefix, message = call(
            functools.partial(step_kernel, bit),
            [((HEADS, HD, HD), F32), ((HEADS, HD), F32), ((MSG, HD), BF)],
            place,
            message,
            other,
            *prefix,
            scalars=1,
            name=f"step{bit}",
        )
        if bit == 0:
            other_ids = swap_core(after(route_ids, message))
            (inner,) = call(
                inner_kernel,
                [((CHUNK * CHUNKS, HEADS * HD), F32)],
                after(queries, message),
                key_rows,
                values,
                log_decay,
            )
        if bit == 1:
            named, selector = call(
                route_kernel,
                [((T_CHIP, ROUTED), F32), ((T_CHIP, 4 * SLOTS), BF)],
                place,
                after(route_ids, message, inner),
                other_ids,
                scalars=1,
            )
    other = swap(message, "y", 2)
    far_low, far_high = after(proj_low, message)[:T_DEV], after(proj_high, message)[T_DEV:]
    other, far_low, far_high, named, selector = group(other, far_low, far_high, named, selector)
    normed = call(
        mix_kernel,
        [((T_CHIP, HEADS * HD), BF)] * 4,
        place,
        queries,
        log_decay,
        inner,
        states,
        passed,
        *prefix,
        other,
        attn_gain.reshape(1, HEADS * HD),
        scalars=1,
    )

    proj_far_low = lax.ppermute(far_low, "x", ring(1))
    proj_far_high = lax.ppermute(far_high, "x", ring(3))
    heads = [lax.ppermute(normed[d], "x", ring(d)) for d in (1, 2, 3)]

    *heads, proj_far_low, proj_far_high = group(*heads, proj_far_low, proj_far_high)

    part, part_sent = call(
        project_kernel,
        [((T_CHIP, D), F32), ((T_CHIP, D), BF)],
        place,
        normed[0],
        *heads,
        residual_in,
        out_proj,
        proj_low,
        proj_far_low,
        proj_far_high,
        proj_high,
        scratch=[((T_CHIP, 4 * CHUNK), BF)],
        scalars=1,
        flops=6 * 10**9,
    )
    stream, mine, theirs, *outgoing, back = call(
        norm_kernel,
        [((T_DEV, D), F32), token_rows, token_rows]
        + [((SLOTS, D), BF)] * 4
        + [((T_CHIP, 8 * SLOTS), BF)],
        place,
        part,
        swap_core(part_sent),
        ffn_gain.reshape(1, D),
        router.T,
        named,
        selector,
        scratch=[((T_CHIP, D), BF)],
        scalars=1,
        flops=3 * 10**10,
    )
    arrived = [lax.ppermute(outgoing[d], "x", ring(d)) for d in (1, 2, 3)]
    expert_weights = call(
        load_kernel,
        [((D, FF), BF), ((D, FF), BF), ((FF, D), BF)],
        after(w_gate, mine)[0],
        w_up[0],
        w_down[0],
        loose=3,
        sems=(3,),
        limit=28,
    )
    *arrived, gate_w, up_w, down_w = group(*arrived, *expert_weights)
    partner_mine = swap(after(mine, *arrived), "x", 1)
    results = call(
        expert_kernel,
        [((SLOTS, D), BF)] * 4,
        outgoing[0],
        *arrived,
        gate_w,
        up_w,
        down_w,
        scratch=[((4 * SLOTS, D), BF), ((4 * SLOTS, FF), BF)],
    )
    returned = [lax.ppermute(results[d], "x", ring(4 - d)) for d in (1, 2, 3)]

    (shared_here,) = call(
        load_kernel,
        [((N_CTX, 3, PART, D), BF)],
        after(shared_weights, *results),
        loose=1,
        sems=(1,),
        limit=24,
        flops=0,
    )
    partner_mine, shared_here, *returned = group(partner_mine, shared_here, *returned)
    partner_theirs = swap_core(partner_mine)

    def shared(own, other):
        return call(
            shared_kernel,
            [((T_DEV, D), F32), token_rows],
            place,
            own,
            other,
            shared_here,
            scratch=[((D, T_CHIP), BF), ((N_CTX * PART, T_CHIP), BF)],
            scalars=1,
            flops=0,
        )

    partner_kept, partner_sent = shared(partner_mine, partner_theirs)
    partner_other = swap_core(partner_sent)
    partner_sum = partner_kept + partner_other.astype(F32)
    from_partner = swap(partner_sum.astype(BF), "x", 1)
    own_kept, own_sent = shared(after(mine, partner_other), theirs)
    kept, sent = call(
        combine_kernel,
        [((T_DEV, D), F32), token_rows],
        own_kept,
        own_sent,
        back,
        results[0],
        *returned,
        scratch=[((4 * SLOTS, D), BF)],
        flops=0,
    )
    return (stream + kept + swap_core(after(sent, from_partner)).astype(F32) + from_partner.astype(F32)).astype(BF)


def solution(mesh):
    fine = Mesh(mesh.devices.reshape(4, 2, 2, 4, 2), ("y", "zh", "zl", "x", "core"))
    ctx = ("y", "zh", "zl")
    exp = ("x", "core")
    return jax.shard_map(
        on_device,
        mesh=fine,
        in_specs=(
            P(ctx + exp, None),
            P(ctx, exp),
            P(ctx, exp),
            P(ctx, exp),
            P(exp, ctx),
            P(exp),
            P(exp, None),
            P(),
            P(),
            P(ctx + exp, None),
            P(exp, None, None),
            P(exp, None, None),
            P(exp, None, None),
            P(None, ctx),
            P(None, ctx),
            P(ctx, None),
        ),
        out_specs=P(ctx + exp, None),
        check_vma=False,
    )
```

time: 199 us -> 137 us (0.69)
  waiting for transfers between devices: 54.3 us -> 35.8 us
  Pallas kernels: 49.1 us -> 33.6 us
  starting transfers between devices: 49.4 us -> 38.7 us
  local copies, waits for them, and re-layouts: 22 us -> 13.5 us
  other arithmetic: 8.98 us -> 1.19 us
    ppermute x23 -> x16, waiting for transfers between devices: 46.1 us -> 21.8 us  [the longest x6 11 us: swap(): return lax.ppermute(a, axis, [(i, i ^ bit) for i in range(count)])]
    pallas_call x10 -> x15, Pallas kernels: 49.1 us -> 33.6 us  [call(): pl.pallas_call(kernel, in_specs=[SM] * scalars + [VM] * (len(args) - scal...]
    ppermute x23 -> x16, starting transfers between devices: 34.4 us -> 26.7 us  [the longest x6 13.1 us: swap(): return lax.ppermute(a, axis, [(i, i ^ bit) for i in range(count)])]
    select_n x4 -> x0, other arithmetic: 6.27 us -> none  [the longest x3 6.13 us: in_order(): jnp.where(core == 0, jnp.concatenate([own, other], 0), jnp.concatenate([o...]
    ppermute x6 -> x5, waiting for transfers between devices: 3 us -> 6.9 us  [swap_core(): return lax.ppermute(a, 'core', [(0, 1), (1, 0)])]
    slice x5 -> x2, local copies, waits for them, and re-layouts: 3.27 us -> 0.08 us  [the longest x1 0.04 us: on_device(): after(proj_high, message)[T_DEV:]]
    ppermute x3, waiting for transfers between devices: 4.42 us -> 7.16 us  [on_device(): heads = [lax.ppermute(normed[d], 'x', ring(d)) for d in (1, 2, 3)]]
    ppermute x3, starting transfers between devices: 4.93 us -> 2.74 us  [on_device(): heads = [lax.ppermute(normed[d], 'x', ring(d)) for d in (1, 2, 3)]]
  transfers between devices with their start and end apart: 33 -> 25, of which waited for: 14 -> 14; matrix products, arithmetic and copies ran while one was open for 9% -> 0% of each run, Pallas kernels for 21% -> 19%
where the time goes in v2:
time: 137 us
  starting transfers between devices  38.7 us (28%)
  waiting for transfers between devices  35.8 us (26%)
  Pallas kernels  33.6 us (25%)
  between operations  13.7 us (10%)
  local copies, waits for them, and re-layouts  13.5 us (10%)
    pallas_call x15, Pallas kernels, call(): pl.pallas_call(kernel, in_specs=[SM] * scalars + [VM] * (len(args) - scal...  33.6 us
    ppermute x6, starting transfers between devices, swap(): return lax.ppermute(a, axis, [(i, i ^ bit) for i in range(count)])  13.1 us
    unnamed x50, local copies, waits for them, and re-layouts  12.6 us
    ppermute x6, waiting for transfers between devices, swap(): return lax.ppermute(a, axis, [(i, i ^ bit) for i in range(count)])  11 us
    ppermute x5, starting transfers between devices, swap_core(): return lax.ppermute(a, 'core', [(0, 1), (1, 0)])  9.21 us
    ppermute x3, waiting for transfers between devices, on_device(): heads = [lax.ppermute(normed[d], 'x', ring(d)) for d in (1, 2, 3)]  7.16 us
    ppermute x5, waiting for transfers between devices, swap_core(): return lax.ppermute(a, 'core', [(0, 1), (1, 0)])  6.9 us
    ppermute x3, waiting for transfers between devices, on_device(): returned = [lax.ppermute(results[d], 'x', ring(4 - d)) for d in (1, 2, 3)]  6.87 us
  transfers between devices with their start and end apart: 25, of which 14 were waited for; matrix products, arithmetic and copies ran while one was open for 0% of the time, Pallas kernels for 19%

profile of v2, /device:TPU:1, one launch (start us, length us, event | category | flops | bytes accessed | tf_op | source)
XLA Modules:
  0.0 136.6 jit_solution(14900736634134716333)
XLA Ops:
  6.5 0.7 stack.31.place_ref
  7.2 4.3 %states.1 = (f32[4,2,128,128]{3,2,1,0:T(8,128)}, f32[4,2,128]{2,1,0:T(2,128)}, bf16[272,128]{1,0:T(8,128)(2,1)}, bf16[3,48,2048]{2,1,0:T(8,128)(2,1)}) custom-call(s32[7]{0:T(128)} %stack.31.place_ref, f32[2,1024]{1,0:T(2,128)} %decay_ref.5, bf16[1024,256]{1,0:T(8,128)(2,1)} %key_ref.3, bf16[1024,256]{1,0:T(8,128)(2,1)} %value_ref.3, ...), custom_call_target="tpu_custom_call" | custom-call | flops 1000000000 | bytes 4407324 | tf_op jit(solution)/shard_map/states/pallas_call | solution.py:383
  11.5 2.1 %collective-permute-start.4 = (bf16[256,2048]{1,0:T(8,128)(2,1)}, bf16[256,2048]{1,0:T(8,128)(2,1)S(1)}, u32[]{:S(2)}, u32[]{:S(2)}) collective-permute-start(bf16[256,2048]{1,0:T(8,128)(2,1)} %w0_ref.1), channel_id=1, source_target_pairs={{0,2},{2,4},{4,6},{6,0},{1,3},{3,5},{5,7},{7,1},{8,10},{10,12},{12... | collective-permute-start | bytes 3145736 | tf_op jit(solution)/shard_map/ppermute | solution.py:443
  13.6 1.3 collective-permute-start.5
  15.0 1.8 %collective-permute-start = (bf16[272,128]{1,0:T(8,128)(2,1)}, bf16[272,128]{1,0:T(8,128)(2,1)S(1)}, u32[]{:S(2)}, u32[]{:S(2)}) collective-permute-start(bf16[272,128]{1,0:T(8,128)(2,1)} %get-tuple-element.78.own_ref), channel_id=1, source_target_pairs={{0,8},{8,0},{1,9},{9,1},{2,10},{10,2},{3,11},{11,3},{4,12},{12,4},... | collective-permute-start | bytes 208904 | tf_op jit(solution)/shard_map/ppermute | solution.py:413
  16.7 2.2 %collective-permute-done.other_ref = bf16[272,128]{1,0:T(8,128)(2,1)S(1)} collective-permute-done((bf16[272,128]{1,0:T(8,128)(2,1)}, bf16[272,128]{1,0:T(8,128)(2,1)S(1)}, u32[]{:S(2)}, u32[]{:S(2)}) %collective-permute-start) | collective-permute-done | bytes 69664 | tf_op jit(solution)/shard_map/ppermute | solution.py:413
  18.9 0.7 copy-done.1
  19.6 0.9 copy-done.10
  20.5 0.6 step0.1
  21.1 0.7 copy-done.18
  21.8 3.4 %collective-permute-start.1 = (bf16[272,128]{1,0:T(8,128)(2,1)S(1)}, bf16[272,128]{1,0:T(8,128)(2,1)S(1)}, u32[]{:S(2)}, u32[]{:S(2)}) collective-permute-start(bf16[272,128]{1,0:T(8,128)(2,1)S(1)} %get-tuple-element.79.own_ref), channel_id=1, source_target_pairs={{0,16},{16,0},{1,17},{17,1},{2,18},{18,2},{3,19},{19,3},{4,20},{20... | collective-permute-start | bytes 208904 | tf_op jit(solution)/shard_map/ppermute | solution.py:413
  25.3 2.4 %collective-permute-start.6 = (s32[128,6]{1,0:T(8,128)S(1)}, s32[128,6]{1,0:T(8,128)S(1)}, u32[]{:S(2)}, u32[]{:S(2)}) collective-permute-start(s32[128,6]{1,0:T(8,128)S(1)} %copy.19), channel_id=1, source_target_pairs={{0,1},{1,0},{2,3},{3,2},{4,5},{5,4},{6,7},{7,6},{8,9},{9,8},{10,11... | collective-permute-start | bytes 9224 | tf_op jit(solution)/shard_map/ppermute | solution.py:408
  27.7 0.9 copy-done.19
  28.6 0.6 step1.1
  29.3 0.6 copy-done.20
  29.9 1.3 collective-permute-start.2
  31.2 1.0 copy-done.6
  32.3 1.0 inner.1.inner_ref
  33.3 1.0 copy-done.15
  34.4 1.0 copy-done.21
  35.4 0.6 step2.1
  36.0 2.7 %collective-permute-start.3 = (bf16[272,128]{1,0:T(8,128)(2,1)S(1)}, bf16[272,128]{1,0:T(8,128)(2,1)S(1)}, u32[]{:S(2)}, u32[]{:S(2)}) collective-permute-start(bf16[272,128]{1,0:T(8,128)(2,1)S(1)} %get-tuple-element.90), channel_id=1, source_target_pairs={{0,64},{32,96},{64,0},{96,32},{1,65},{33,97},{65,1},{97,33},{2,66}... | collective-permute-start | bytes 208904 | tf_op jit(solution)/shard_map/ppermute | solution.py:413
  38.7 1.3 route.1
  40.1 2.0 %collective-permute-done.3.other_ref = bf16[272,128]{1,0:T(8,128)(2,1)S(1)} collective-permute-done((bf16[272,128]{1,0:T(8,128)(2,1)S(1)}, bf16[272,128]{1,0:T(8,128)(2,1)S(1)}, u32[]{:S(2)}, u32[]{:S(2)}) %collective-permute-start.3) | collective-permute-done | bytes 69664 | tf_op jit(solution)/shard_map/ppermute | solution.py:413
  42.0 0.2 collective-permute-start.10
  42.3 2.4 %collective-permute-start.11 = (bf16[128,2048]{1,0:T(8,128)(2,1)S(1)}, bf16[128,2048]{1,0:T(8,128)(2,1)S(1)}, u32[]{:S(2)}, u32[]{:S(2)}) collective-permute-start(bf16[128,2048]{1,0:T(8,128)(2,1)S(1)} %slice.7), channel_id=1, source_target_pairs={{0,6},{2,0},{4,2},{6,4},{1,7},{3,1},{5,3},{7,5},{8,14},{10,8},{12,... | collective-permute-start | bytes 1572872 | tf_op jit(solution)/shard_map/ppermute | solution.py:519
  44.7 1.0 copy-done.7
  45.8 1.0 copy-done.14
  46.8 2.4 %mix.1 = (bf16[256,256]{1,0:T(8,128)(2,1)S(1)}, bf16[256,256]{1,0:T(8,128)(2,1)S(1)}, bf16[256,256]{1,0:T(8,128)(2,1)S(1)}, bf16[256,256]{1,0:T(8,128)(2,1)S(1)}) custom-call(s32[7]{0:T(128)S(1)} %copy-done.2, bf16[1024,256]{1,0:T(8,128)(2,1)S(1)} %copy-done.7, f32[2,1024]{1,0:T(2,128)S(1)} %copy-done.11, f32[1024,256]{1,0:T(8,128)S(1)} %copy-done.16, ...), custom_call_target="tpu_custom_call" | custom-call | flops 1000000000 | bytes 2836508 | tf_op jit(solution)/shard_map/mix/pallas_call | solution.py:383
  49.3 1.5 %collective-permute-start.8 = (bf16[256,256]{1,0:T(8,128)(2,1)S(1)}, bf16[256,256]{1,0:T(8,128)(2,1)S(1)}, u32[]{:S(2)}, u32[]{:S(2)}) collective-permute-start(bf16[256,256]{1,0:T(8,128)(2,1)S(1)} %get-tuple-element.100), channel_id=1, source_target_pairs={{0,4},{2,6},{4,0},{6,2},{1,5},{3,7},{5,1},{7,3},{8,12},{10,14},{12... | collective-permute-start | bytes 393224 | tf_op jit(solution)/shard_map/ppermute | solution.py:520
  50.8 1.2 collective-permute-start.9
  52.0 4.2 %collective-permute-done.7.one_ref = bf16[256,256]{1,0:T(8,128)(2,1)S(1)} collective-permute-done((bf16[256,256]{1,0:T(8,128)(2,1)S(1)}, bf16[256,256]{1,0:T(8,128)(2,1)S(1)}, u32[]{:S(2)}, u32[]{:S(2)}) %collective-permute-start.7) | collective-permute-done | bytes 131104 | tf_op jit(solution)/shard_map/ppermute | solution.py:520
  56.2 2.5 %collective-permute-done.8.two_ref = bf16[256,256]{1,0:T(8,128)(2,1)S(1)} collective-permute-done((bf16[256,256]{1,0:T(8,128)(2,1)S(1)}, bf16[256,256]{1,0:T(8,128)(2,1)S(1)}, u32[]{:S(2)}, u32[]{:S(2)}) %collective-permute-start.8) | collective-permute-done | bytes 131104 | tf_op jit(solution)/shard_map/ppermute | solution.py:520
  58.7 0.4 collective-permute-done.9.three_ref
  59.2 2.1 %project.1 = (f32[256,2048]{1,0:T(8,128)S(1)}, bf16[256,2048]{1,0:T(8,128)(2,1)S(1)}) custom-call(s32[7]{0:T(128)S(1)} %copy-done.2, bf16[256,256]{1,0:T(8,128)(2,1)S(1)} %get-tuple-element.98.own_ref, bf16[256,256]{1,0:T(8,128)(2,1)S(1)} %collective-permute-done.7.one_ref, bf16[256,256]{1,0:T(8,128)(2,1)S(1)} %collective-permute-done.8.two_ref, ...), custom_call_target="tpu_custom_call" | custom-call | flops 6000000000 | bytes 8388636 | tf_op jit(solution)/shard_map/project/pallas_call | solution.py:383
  61.3 4.2 %collective-permute-start.12 = (bf16[256,2048]{1,0:T(8,128)(2,1)S(1)}, bf16[256,2048]{1,0:T(8,128)(2,1)S(1)}, u32[]{:S(2)}, u32[]{:S(2)}) collective-permute-start(bf16[256,2048]{1,0:T(8,128)(2,1)S(1)} %get-tuple-element.110), channel_id=1, source_target_pairs={{0,1},{1,0},{2,3},{3,2},{4,5},{5,4},{6,7},{7,6},{8,9},{9,8},{10,11... | collective-permute-start | bytes 3145736 | tf_op jit(solution)/shard_map/ppermute | solution.py:408
  65.5 2.3 %collective-permute-done.12.other_ref = bf16[256,2048]{1,0:T(8,128)(2,1)S(1)} collective-permute-done((bf16[256,2048]{1,0:T(8,128)(2,1)S(1)}, bf16[256,2048]{1,0:T(8,128)(2,1)S(1)}, u32[]{:S(2)}, u32[]{:S(2)}) %collective-permute-start.12) | collective-permute-done | bytes 1048608 | tf_op jit(solution)/shard_map/ppermute | solution.py:408
  67.8 1.9 %norm.1 = (f32[128,2048]{1,0:T(8,128)S(1)}, bf16[128,2048]{1,0:T(8,128)(2,1)S(1)}, bf16[128,2048]{1,0:T(8,128)(2,1)S(1)}, bf16[48,2048]{1,0:T(8,128)(2,1)S(1)}, ...) custom-call(s32[7]{0:T(128)S(1)} %copy-done.2, ...), custom_call_target="tpu_custom_call" | custom-call | flops 30000001024 | bytes 6660124 | tf_op jit(solution)/shard_map/norm/pallas_call | solution.py:383
  69.7 0.9 collective-permute-start.13
  70.6 3.0 %collective-permute-start.14 = (bf16[48,2048]{1,0:T(8,128)(2,1)S(1)}, bf16[48,2048]{1,0:T(8,128)(2,1)S(1)}, u32[]{:S(2)}, u32[]{:S(2)}) collective-permute-start(bf16[48,2048]{1,0:T(8,128)(2,1)S(1)} %get-tuple-element.116), channel_id=1, source_target_pairs={{0,4},{2,6},{4,0},{6,2},{1,5},{3,7},{5,1},{7,3},{8,12},{10,14},{12... | collective-permute-start | bytes 589832 | tf_op jit(solution)/shard_map/ppermute | solution.py:556
  73.6 4.9 %load.2 = (bf16[2048,1408]{1,0:T(8,128)(2,1)S(1)}, bf16[2048,1408]{1,0:T(8,128)(2,1)S(1)}, bf16[1408,2048]{1,0:T(8,128)(2,1)S(1)}) custom-call(bf16[2048,1408]{1,0:T(8,128)(2,1)S(1)} %bitcast.19, bf16[2048,1408]{1,0:T(8,128)(2,1)} %bitcast.23, bf16[1408,2048]{1,0:T(8,128)(2,1)} %bitcast.24), custom_call_target="tpu_custom_call" | custom-call | flops 1000000000 | bytes 34603008 | tf_op jit(solution)/shard_map/load/pallas_call | solution.py:383
  78.6 3.9 %collective-permute-done.14.two_ref = bf16[48,2048]{1,0:T(8,128)(2,1)S(1)} collective-permute-done((bf16[48,2048]{1,0:T(8,128)(2,1)S(1)}, bf16[48,2048]{1,0:T(8,128)(2,1)S(1)}, u32[]{:S(2)}, u32[]{:S(2)}) %collective-permute-start.14) | collective-permute-done | bytes 196640 | tf_op jit(solution)/shard_map/ppermute | solution.py:556
  82.4 1.1 collective-permute-start.16
  83.5 4.6 %expert.1 = (bf16[48,2048]{1,0:T(8,128)(2,1)S(1)}, bf16[48,2048]{1,0:T(8,128)(2,1)}, bf16[48,2048]{1,0:T(8,128)(2,1)}, bf16[48,2048]{1,0:T(8,128)(2,1)}) custom-call(bf16[48,2048]{1,0:T(8,128)(2,1)S(1)} %get-tuple-element.127.own_ref, bf16[48,2048]{1,0:T(8,128)(2,1)S(1)} %collective-permute-done.13.one_ref, ...), custom_call_target="tpu_custom_call" | custom-call | flops 1000000000 | bytes 18874368 | tf_op jit(solution)/shard_map/expert/pallas_call | solution.py:383
  88.2 1.6 %collective-permute-start.17 = (bf16[48,2048]{1,0:T(8,128)(2,1)}, bf16[48,2048]{1,0:T(8,128)(2,1)S(1)}, u32[]{:S(2)}, u32[]{:S(2)}) collective-permute-start(bf16[48,2048]{1,0:T(8,128)(2,1)} %get-tuple-element.132), channel_id=1, source_target_pairs={{0,6},{2,0},{4,2},{6,4},{1,7},{3,1},{5,3},{7,5},{8,14},{10,8},{12,... | collective-permute-start | bytes 589832 | tf_op jit(solution)/shard_map/ppermute | solution.py:579
  89.8 1.2 collective-permute-start.18
  91.0 0.9 collective-permute-start.19
  91.8 3.7 %copy-done = bf16[48,48,2048]{2,1,0:T(8,128)(2,1)S(1)} copy-done((bf16[48,48,2048]{2,1,0:T(8,128)(2,1)S(1)}, bf16[48,48,2048]{2,1,0:T(8,128)(2,1)}, u32[]{:S(2)}) %copy-start) | copy-done | bytes 9437208
  95.5 0.6 load.3.weights_ref
  96.1 2.8 %collective-permute-done.17.two_ref = bf16[48,2048]{1,0:T(8,128)(2,1)S(1)} collective-permute-done((bf16[48,2048]{1,0:T(8,128)(2,1)}, bf16[48,2048]{1,0:T(8,128)(2,1)S(1)}, u32[]{:S(2)}, u32[]{:S(2)}) %collective-permute-start.17) | collective-permute-done | bytes 196640 | tf_op jit(solution)/shard_map/ppermute | solution.py:579
  99.0 3.3 %collective-permute-done.18.three_ref = bf16[48,2048]{1,0:T(8,128)(2,1)S(1)} collective-permute-done((bf16[48,2048]{1,0:T(8,128)(2,1)}, bf16[48,2048]{1,0:T(8,128)(2,1)S(1)}, u32[]{:S(2)}, u32[]{:S(2)}) %collective-permute-start.18) | collective-permute-done | bytes 196640 | tf_op jit(solution)/shard_map/ppermute | solution.py:579
  102.2 0.8 collective-permute-done.19.four_ref
  103.0 1.3 collective-permute-start.20
  104.3 1.5 %collective-permute-done.20.other_ref = bf16[128,2048]{1,0:T(8,128)(2,1)S(1)} collective-permute-done((bf16[128,2048]{1,0:T(8,128)(2,1)S(1)}, bf16[128,2048]{1,0:T(8,128)(2,1)S(1)}, u32[]{:S(2)}, u32[]{:S(2)}) %collective-permute-start.20) | collective-permute-done | bytes 524320 | tf_op jit(solution)/shard_map/ppermute | solution.py:408
  105.8 3.5 %shared.2 = (f32[128,2048]{1,0:T(8,128)S(1)}, bf16[128,2048]{1,0:T(8,128)(2,1)S(1)}) custom-call(s32[7]{0:T(128)S(1)} %copy-done.2, bf16[128,2048]{1,0:T(8,128)(2,1)S(1)} %collective-permute-done.16.own_ref, bf16[128,2048]{1,0:T(8,128)(2,1)S(1)} %collective-permute-done.20.other_ref, bf16[16,3,48,2048]{3,2,1,0:T(8,128)(2,1)S(1)} %load.3.weights_ref), custom_call_target="tpu_custom_call" | custom-call | tf_op jit(solution)/shard_map/shared/pallas_call | solution.py:383
  109.3 0.5 collective-permute-start.21
  109.7 1.5 %collective-permute-done.21 = bf16[128,2048]{1,0:T(8,128)(2,1)S(1)} collective-permute-done((bf16[128,2048]{1,0:T(8,128)(2,1)S(1)}, bf16[128,2048]{1,0:T(8,128)(2,1)S(1)}, u32[]{:S(2)}, u32[]{:S(2)}) %collective-permute-start.21) | collective-permute-done | bytes 524320 | tf_op jit(solution)/shard_map/ppermute | solution.py:408
  111.4 2.8 %collective-permute-start.22 = (bf16[128,2048]{1,0:T(8,128)(2,1)S(1)}, bf16[128,2048]{1,0:T(8,128)(2,1)S(1)}, u32[]{:S(2)}, u32[]{:S(2)}) collective-permute-start(bf16[128,2048]{1,0:T(8,128)(2,1)S(1)} %add_convert_fusion.1), channel_id=1, source_target_pairs={{0,2},{2,0},{4,6},{6,4},{1,3},{3,1},{5,7},{7,5},{8,10},{10,8},{12,... | collective-permute-start | bytes 1572872 | tf_op jit(solution)/shard_map/ppermute | solution.py:413
  114.2 3.5 %shared.3 = (f32[128,2048]{1,0:T(8,128)S(1)}, bf16[128,2048]{1,0:T(8,128)(2,1)S(1)}) custom-call(s32[7]{0:T(128)S(1)} %copy-done.2, bf16[128,2048]{1,0:T(8,128)(2,1)S(1)} %get-tuple-element.139.own_ref, bf16[128,2048]{1,0:T(8,128)(2,1)S(1)} %get-tuple-element.140.other_ref, bf16[16,3,48,2048]{3,2,1,0:T(8,128)(2,1)S(1)} %load.3.weights_ref), custom_call_target="tpu_custom_call" | custom-call | tf_op jit(solution)/shard_map/shared/pallas_call | solution.py:383
  117.7 1.7 %combine.1 = (f32[128,2048]{1,0:T(8,128)S(1)}, bf16[128,2048]{1,0:T(8,128)(2,1)S(1)}) custom-call(f32[128,2048]{1,0:T(8,128)S(1)} %get-tuple-element.141.mine_ref, bf16[128,2048]{1,0:T(8,128)(2,1)S(1)} %get-tuple-element.142.theirs_ref, bf16[256,384]{1,0:T(8,128)(2,1)S(1)} %get-tuple-element.143.back_ref, bf16[48,2048]{1,0:T(8,128)(2,1)S(1)} %get-tuple-element.131.one_ref, ...), custom_call_target="tpu_custom_call" | custom-call | tf_op jit(solution)/shard_map/combine/pallas_call | solution.py:383
  119.4 6.8 %collective-permute-done.22 = bf16[128,2048]{1,0:T(8,128)(2,1)S(1)} collective-permute-done((bf16[128,2048]{1,0:T(8,128)(2,1)S(1)}, bf16[128,2048]{1,0:T(8,128)(2,1)S(1)}, u32[]{:S(2)}, u32[]{:S(2)}) %collective-permute-start.22) | collective-permute-done | bytes 524320 | tf_op jit(solution)/shard_map/ppermute | solution.py:413
  126.2 0.9 collective-permute-start.23
  127.1 1.5 %collective-permute-done.23 = bf16[128,2048]{1,0:T(8,128)(2,1)S(1)} collective-permute-done((bf16[128,2048]{1,0:T(8,128)(2,1)S(1)}, bf16[128,2048]{1,0:T(8,128)(2,1)S(1)}, u32[]{:S(2)}, u32[]{:S(2)}) %collective-permute-start.23) | collective-permute-done | bytes 524320 | tf_op jit(solution)/shard_map/ppermute | solution.py:408
  128.7 1.1 add_convert_fusion
  (60 shorter events, 0.6 us)
Async XLA Ops:
  6.5 18.6 %copy-start.22 = (s32[128,6]{0,1:T(8,128)S(1)}, s32[128,6]{0,1:T(8,128)}, u32[]{:S(2)}) copy-start(s32[128,6]{0,1:T(8,128)} %param.25) | copy-start | bytes 9220
  6.5 85.3 %all-gather.3.cloned.1.call-start = ((), (), s32[]{:S(2)}) async-start(), calls=%async_computation | async-start | bytes 10027008 | tf_op jit(solution)/shard_map/all_gather | solution.py:467
  7.2 20.5 %copy-start.2 = (s32[7]{0:T(128)S(1)}, s32[7]{0:T(128)}, u32[]{:S(2)}) copy-start(s32[7]{0:T(128)} %stack.31.place_ref) | copy-start | bytes 88
  7.2 24.0 %copy-start.4 = (bf16[1024,256]{1,0:T(8,128)(2,1)S(1)}, bf16[1024,256]{1,0:T(8,128)(2,1)}, u32[]{:S(2)}) copy-start(bf16[1024,256]{1,0:T(8,128)(2,1)} %key_ref.3) | copy-start | bytes 1572868
  7.2 24.0 %copy-start.5 = (bf16[1024,256]{1,0:T(8,128)(2,1)S(1)}, bf16[1024,256]{1,0:T(8,128)(2,1)}, u32[]{:S(2)}) copy-start(bf16[1024,256]{1,0:T(8,128)(2,1)} %value_ref.3) | copy-start | bytes 1572868
  7.2 24.0 %copy-start.11 = (f32[2,1024]{1,0:T(2,128)S(1)}, f32[2,1024]{1,0:T(2,128)}, u32[]{:S(2)}) copy-start(f32[2,1024]{1,0:T(2,128)} %decay_ref.5) | copy-start | bytes 24580
  11.5 28.4 %collective-permute-start.4 = (bf16[256,2048]{1,0:T(8,128)(2,1)}, bf16[256,2048]{1,0:T(8,128)(2,1)S(1)}, u32[]{:S(2)}, u32[]{:S(2)}) collective-permute-start(bf16[256,2048]{1,0:T(8,128)(2,1)} %w0_ref.1), channel_id=1, source_target_pairs={{0,2},{2,4},{4,6},{6,0},{1,3},{3,5},{5,7},{7,1},{8,10},{10,12},{12... | collective-permute-start | bytes 3145736 | tf_op jit(solution)/shard_map/ppermute | solution.py:443
  13.6 26.4 %collective-permute-start.5 = (bf16[256,2048]{1,0:T(8,128)(2,1)}, bf16[256,2048]{1,0:T(8,128)(2,1)S(1)}, u32[]{:S(2)}, u32[]{:S(2)}) collective-permute-start(bf16[256,2048]{1,0:T(8,128)(2,1)} %w0_ref.1), channel_id=1, source_target_pairs={{0,6},{2,0},{4,2},{6,4},{1,7},{3,1},{5,3},{7,5},{8,14},{10,8},{12,... | collective-permute-start | bytes 3145736 | tf_op jit(solution)/shard_map/ppermute | solution.py:444
  15.0 4.0 %collective-permute-start = (bf16[272,128]{1,0:T(8,128)(2,1)}, bf16[272,128]{1,0:T(8,128)(2,1)S(1)}, u32[]{:S(2)}, u32[]{:S(2)}) collective-permute-start(bf16[272,128]{1,0:T(8,128)(2,1)} %get-tuple-element.78.own_ref), channel_id=1, source_target_pairs={{0,8},{8,0},{1,9},{9,1},{2,10},{10,2},{3,11},{11,3},{4,12},{12,4},... | collective-permute-start | bytes 208904 | tf_op jit(solution)/shard_map/ppermute | solution.py:413
  18.9 0.7 copy-start.1
  19.6 0.9 copy-start.10
  21.1 0.7 copy-start.18
  21.8 6.0 %collective-permute-start.1 = (bf16[272,128]{1,0:T(8,128)(2,1)S(1)}, bf16[272,128]{1,0:T(8,128)(2,1)S(1)}, u32[]{:S(2)}, u32[]{:S(2)}) collective-permute-start(bf16[272,128]{1,0:T(8,128)(2,1)S(1)} %get-tuple-element.79.own_ref), channel_id=1, source_target_pairs={{0,16},{16,0},{1,17},{17,1},{2,18},{18,2},{3,19},{19,3},{4,20},{20... | collective-permute-start | bytes 208904 | tf_op jit(solution)/shard_map/ppermute | solution.py:413
  25.3 13.4 %collective-permute-start.6 = (s32[128,6]{1,0:T(8,128)S(1)}, s32[128,6]{1,0:T(8,128)S(1)}, u32[]{:S(2)}, u32[]{:S(2)}) collective-permute-start(s32[128,6]{1,0:T(8,128)S(1)} %copy.19), channel_id=1, source_target_pairs={{0,1},{1,0},{2,3},{3,2},{4,5},{5,4},{6,7},{7,6},{8,9},{9,8},{10,11... | collective-permute-start | bytes 9224 | tf_op jit(solution)/shard_map/ppermute | solution.py:408
  27.7 0.9 copy-start.19
  29.3 0.6 copy-start.20
  29.9 4.5 %collective-permute-start.2 = (bf16[272,128]{1,0:T(8,128)(2,1)S(1)}, bf16[272,128]{1,0:T(8,128)(2,1)S(1)}, u32[]{:S(2)}, u32[]{:S(2)}) collective-permute-start(bf16[272,128]{1,0:T(8,128)(2,1)S(1)} %get-tuple-element.85.own_ref), channel_id=1, source_target_pairs={{0,32},{32,0},{64,96},{96,64},{1,33},{33,1},{65,97},{97,65},{2,34}... | collective-permute-start | bytes 208904 | tf_op jit(solution)/shard_map/ppermute | solution.py:413
  31.2 1.1 copy-start.6
  32.3 12.5 %copy-start.13 = (f32[256]{0:T(256)S(1)}, f32[256]{0:T(256)}, u32[]{:S(2)}) copy-start(f32[256]{0:T(256)} %param.21) | copy-start | bytes 3076
  32.3 12.5 %copy-start.17 = (f32[4,2,128]{2,1,0:T(2,128)S(1)}, f32[4,2,128]{2,1,0:T(2,128)}, u32[]{:S(2)}) copy-start(f32[4,2,128]{2,1,0:T(2,128)} %get-tuple-element.82.passed_ref) | copy-start | bytes 12292
  33.3 1.0 copy-start.15
  34.4 10.4 %copy-start.16 = (f32[1024,256]{1,0:T(8,128)S(1)}, f32[1024,256]{1,0:T(8,128)}, u32[]{:S(2)}) copy-start(f32[1024,256]{1,0:T(8,128)} %copy-done.15) | copy-start | bytes 3145732
  34.4 1.0 copy-start.21
  35.4 23.8 %copy-start.3 = (bf16[256,2048]{1,0:T(8,128)(2,1)S(1)}, bf16[256,2048]{1,0:T(8,128)(2,1)}, u32[]{:S(2)}) copy-start(bf16[256,2048]{1,0:T(8,128)(2,1)} %w0_ref.1) | copy-start | bytes 3145732
  35.4 23.8 %copy-start.8 = (bf16[128,2048]{1,0:T(8,128)(2,1)S(1)}, bf16[128,2048]{1,0:T(8,128)(2,1)}, u32[]{:S(2)}) copy-start(bf16[128,2048]{1,0:T(8,128)(2,1)} %residual_ref.1) | copy-start | bytes 1572868
  36.0 6.1 %collective-permute-start.3 = (bf16[272,128]{1,0:T(8,128)(2,1)S(1)}, bf16[272,128]{1,0:T(8,128)(2,1)S(1)}, u32[]{:S(2)}, u32[]{:S(2)}) collective-permute-start(bf16[272,128]{1,0:T(8,128)(2,1)S(1)} %get-tuple-element.90), channel_id=1, source_target_pairs={{0,64},{32,96},{64,0},{96,32},{1,65},{33,97},{65,1},{97,33},{2,66}... | collective-permute-start | bytes 208904 | tf_op jit(solution)/shard_map/ppermute | solution.py:413
  42.0 17.1 %collective-permute-start.10 = (bf16[128,2048]{1,0:T(8,128)(2,1)S(1)}, bf16[128,2048]{1,0:T(8,128)(2,1)S(1)}, u32[]{:S(2)}, u32[]{:S(2)}) collective-permute-start(bf16[128,2048]{1,0:T(8,128)(2,1)S(1)} %slice.6), channel_id=1, source_target_pairs={{0,2},{2,4},{4,6},{6,0},{1,3},{3,5},{5,7},{7,1},{8,10},{10,12},{12... | collective-permute-start | bytes 1572872 | tf_op jit(solution)/shard_map/ppermute | solution.py:518
  42.3 16.9 %collective-permute-start.11 = (bf16[128,2048]{1,0:T(8,128)(2,1)S(1)}, bf16[128,2048]{1,0:T(8,128)(2,1)S(1)}, u32[]{:S(2)}, u32[]{:S(2)}) collective-permute-start(bf16[128,2048]{1,0:T(8,128)(2,1)S(1)} %slice.7), channel_id=1, source_target_pairs={{0,6},{2,0},{4,2},{6,4},{1,7},{3,1},{5,3},{7,5},{8,14},{10,8},{12,... | collective-permute-start | bytes 1572872 | tf_op jit(solution)/shard_map/ppermute | solution.py:519
  44.7 1.0 copy-start.7
  45.8 1.0 copy-start.14
  49.2 7.0 %collective-permute-start.7 = (bf16[256,256]{1,0:T(8,128)(2,1)S(1)}, bf16[256,256]{1,0:T(8,128)(2,1)S(1)}, u32[]{:S(2)}, u32[]{:S(2)}) collective-permute-start(bf16[256,256]{1,0:T(8,128)(2,1)S(1)} %get-tuple-element.99), channel_id=1, source_target_pairs={{0,2},{2,4},{4,6},{6,0},{1,3},{3,5},{5,7},{7,1},{8,10},{10,12},{12... | collective-permute-start | bytes 393224 | tf_op jit(solution)/shard_map/ppermute | solution.py:520
  49.3 9.4 %collective-permute-start.8 = (bf16[256,256]{1,0:T(8,128)(2,1)S(1)}, bf16[256,256]{1,0:T(8,128)(2,1)S(1)}, u32[]{:S(2)}, u32[]{:S(2)}) collective-permute-start(bf16[256,256]{1,0:T(8,128)(2,1)S(1)} %get-tuple-element.100), channel_id=1, source_target_pairs={{0,4},{2,6},{4,0},{6,2},{1,5},{3,7},{5,1},{7,3},{8,12},{10,14},{12... | collective-permute-start | bytes 393224 | tf_op jit(solution)/shard_map/ppermute | solution.py:520
  50.8 8.4 %collective-permute-start.9 = (bf16[256,256]{1,0:T(8,128)(2,1)S(1)}, bf16[256,256]{1,0:T(8,128)(2,1)S(1)}, u32[]{:S(2)}, u32[]{:S(2)}) collective-permute-start(bf16[256,256]{1,0:T(8,128)(2,1)S(1)} %get-tuple-element.101), channel_id=1, source_target_pairs={{0,6},{2,0},{4,2},{6,4},{1,7},{3,1},{5,3},{7,5},{8,14},{10,8},{12,... | collective-permute-start | bytes 393224 | tf_op jit(solution)/shard_map/ppermute | solution.py:520
  59.2 8.6 %copy-start.9 = (bf16[2048,64]{0,1:T(8,128)(2,1)S(1)}, bf16[2048,64]{0,1:T(8,128)(2,1)}, u32[]{:S(2)}) copy-start(bf16[2048,64]{0,1:T(8,128)(2,1)} %param.24) | copy-start | bytes 786436
  59.2 8.6 %copy-start.12 = (f32[2048]{0:T(1024)S(1)}, f32[2048]{0:T(1024)}, u32[]{:S(2)}) copy-start(f32[2048]{0:T(1024)} %param.23) | copy-start | bytes 24580
  59.2 14.4 %slice-start = ((s8[5767168]{0:T(1024)(128)(4,1)}), s8[4194304]{0:T(1024)(128)(4,1)S(1)}, s32[]{:S(2)}) async-start(s8[5767168]{0:T(1024)(128)(4,1)} %bitcast.17), calls=%async_computation.1 | async-start | bytes 8388608
  61.3 6.5 %collective-permute-start.12 = (bf16[256,2048]{1,0:T(8,128)(2,1)S(1)}, bf16[256,2048]{1,0:T(8,128)(2,1)S(1)}, u32[]{:S(2)}, u32[]{:S(2)}) collective-permute-start(bf16[256,2048]{1,0:T(8,128)(2,1)S(1)} %get-tuple-element.110), channel_id=1, source_target_pairs={{0,1},{1,0},{2,3},{3,2},{4,5},{5,4},{6,7},{7,6},{8,9},{9,8},{10,11... | collective-permute-start | bytes 3145736 | tf_op jit(solution)/shard_map/ppermute | solution.py:408
  67.8 5.8 %slice-start.1 = ((s8[5767168]{0:T(1024)(128)(4,1)}), s8[1572864]{0:T(1024)(128)(4,1)S(1)}, s32[]{:S(2)}) async-start(s8[5767168]{0:T(1024)(128)(4,1)} %bitcast.17), calls=%async_computation.2 | async-start | bytes 3145728
  69.7 8.9 %collective-permute-start.13 = (bf16[48,2048]{1,0:T(8,128)(2,1)S(1)}, bf16[48,2048]{1,0:T(8,128)(2,1)S(1)}, u32[]{:S(2)}, u32[]{:S(2)}) collective-permute-start(bf16[48,2048]{1,0:T(8,128)(2,1)S(1)} %get-tuple-element.115), channel_id=1, source_target_pairs={{0,2},{2,4},{4,6},{6,0},{1,3},{3,5},{5,7},{7,1},{8,10},{10,12},{12... | collective-permute-start | bytes 589832 | tf_op jit(solution)/shard_map/ppermute | solution.py:556
  70.6 11.8 %collective-permute-start.14 = (bf16[48,2048]{1,0:T(8,128)(2,1)S(1)}, bf16[48,2048]{1,0:T(8,128)(2,1)S(1)}, u32[]{:S(2)}, u32[]{:S(2)}) collective-permute-start(bf16[48,2048]{1,0:T(8,128)(2,1)S(1)} %get-tuple-element.116), channel_id=1, source_target_pairs={{0,4},{2,6},{4,0},{6,2},{1,5},{3,7},{5,1},{7,3},{8,12},{10,14},{12... | collective-permute-start | bytes 589832 | tf_op jit(solution)/shard_map/ppermute | solution.py:556
  73.6 8.9 %collective-permute-start.15 = (bf16[48,2048]{1,0:T(8,128)(2,1)S(1)}, bf16[48,2048]{1,0:T(8,128)(2,1)S(1)}, u32[]{:S(2)}, u32[]{:S(2)}) collective-permute-start(bf16[48,2048]{1,0:T(8,128)(2,1)S(1)} %get-tuple-element.117), channel_id=1, source_target_pairs={{0,6},{2,0},{4,2},{6,4},{1,7},{3,1},{5,3},{7,5},{8,14},{10,8},{12,... | collective-permute-start | bytes 589832 | tf_op jit(solution)/shard_map/ppermute | solution.py:556
  82.4 20.6 %collective-permute-start.16 = (bf16[128,2048]{1,0:T(8,128)(2,1)S(1)}, bf16[128,2048]{1,0:T(8,128)(2,1)S(1)}, u32[]{:S(2)}, u32[]{:S(2)}) collective-permute-start(bf16[128,2048]{1,0:T(8,128)(2,1)S(1)} %get-tuple-element.139.own_ref), channel_id=1, source_target_pairs={{0,2},{2,0},{4,6},{6,4},{1,3},{3,1},{5,7},{7,5},{8,10},{10,8},{12,... | collective-permute-start | bytes 1572872 | tf_op jit(solution)/shard_map/ppermute | solution.py:413
  88.2 10.8 %collective-permute-start.17 = (bf16[48,2048]{1,0:T(8,128)(2,1)}, bf16[48,2048]{1,0:T(8,128)(2,1)S(1)}, u32[]{:S(2)}, u32[]{:S(2)}) collective-permute-start(bf16[48,2048]{1,0:T(8,128)(2,1)} %get-tuple-element.132), channel_id=1, source_target_pairs={{0,6},{2,0},{4,2},{6,4},{1,7},{3,1},{5,3},{7,5},{8,14},{10,8},{12,... | collective-permute-start | bytes 589832 | tf_op jit(solution)/shard_map/ppermute | solution.py:579
  89.8 12.4 %collective-permute-start.18 = (bf16[48,2048]{1,0:T(8,128)(2,1)}, bf16[48,2048]{1,0:T(8,128)(2,1)S(1)}, u32[]{:S(2)}, u32[]{:S(2)}) collective-permute-start(bf16[48,2048]{1,0:T(8,128)(2,1)} %get-tuple-element.133), channel_id=1, source_target_pairs={{0,4},{2,6},{4,0},{6,2},{1,5},{3,7},{5,1},{7,3},{8,12},{10,14},{12... | collective-permute-start | bytes 589832 | tf_op jit(solution)/shard_map/ppermute | solution.py:579
  91.0 12.1 %collective-permute-start.19 = (bf16[48,2048]{1,0:T(8,128)(2,1)}, bf16[48,2048]{1,0:T(8,128)(2,1)}, u32[]{:S(2)}, u32[]{:S(2)}) collective-permute-start(bf16[48,2048]{1,0:T(8,128)(2,1)} %get-tuple-element.134), channel_id=1, source_target_pairs={{0,2},{2,4},{4,6},{6,0},{1,3},{3,5},{5,7},{7,1},{8,10},{10,12},{12... | collective-permute-start | bytes 589832 | tf_op jit(solution)/shard_map/ppermute | solution.py:579
  91.8 3.7 %copy-start = (bf16[48,48,2048]{2,1,0:T(8,128)(2,1)S(1)}, bf16[48,48,2048]{2,1,0:T(8,128)(2,1)}, u32[]{:S(2)}) copy-start(bf16[48,48,2048]{2,1,0:T(8,128)(2,1)} %all-gather.3.cloned.1.call-done) | copy-start | bytes 28311556
  103.0 2.8 %collective-permute-start.20 = (bf16[128,2048]{1,0:T(8,128)(2,1)S(1)}, bf16[128,2048]{1,0:T(8,128)(2,1)S(1)}, u32[]{:S(2)}, u32[]{:S(2)}) collective-permute-start(bf16[128,2048]{1,0:T(8,128)(2,1)S(1)} %collective-permute-done.16.own_ref), channel_id=1, source_target_pairs={{0,1},{1,0},{2,3},{3,2},{4,5},{5,4},{6,7},{7,6},{8,9},{9,8},{10,11... | collective-permute-start | bytes 1572872 | tf_op jit(solution)/shard_map/ppermute | solution.py:408
  109.3 2.0 %collective-permute-start.21 = (bf16[128,2048]{1,0:T(8,128)(2,1)S(1)}, bf16[128,2048]{1,0:T(8,128)(2,1)S(1)}, u32[]{:S(2)}, u32[]{:S(2)}) collective-permute-start(bf16[128,2048]{1,0:T(8,128)(2,1)S(1)} %get-tuple-element.138), channel_id=1, source_target_pairs={{0,1},{1,0},{2,3},{3,2},{4,5},{5,4},{6,7},{7,6},{8,9},{9,8},{10,11... | collective-permute-start | bytes 1572872 | tf_op jit(solution)/shard_map/ppermute | solution.py:408
  111.4 14.8 %collective-permute-start.22 = (bf16[128,2048]{1,0:T(8,128)(2,1)S(1)}, bf16[128,2048]{1,0:T(8,128)(2,1)S(1)}, u32[]{:S(2)}, u32[]{:S(2)}) collective-permute-start(bf16[128,2048]{1,0:T(8,128)(2,1)S(1)} %add_convert_fusion.1), channel_id=1, source_target_pairs={{0,2},{2,0},{4,6},{6,4},{1,3},{3,1},{5,7},{7,5},{8,10},{10,8},{12,... | collective-permute-start | bytes 1572872 | tf_op jit(solution)/shard_map/ppermute | solution.py:413
  126.2 2.4 %collective-permute-start.23 = (bf16[128,2048]{1,0:T(8,128)(2,1)S(1)}, bf16[128,2048]{1,0:T(8,128)(2,1)S(1)}, u32[]{:S(2)}, u32[]{:S(2)}) collective-permute-start(bf16[128,2048]{1,0:T(8,128)(2,1)S(1)} %get-tuple-element.150), channel_id=1, source_target_pairs={{0,1},{1,0},{2,3},{3,2},{4,5},{5,4},{6,7},{7,6},{8,9},{9,8},{10,11... | collective-permute-start | bytes 1572872 | tf_op jit(solution)/shard_map/ppermute | solution.py:408
Sparse Core Ops, SparseCore 0:
  11.7 79.3 all-gather.2

commit v3 on v2

--- a/solution.py
+++ b/solution.py
@@ -443,6 +443,8 @@
     proj_low = lax.ppermute(out_proj, "x", ring(1))
     proj_high = lax.ppermute(out_proj, "x", ring(3))
 
+    other_ids = swap_core(route_ids)
+
     states, passed, message, slab = call(
         states_kernel,
         [
@@ -451,7 +453,7 @@
             ((MSG, HD), BF),
             ((3, PART, D), BF),
         ],
-        place,
+        after(place, other_ids),
         log_decay,
         key_rows,
         values,
@@ -479,7 +481,6 @@
             name=f"step{bit}",
         )
         if bit == 0:
-            other_ids = swap_core(after(route_ids, message))
             (inner,) = call(
                 inner_kernel,
                 [((CHUNK * CHUNKS, HEADS * HD), F32)],

time: 137 us -> 136 us (level)
  waiting for transfers between devices: 35.8 us -> 38.8 us
  local copies, waits for them, and re-layouts: 13.5 us -> 10.9 us
  starting transfers between devices: 38.7 us -> 37.3 us
    unnamed x50 -> x43, local copies, waits for them, and re-layouts: 12.6 us -> 10.1 us
    all_gather x1, waiting for transfers between devices: 0.01 us -> 1.82 us  [on_device(): shared_weights = lax.all_gather(slab, ('y', 'zh', 'zl'))]
    ppermute x3, waiting for transfers between devices: 6.87 us -> 5.18 us  [on_device(): returned = [lax.ppermute(results[d], 'x', ring(4 - d)) for d in (1, 2, 3)]]
    ppermute x1, waiting for transfers between devices: 0.01 us -> 1.47 us  [on_device(): proj_low = lax.ppermute(out_proj, 'x', ring(1))]
  transfers between devices with their start and end apart: 25 -> 25, of which waited for: 14 -> 19; matrix products, arithmetic and copies ran while one was open for 0% -> 1% of each run, Pallas kernels for 19% -> 19%
where the time goes in v3:
time: 136 us
  waiting for transfers between devices  38.8 us (29%)
  starting transfers between devices  37.3 us (27%)
  Pallas kernels  33.6 us (25%)
  between operations  13.6 us (10%)
  local copies, waits for them, and re-layouts  10.9 us (8%)
    pallas_call x15, Pallas kernels, call(): pl.pallas_call(kernel, in_specs=[SM] * scalars + [VM] * (len(args) - scal...  33.6 us
    ppermute x6, starting transfers between devices, swap(): return lax.ppermute(a, axis, [(i, i ^ bit) for i in range(count)])  13.8 us
    ppermute x6, waiting for transfers between devices, swap(): return lax.ppermute(a, axis, [(i, i ^ bit) for i in range(count)])  11.8 us
    unnamed x43, local copies, waits for them, and re-layouts  10.1 us
    ppermute x5, starting transfers between devices, swap_core(): return lax.ppermute(a, 'core', [(0, 1), (1, 0)])  8.22 us
    ppermute x3, waiting for transfers between devices, on_device(): heads = [lax.ppermute(normed[d], 'x', ring(d)) for d in (1, 2, 3)]  7.48 us
    ppermute x5, waiting for transfers between devices, swap_core(): return lax.ppermute(a, 'core', [(0, 1), (1, 0)])  7.2 us
    ppermute x3, waiting for transfers between devices, on_device(): returned = [lax.ppermute(results[d], 'x', ring(4 - d)) for d in (1, 2, 3)]  5.18 us
  transfers between devices with their start and end apart: 25, of which 19 were waited for; matrix products, arithmetic and copies ran while one was open for 1% of the time, Pallas kernels for 19%

profile of v3, /device:TPU:1, one launch (start us, length us, event | category | flops | bytes accessed | tf_op | source)
XLA Modules:
  0.0 135.5 jit_solution(1263489435320320411)
XLA Ops:
  6.5 0.8 copy.19
  7.3 1.5 %collective-permute-start = (s32[128,6]{1,0:T(8,128)S(1)}, s32[128,6]{1,0:T(8,128)S(1)}, u32[]{:S(2)}, u32[]{:S(2)}) collective-permute-start(s32[128,6]{1,0:T(8,128)S(1)} %copy.19), channel_id=1, source_target_pairs={{0,1},{1,0},{2,3},{3,2},{4,5},{5,4},{6,7},{7,6},{8,9},{9,8},{10,11... | collective-permute-start | bytes 9224 | tf_op jit(solution)/shard_map/ppermute | solution.py:408
  8.8 0.6 stack.31.place_ref
  9.7 4.3 %states.1 = (f32[4,2,128,128]{3,2,1,0:T(8,128)}, f32[4,2,128]{2,1,0:T(2,128)}, bf16[272,128]{1,0:T(8,128)(2,1)}, bf16[3,48,2048]{2,1,0:T(8,128)(2,1)}) custom-call(s32[7]{0:T(128)} %stack.31.place_ref, f32[2,1024]{1,0:T(2,128)} %decay_ref.5, bf16[1024,256]{1,0:T(8,128)(2,1)} %key_ref.3, bf16[1024,256]{1,0:T(8,128)(2,1)} %value_ref.3, ...), custom_call_target="tpu_custom_call" | custom-call | flops 1000000000 | bytes 4407324 | tf_op jit(solution)/shard_map/states/pallas_call | solution.py:383
  14.1 1.4 %collective-permute-start.5 = (bf16[256,2048]{1,0:T(8,128)(2,1)}, bf16[256,2048]{1,0:T(8,128)(2,1)S(1)}, u32[]{:S(2)}, u32[]{:S(2)}) collective-permute-start(bf16[256,2048]{1,0:T(8,128)(2,1)} %w0_ref.1), channel_id=1, source_target_pairs={{0,2},{2,4},{4,6},{6,0},{1,3},{3,5},{5,7},{7,1},{8,10},{10,12},{12... | collective-permute-start | bytes 3145736 | tf_op jit(solution)/shard_map/ppermute | solution.py:443
  15.4 1.4 %collective-permute-start.6 = (bf16[256,2048]{1,0:T(8,128)(2,1)}, bf16[256,2048]{1,0:T(8,128)(2,1)S(1)}, u32[]{:S(2)}, u32[]{:S(2)}) collective-permute-start(bf16[256,2048]{1,0:T(8,128)(2,1)} %w0_ref.1), channel_id=1, source_target_pairs={{0,6},{2,0},{4,2},{6,4},{1,7},{3,1},{5,3},{7,5},{8,14},{10,8},{12,... | collective-permute-start | bytes 3145736 | tf_op jit(solution)/shard_map/ppermute | solution.py:444
  16.8 1.7 %collective-permute-start.1 = (bf16[272,128]{1,0:T(8,128)(2,1)}, bf16[272,128]{1,0:T(8,128)(2,1)S(1)}, u32[]{:S(2)}, u32[]{:S(2)}) collective-permute-start(bf16[272,128]{1,0:T(8,128)(2,1)} %get-tuple-element.79.own_ref), channel_id=1, source_target_pairs={{0,8},{8,0},{1,9},{9,1},{2,10},{10,2},{3,11},{11,3},{4,12},{12,4},... | collective-permute-start | bytes 208904 | tf_op jit(solution)/shard_map/ppermute | solution.py:413
  18.5 2.2 %collective-permute-done.1.other_ref = bf16[272,128]{1,0:T(8,128)(2,1)S(1)} collective-permute-done((bf16[272,128]{1,0:T(8,128)(2,1)}, bf16[272,128]{1,0:T(8,128)(2,1)S(1)}, u32[]{:S(2)}, u32[]{:S(2)}) %collective-permute-start.1) | collective-permute-done | bytes 69664 | tf_op jit(solution)/shard_map/ppermute | solution.py:413
  20.8 0.6 copy-done.1
  21.4 0.9 copy-done.10
  22.2 0.6 step0.1
  22.8 3.5 %collective-permute-start.2 = (bf16[272,128]{1,0:T(8,128)(2,1)S(1)}, bf16[272,128]{1,0:T(8,128)(2,1)S(1)}, u32[]{:S(2)}, u32[]{:S(2)}) collective-permute-start(bf16[272,128]{1,0:T(8,128)(2,1)S(1)} %get-tuple-element.80.own_ref), channel_id=1, source_target_pairs={{0,16},{16,0},{1,17},{17,1},{2,18},{18,2},{3,19},{19,3},{4,20},{20... | collective-permute-start | bytes 208904 | tf_op jit(solution)/shard_map/ppermute | solution.py:413
  26.3 1.7 %collective-permute-done.2.other_ref = bf16[272,128]{1,0:T(8,128)(2,1)S(1)} collective-permute-done((bf16[272,128]{1,0:T(8,128)(2,1)S(1)}, bf16[272,128]{1,0:T(8,128)(2,1)S(1)}, u32[]{:S(2)}, u32[]{:S(2)}) %collective-permute-start.2) | collective-permute-done | bytes 69664 | tf_op jit(solution)/shard_map/ppermute | solution.py:413
  28.0 0.6 step1.1
  28.6 1.4 %collective-permute-start.3 = (bf16[272,128]{1,0:T(8,128)(2,1)S(1)}, bf16[272,128]{1,0:T(8,128)(2,1)S(1)}, u32[]{:S(2)}, u32[]{:S(2)}) collective-permute-start(bf16[272,128]{1,0:T(8,128)(2,1)S(1)} %get-tuple-element.86.own_ref), channel_id=1, source_target_pairs={{0,32},{32,0},{64,96},{96,64},{1,33},{33,1},{65,97},{97,65},{2,34}... | collective-permute-start | bytes 208904 | tf_op jit(solution)/shard_map/ppermute | solution.py:413
  30.0 1.0 copy-done.6
  31.1 1.0 inner.1.inner_ref
  32.1 1.0 copy-done.15
  33.2 0.5 collective-permute-done.3.other_ref
  33.7 0.6 step2.1
  34.3 3.0 %collective-permute-start.4 = (bf16[272,128]{1,0:T(8,128)(2,1)S(1)}, bf16[272,128]{1,0:T(8,128)(2,1)S(1)}, u32[]{:S(2)}, u32[]{:S(2)}) collective-permute-start(bf16[272,128]{1,0:T(8,128)(2,1)S(1)} %get-tuple-element.91), channel_id=1, source_target_pairs={{0,64},{32,96},{64,0},{96,32},{1,65},{33,97},{65,1},{97,33},{2,66}... | collective-permute-start | bytes 208904 | tf_op jit(solution)/shard_map/ppermute | solution.py:413
  37.3 1.3 route.1
  38.6 1.5 %collective-permute-done.5.w1_ref = bf16[256,2048]{1,0:T(8,128)(2,1)S(1)} collective-permute-done((bf16[256,2048]{1,0:T(8,128)(2,1)}, bf16[256,2048]{1,0:T(8,128)(2,1)S(1)}, u32[]{:S(2)}, u32[]{:S(2)}) %collective-permute-start.5) | collective-permute-done | bytes 1048608 | tf_op jit(solution)/shard_map/ppermute | solution.py:443
  40.2 0.6 collective-permute-done.4.other_ref
  41.2 2.2 %collective-permute-start.11 = (bf16[128,2048]{1,0:T(8,128)(2,1)S(1)}, bf16[128,2048]{1,0:T(8,128)(2,1)S(1)}, u32[]{:S(2)}, u32[]{:S(2)}) collective-permute-start(bf16[128,2048]{1,0:T(8,128)(2,1)S(1)} %slice.7), channel_id=1, source_target_pairs={{0,6},{2,0},{4,2},{6,4},{1,7},{3,1},{5,3},{7,5},{8,14},{10,8},{12,... | collective-permute-start | bytes 1572872 | tf_op jit(solution)/shard_map/ppermute | solution.py:520
  43.4 1.0 copy-done.7
  44.5 1.0 copy-done.14
  45.5 2.4 %mix.1 = (bf16[256,256]{1,0:T(8,128)(2,1)S(1)}, bf16[256,256]{1,0:T(8,128)(2,1)S(1)}, bf16[256,256]{1,0:T(8,128)(2,1)S(1)}, bf16[256,256]{1,0:T(8,128)(2,1)S(1)}) custom-call(s32[7]{0:T(128)S(1)} %copy-done.2, bf16[1024,256]{1,0:T(8,128)(2,1)S(1)} %copy-done.7, f32[2,1024]{1,0:T(2,128)S(1)} %copy-done.11, f32[1024,256]{1,0:T(8,128)S(1)} %copy-done.16, ...), custom_call_target="tpu_custom_call" | custom-call | flops 1000000000 | bytes 2836508 | tf_op jit(solution)/shard_map/mix/pallas_call | solution.py:383
  48.0 1.8 %collective-permute-start.8 = (bf16[256,256]{1,0:T(8,128)(2,1)S(1)}, bf16[256,256]{1,0:T(8,128)(2,1)S(1)}, u32[]{:S(2)}, u32[]{:S(2)}) collective-permute-start(bf16[256,256]{1,0:T(8,128)(2,1)S(1)} %get-tuple-element.100), channel_id=1, source_target_pairs={{0,4},{2,6},{4,0},{6,2},{1,5},{3,7},{5,1},{7,3},{8,12},{10,14},{12... | collective-permute-start | bytes 393224 | tf_op jit(solution)/shard_map/ppermute | solution.py:521
  49.8 0.9 collective-permute-start.9
  50.7 4.2 %collective-permute-done.7.one_ref = bf16[256,256]{1,0:T(8,128)(2,1)S(1)} collective-permute-done((bf16[256,256]{1,0:T(8,128)(2,1)S(1)}, bf16[256,256]{1,0:T(8,128)(2,1)S(1)}, u32[]{:S(2)}, u32[]{:S(2)}) %collective-permute-start.7) | collective-permute-done | bytes 131104 | tf_op jit(solution)/shard_map/ppermute | solution.py:521
  54.9 2.4 %collective-permute-done.8.two_ref = bf16[256,256]{1,0:T(8,128)(2,1)S(1)} collective-permute-done((bf16[256,256]{1,0:T(8,128)(2,1)S(1)}, bf16[256,256]{1,0:T(8,128)(2,1)S(1)}, u32[]{:S(2)}, u32[]{:S(2)}) %collective-permute-start.8) | collective-permute-done | bytes 131104 | tf_op jit(solution)/shard_map/ppermute | solution.py:521
  57.3 0.8 collective-permute-done.9.three_ref
  58.2 2.1 %project.1 = (f32[256,2048]{1,0:T(8,128)S(1)}, bf16[256,2048]{1,0:T(8,128)(2,1)S(1)}) custom-call(s32[7]{0:T(128)S(1)} %copy-done.2, bf16[256,256]{1,0:T(8,128)(2,1)S(1)} %get-tuple-element.98.own_ref, bf16[256,256]{1,0:T(8,128)(2,1)S(1)} %collective-permute-done.7.one_ref, bf16[256,256]{1,0:T(8,128)(2,1)S(1)} %collective-permute-done.8.two_ref, ...), custom_call_target="tpu_custom_call" | custom-call | flops 6000000000 | bytes 8388636 | tf_op jit(solution)/shard_map/project/pallas_call | solution.py:383
  60.3 4.2 %collective-permute-start.12 = (bf16[256,2048]{1,0:T(8,128)(2,1)S(1)}, bf16[256,2048]{1,0:T(8,128)(2,1)S(1)}, u32[]{:S(2)}, u32[]{:S(2)}) collective-permute-start(bf16[256,2048]{1,0:T(8,128)(2,1)S(1)} %get-tuple-element.110), channel_id=1, source_target_pairs={{0,1},{1,0},{2,3},{3,2},{4,5},{5,4},{6,7},{7,6},{8,9},{9,8},{10,11... | collective-permute-start | bytes 3145736 | tf_op jit(solution)/shard_map/ppermute | solution.py:408
  64.5 2.3 %collective-permute-done.12.other_ref = bf16[256,2048]{1,0:T(8,128)(2,1)S(1)} collective-permute-done((bf16[256,2048]{1,0:T(8,128)(2,1)S(1)}, bf16[256,2048]{1,0:T(8,128)(2,1)S(1)}, u32[]{:S(2)}, u32[]{:S(2)}) %collective-permute-start.12) | collective-permute-done | bytes 1048608 | tf_op jit(solution)/shard_map/ppermute | solution.py:408
  66.8 1.9 %norm.1 = (f32[128,2048]{1,0:T(8,128)S(1)}, bf16[128,2048]{1,0:T(8,128)(2,1)S(1)}, bf16[128,2048]{1,0:T(8,128)(2,1)S(1)}, bf16[48,2048]{1,0:T(8,128)(2,1)S(1)}, ...) custom-call(s32[7]{0:T(128)S(1)} %copy-done.2, ...), custom_call_target="tpu_custom_call" | custom-call | flops 30000001024 | bytes 6660124 | tf_op jit(solution)/shard_map/norm/pallas_call | solution.py:383
  68.7 0.5 collective-permute-start.13
  69.2 3.1 %collective-permute-start.14 = (bf16[48,2048]{1,0:T(8,128)(2,1)S(1)}, bf16[48,2048]{1,0:T(8,128)(2,1)S(1)}, u32[]{:S(2)}, u32[]{:S(2)}) collective-permute-start(bf16[48,2048]{1,0:T(8,128)(2,1)S(1)} %get-tuple-element.116), channel_id=1, source_target_pairs={{0,4},{2,6},{4,0},{6,2},{1,5},{3,7},{5,1},{7,3},{8,12},{10,14},{12... | collective-permute-start | bytes 589832 | tf_op jit(solution)/shard_map/ppermute | solution.py:557
  72.3 4.9 %load.2 = (bf16[2048,1408]{1,0:T(8,128)(2,1)S(1)}, bf16[2048,1408]{1,0:T(8,128)(2,1)S(1)}, bf16[1408,2048]{1,0:T(8,128)(2,1)S(1)}) custom-call(bf16[2048,1408]{1,0:T(8,128)(2,1)S(1)} %bitcast.19, bf16[2048,1408]{1,0:T(8,128)(2,1)} %bitcast.23, bf16[1408,2048]{1,0:T(8,128)(2,1)} %bitcast.24), custom_call_target="tpu_custom_call" | custom-call | flops 1000000000 | bytes 34603008 | tf_op jit(solution)/shard_map/load/pallas_call | solution.py:383
  77.3 3.9 %collective-permute-done.14.two_ref = bf16[48,2048]{1,0:T(8,128)(2,1)S(1)} collective-permute-done((bf16[48,2048]{1,0:T(8,128)(2,1)S(1)}, bf16[48,2048]{1,0:T(8,128)(2,1)S(1)}, u32[]{:S(2)}, u32[]{:S(2)}) %collective-permute-start.14) | collective-permute-done | bytes 196640 | tf_op jit(solution)/shard_map/ppermute | solution.py:557
  81.1 1.4 %collective-permute-start.16 = (bf16[128,2048]{1,0:T(8,128)(2,1)S(1)}, bf16[128,2048]{1,0:T(8,128)(2,1)S(1)}, u32[]{:S(2)}, u32[]{:S(2)}) collective-permute-start(bf16[128,2048]{1,0:T(8,128)(2,1)S(1)} %get-tuple-element.139.own_ref), channel_id=1, source_target_pairs={{0,2},{2,0},{4,6},{6,4},{1,3},{3,1},{5,7},{7,5},{8,10},{10,8},{12,... | collective-permute-start | bytes 1572872 | tf_op jit(solution)/shard_map/ppermute | solution.py:413
  82.6 4.6 %expert.1 = (bf16[48,2048]{1,0:T(8,128)(2,1)S(1)}, bf16[48,2048]{1,0:T(8,128)(2,1)}, bf16[48,2048]{1,0:T(8,128)(2,1)}, bf16[48,2048]{1,0:T(8,128)(2,1)}) custom-call(bf16[48,2048]{1,0:T(8,128)(2,1)S(1)} %get-tuple-element.127.own_ref, bf16[48,2048]{1,0:T(8,128)(2,1)S(1)} %collective-permute-done.13.one_ref, ...), custom_call_target="tpu_custom_call" | custom-call | flops 1000000000 | bytes 18874368 | tf_op jit(solution)/shard_map/expert/pallas_call | solution.py:383
  87.2 1.5 %collective-permute-start.17 = (bf16[48,2048]{1,0:T(8,128)(2,1)}, bf16[48,2048]{1,0:T(8,128)(2,1)S(1)}, u32[]{:S(2)}, u32[]{:S(2)}) collective-permute-start(bf16[48,2048]{1,0:T(8,128)(2,1)} %get-tuple-element.132), channel_id=1, source_target_pairs={{0,6},{2,0},{4,2},{6,4},{1,7},{3,1},{5,3},{7,5},{8,14},{10,8},{12,... | collective-permute-start | bytes 589832 | tf_op jit(solution)/shard_map/ppermute | solution.py:580
  88.7 1.2 collective-permute-start.18
  89.9 0.9 collective-permute-start.19
  90.7 1.8 %all-gather.3.cloned.1.call-done = bf16[48,48,2048]{2,1,0:T(8,128)(2,1)} async-done(((bf16[3,48,2048]{2,1,0:T(8,128)(2,1)}), bf16[48,48,2048]{2,1,0:T(8,128)(2,1)}) %all-gather.3.cloned.1.call-update) | async-done | bytes 9437200 | tf_op jit(solution)/shard_map/all_gather | solution.py:469
  92.6 3.7 %copy-done = bf16[48,48,2048]{2,1,0:T(8,128)(2,1)S(1)} copy-done((bf16[48,48,2048]{2,1,0:T(8,128)(2,1)S(1)}, bf16[48,48,2048]{2,1,0:T(8,128)(2,1)}, u32[]{:S(2)}) %copy-start) | copy-done | bytes 9437208
  96.2 0.6 load.3.weights_ref
  96.9 0.8 collective-permute-done.17.two_ref
  97.7 3.5 %collective-permute-done.18.three_ref = bf16[48,2048]{1,0:T(8,128)(2,1)S(1)} collective-permute-done((bf16[48,2048]{1,0:T(8,128)(2,1)}, bf16[48,2048]{1,0:T(8,128)(2,1)S(1)}, u32[]{:S(2)}, u32[]{:S(2)}) %collective-permute-start.18) | collective-permute-done | bytes 196640 | tf_op jit(solution)/shard_map/ppermute | solution.py:580
  101.2 0.9 collective-permute-done.19.four_ref
  102.1 1.2 collective-permute-start.20
  103.3 1.5 %collective-permute-done.20.other_ref = bf16[128,2048]{1,0:T(8,128)(2,1)S(1)} collective-permute-done((bf16[128,2048]{1,0:T(8,128)(2,1)S(1)}, bf16[128,2048]{1,0:T(8,128)(2,1)S(1)}, u32[]{:S(2)}, u32[]{:S(2)}) %collective-permute-start.20) | collective-permute-done | bytes 524320 | tf_op jit(solution)/shard_map/ppermute | solution.py:408
  104.8 3.5 %shared.2 = (f32[128,2048]{1,0:T(8,128)S(1)}, bf16[128,2048]{1,0:T(8,128)(2,1)S(1)}) custom-call(s32[7]{0:T(128)S(1)} %copy-done.2, bf16[128,2048]{1,0:T(8,128)(2,1)S(1)} %collective-permute-done.16.own_ref, bf16[128,2048]{1,0:T(8,128)(2,1)S(1)} %collective-permute-done.20.other_ref, bf16[16,3,48,2048]{3,2,1,0:T(8,128)(2,1)S(1)} %load.3.weights_ref), custom_call_target="tpu_custom_call" | custom-call | tf_op jit(solution)/shard_map/shared/pallas_call | solution.py:383
  108.3 0.5 collective-permute-start.21
  108.8 1.5 %collective-permute-done.21 = bf16[128,2048]{1,0:T(8,128)(2,1)S(1)} collective-permute-done((bf16[128,2048]{1,0:T(8,128)(2,1)S(1)}, bf16[128,2048]{1,0:T(8,128)(2,1)S(1)}, u32[]{:S(2)}, u32[]{:S(2)}) %collective-permute-start.21) | collective-permute-done | bytes 524320 | tf_op jit(solution)/shard_map/ppermute | solution.py:408
  110.4 2.7 %collective-permute-start.22 = (bf16[128,2048]{1,0:T(8,128)(2,1)S(1)}, bf16[128,2048]{1,0:T(8,128)(2,1)S(1)}, u32[]{:S(2)}, u32[]{:S(2)}) collective-permute-start(bf16[128,2048]{1,0:T(8,128)(2,1)S(1)} %add_convert_fusion.1), channel_id=1, source_target_pairs={{0,2},{2,0},{4,6},{6,4},{1,3},{3,1},{5,7},{7,5},{8,10},{10,8},{12,... | collective-permute-start | bytes 1572872 | tf_op jit(solution)/shard_map/ppermute | solution.py:413
  113.2 3.5 %shared.3 = (f32[128,2048]{1,0:T(8,128)S(1)}, bf16[128,2048]{1,0:T(8,128)(2,1)S(1)}) custom-call(s32[7]{0:T(128)S(1)} %copy-done.2, bf16[128,2048]{1,0:T(8,128)(2,1)S(1)} %get-tuple-element.139.own_ref, bf16[128,2048]{1,0:T(8,128)(2,1)S(1)} %get-tuple-element.140.other_ref, bf16[16,3,48,2048]{3,2,1,0:T(8,128)(2,1)S(1)} %load.3.weights_ref), custom_call_target="tpu_custom_call" | custom-call | tf_op jit(solution)/shard_map/shared/pallas_call | solution.py:383
  116.6 1.7 %combine.1 = (f32[128,2048]{1,0:T(8,128)S(1)}, bf16[128,2048]{1,0:T(8,128)(2,1)S(1)}) custom-call(f32[128,2048]{1,0:T(8,128)S(1)} %get-tuple-element.141.mine_ref, bf16[128,2048]{1,0:T(8,128)(2,1)S(1)} %get-tuple-element.142.theirs_ref, bf16[256,384]{1,0:T(8,128)(2,1)S(1)} %get-tuple-element.143.back_ref, bf16[48,2048]{1,0:T(8,128)(2,1)S(1)} %get-tuple-element.131.one_ref, ...), custom_call_target="tpu_custom_call" | custom-call | tf_op jit(solution)/shard_map/combine/pallas_call | solution.py:383
  118.3 6.8 %collective-permute-done.22 = bf16[128,2048]{1,0:T(8,128)(2,1)S(1)} collective-permute-done((bf16[128,2048]{1,0:T(8,128)(2,1)S(1)}, bf16[128,2048]{1,0:T(8,128)(2,1)S(1)}, u32[]{:S(2)}, u32[]{:S(2)}) %collective-permute-start.22) | collective-permute-done | bytes 524320 | tf_op jit(solution)/shard_map/ppermute | solution.py:413
  125.2 0.9 collective-permute-start.23
  126.0 1.5 %collective-permute-done.23 = bf16[128,2048]{1,0:T(8,128)(2,1)S(1)} collective-permute-done((bf16[128,2048]{1,0:T(8,128)(2,1)S(1)}, bf16[128,2048]{1,0:T(8,128)(2,1)S(1)}, u32[]{:S(2)}, u32[]{:S(2)}) %collective-permute-start.23) | collective-permute-done | bytes 524320 | tf_op jit(solution)/shard_map/ppermute | solution.py:408
  127.6 1.1 add_convert_fusion
  (52 shorter events, 1.3 us)
Async XLA Ops:
  6.5 86.0 %all-gather.3.cloned.1.call-start = ((), (), s32[]{:S(2)}) async-start(), calls=%async_computation | async-start | bytes 10027008 | tf_op jit(solution)/shard_map/all_gather | solution.py:469
  7.3 2.4 %collective-permute-start = (s32[128,6]{1,0:T(8,128)S(1)}, s32[128,6]{1,0:T(8,128)S(1)}, u32[]{:S(2)}, u32[]{:S(2)}) collective-permute-start(s32[128,6]{1,0:T(8,128)S(1)} %copy.19), channel_id=1, source_target_pairs={{0,1},{1,0},{2,3},{3,2},{4,5},{5,4},{6,7},{7,6},{8,9},{9,8},{10,11... | collective-permute-start | bytes 9224 | tf_op jit(solution)/shard_map/ppermute | solution.py:408
  9.7 20.3 %copy-start.4 = (bf16[1024,256]{1,0:T(8,128)(2,1)S(1)}, bf16[1024,256]{1,0:T(8,128)(2,1)}, u32[]{:S(2)}) copy-start(bf16[1024,256]{1,0:T(8,128)(2,1)} %key_ref.3) | copy-start | bytes 1572868
  9.7 20.3 %copy-start.5 = (bf16[1024,256]{1,0:T(8,128)(2,1)S(1)}, bf16[1024,256]{1,0:T(8,128)(2,1)}, u32[]{:S(2)}) copy-start(bf16[1024,256]{1,0:T(8,128)(2,1)} %value_ref.3) | copy-start | bytes 1572868
  9.7 20.3 %copy-start.11 = (f32[2,1024]{1,0:T(2,128)S(1)}, f32[2,1024]{1,0:T(2,128)}, u32[]{:S(2)}) copy-start(f32[2,1024]{1,0:T(2,128)} %decay_ref.5) | copy-start | bytes 24580
  14.0 19.0 %copy-start.18 = (s32[128,6]{0,1:T(8,128)S(1)}, s32[128,6]{0,1:T(8,128)}, u32[]{:S(2)}) copy-start(s32[128,6]{0,1:T(8,128)} %param.25) | copy-start | bytes 9220
  14.0 19.6 %copy-start.2 = (s32[7]{0:T(128)S(1)}, s32[7]{0:T(128)}, u32[]{:S(2)}) copy-start(s32[7]{0:T(128)} %stack.31.place_ref) | copy-start | bytes 88
  14.1 26.0 %collective-permute-start.5 = (bf16[256,2048]{1,0:T(8,128)(2,1)}, bf16[256,2048]{1,0:T(8,128)(2,1)S(1)}, u32[]{:S(2)}, u32[]{:S(2)}) collective-permute-start(bf16[256,2048]{1,0:T(8,128)(2,1)} %w0_ref.1), channel_id=1, source_target_pairs={{0,2},{2,4},{4,6},{6,0},{1,3},{3,5},{5,7},{7,1},{8,10},{10,12},{12... | collective-permute-start | bytes 3145736 | tf_op jit(solution)/shard_map/ppermute | solution.py:443
  15.4 24.7 %collective-permute-start.6 = (bf16[256,2048]{1,0:T(8,128)(2,1)}, bf16[256,2048]{1,0:T(8,128)(2,1)S(1)}, u32[]{:S(2)}, u32[]{:S(2)}) collective-permute-start(bf16[256,2048]{1,0:T(8,128)(2,1)} %w0_ref.1), channel_id=1, source_target_pairs={{0,6},{2,0},{4,2},{6,4},{1,7},{3,1},{5,3},{7,5},{8,14},{10,8},{12,... | collective-permute-start | bytes 3145736 | tf_op jit(solution)/shard_map/ppermute | solution.py:444
  16.8 3.9 %collective-permute-start.1 = (bf16[272,128]{1,0:T(8,128)(2,1)}, bf16[272,128]{1,0:T(8,128)(2,1)S(1)}, u32[]{:S(2)}, u32[]{:S(2)}) collective-permute-start(bf16[272,128]{1,0:T(8,128)(2,1)} %get-tuple-element.79.own_ref), channel_id=1, source_target_pairs={{0,8},{8,0},{1,9},{9,1},{2,10},{10,2},{3,11},{11,3},{4,12},{12,4},... | collective-permute-start | bytes 208904 | tf_op jit(solution)/shard_map/ppermute | solution.py:413
  20.8 0.6 copy-start.1
  21.4 0.9 copy-start.10
  22.8 5.2 %collective-permute-start.2 = (bf16[272,128]{1,0:T(8,128)(2,1)S(1)}, bf16[272,128]{1,0:T(8,128)(2,1)S(1)}, u32[]{:S(2)}, u32[]{:S(2)}) collective-permute-start(bf16[272,128]{1,0:T(8,128)(2,1)S(1)} %get-tuple-element.80.own_ref), channel_id=1, source_target_pairs={{0,16},{16,0},{1,17},{17,1},{2,18},{18,2},{3,19},{19,3},{4,20},{20... | collective-permute-start | bytes 208904 | tf_op jit(solution)/shard_map/ppermute | solution.py:413
  28.6 5.1 %collective-permute-start.3 = (bf16[272,128]{1,0:T(8,128)(2,1)S(1)}, bf16[272,128]{1,0:T(8,128)(2,1)S(1)}, u32[]{:S(2)}, u32[]{:S(2)}) collective-permute-start(bf16[272,128]{1,0:T(8,128)(2,1)S(1)} %get-tuple-element.86.own_ref), channel_id=1, source_target_pairs={{0,32},{32,0},{64,96},{96,64},{1,33},{33,1},{65,97},{97,65},{2,34}... | collective-permute-start | bytes 208904 | tf_op jit(solution)/shard_map/ppermute | solution.py:413
  30.0 1.0 copy-start.6
  31.1 12.4 %copy-start.13 = (f32[256]{0:T(256)S(1)}, f32[256]{0:T(256)}, u32[]{:S(2)}) copy-start(f32[256]{0:T(256)} %param.21) | copy-start | bytes 3076
  31.1 12.4 %copy-start.17 = (f32[4,2,128]{2,1,0:T(2,128)S(1)}, f32[4,2,128]{2,1,0:T(2,128)}, u32[]{:S(2)}) copy-start(f32[4,2,128]{2,1,0:T(2,128)} %get-tuple-element.83.passed_ref) | copy-start | bytes 12292
  32.1 1.0 copy-start.15
  33.2 10.2 %copy-start.16 = (f32[1024,256]{1,0:T(8,128)S(1)}, f32[1024,256]{1,0:T(8,128)}, u32[]{:S(2)}) copy-start(f32[1024,256]{1,0:T(8,128)} %copy-done.15) | copy-start | bytes 3145732
  33.7 24.5 %copy-start.3 = (bf16[256,2048]{1,0:T(8,128)(2,1)S(1)}, bf16[256,2048]{1,0:T(8,128)(2,1)}, u32[]{:S(2)}) copy-start(bf16[256,2048]{1,0:T(8,128)(2,1)} %w0_ref.1) | copy-start | bytes 3145732
  33.7 24.5 %copy-start.8 = (bf16[128,2048]{1,0:T(8,128)(2,1)S(1)}, bf16[128,2048]{1,0:T(8,128)(2,1)}, u32[]{:S(2)}) copy-start(bf16[128,2048]{1,0:T(8,128)(2,1)} %residual_ref.1) | copy-start | bytes 1572868
  34.3 6.4 %collective-permute-start.4 = (bf16[272,128]{1,0:T(8,128)(2,1)S(1)}, bf16[272,128]{1,0:T(8,128)(2,1)S(1)}, u32[]{:S(2)}, u32[]{:S(2)}) collective-permute-start(bf16[272,128]{1,0:T(8,128)(2,1)S(1)} %get-tuple-element.91), channel_id=1, source_target_pairs={{0,64},{32,96},{64,0},{96,32},{1,65},{33,97},{65,1},{97,33},{2,66}... | collective-permute-start | bytes 208904 | tf_op jit(solution)/shard_map/ppermute | solution.py:413
  40.7 17.4 %collective-permute-start.10 = (bf16[128,2048]{1,0:T(8,128)(2,1)S(1)}, bf16[128,2048]{1,0:T(8,128)(2,1)S(1)}, u32[]{:S(2)}, u32[]{:S(2)}) collective-permute-start(bf16[128,2048]{1,0:T(8,128)(2,1)S(1)} %slice.6), channel_id=1, source_target_pairs={{0,2},{2,4},{4,6},{6,0},{1,3},{3,5},{5,7},{7,1},{8,10},{10,12},{12... | collective-permute-start | bytes 1572872 | tf_op jit(solution)/shard_map/ppermute | solution.py:519
  41.2 17.0 %collective-permute-start.11 = (bf16[128,2048]{1,0:T(8,128)(2,1)S(1)}, bf16[128,2048]{1,0:T(8,128)(2,1)S(1)}, u32[]{:S(2)}, u32[]{:S(2)}) collective-permute-start(bf16[128,2048]{1,0:T(8,128)(2,1)S(1)} %slice.7), channel_id=1, source_target_pairs={{0,6},{2,0},{4,2},{6,4},{1,7},{3,1},{5,3},{7,5},{8,14},{10,8},{12,... | collective-permute-start | bytes 1572872 | tf_op jit(solution)/shard_map/ppermute | solution.py:520
  43.4 1.0 copy-start.7
  44.5 1.0 copy-start.14
  47.9 7.0 %collective-permute-start.7 = (bf16[256,256]{1,0:T(8,128)(2,1)S(1)}, bf16[256,256]{1,0:T(8,128)(2,1)S(1)}, u32[]{:S(2)}, u32[]{:S(2)}) collective-permute-start(bf16[256,256]{1,0:T(8,128)(2,1)S(1)} %get-tuple-element.99), channel_id=1, source_target_pairs={{0,2},{2,4},{4,6},{6,0},{1,3},{3,5},{5,7},{7,1},{8,10},{10,12},{12... | collective-permute-start | bytes 393224 | tf_op jit(solution)/shard_map/ppermute | solution.py:521
  48.0 9.3 %collective-permute-start.8 = (bf16[256,256]{1,0:T(8,128)(2,1)S(1)}, bf16[256,256]{1,0:T(8,128)(2,1)S(1)}, u32[]{:S(2)}, u32[]{:S(2)}) collective-permute-start(bf16[256,256]{1,0:T(8,128)(2,1)S(1)} %get-tuple-element.100), channel_id=1, source_target_pairs={{0,4},{2,6},{4,0},{6,2},{1,5},{3,7},{5,1},{7,3},{8,12},{10,14},{12... | collective-permute-start | bytes 393224 | tf_op jit(solution)/shard_map/ppermute | solution.py:521
  49.8 8.4 %collective-permute-start.9 = (bf16[256,256]{1,0:T(8,128)(2,1)S(1)}, bf16[256,256]{1,0:T(8,128)(2,1)S(1)}, u32[]{:S(2)}, u32[]{:S(2)}) collective-permute-start(bf16[256,256]{1,0:T(8,128)(2,1)S(1)} %get-tuple-element.101), channel_id=1, source_target_pairs={{0,6},{2,0},{4,2},{6,4},{1,7},{3,1},{5,3},{7,5},{8,14},{10,8},{12,... | collective-permute-start | bytes 393224 | tf_op jit(solution)/shard_map/ppermute | solution.py:521
  58.2 8.6 %copy-start.9 = (bf16[2048,64]{0,1:T(8,128)(2,1)S(1)}, bf16[2048,64]{0,1:T(8,128)(2,1)}, u32[]{:S(2)}) copy-start(bf16[2048,64]{0,1:T(8,128)(2,1)} %param.24) | copy-start | bytes 786436
  58.2 8.6 %copy-start.12 = (f32[2048]{0:T(1024)S(1)}, f32[2048]{0:T(1024)}, u32[]{:S(2)}) copy-start(f32[2048]{0:T(1024)} %param.23) | copy-start | bytes 24580
  58.2 14.1 %slice-start = ((s8[5767168]{0:T(1024)(128)(4,1)}), s8[4194304]{0:T(1024)(128)(4,1)S(1)}, s32[]{:S(2)}) async-start(s8[5767168]{0:T(1024)(128)(4,1)} %bitcast.17), calls=%async_computation.1 | async-start | bytes 8388608
  60.3 6.5 %collective-permute-start.12 = (bf16[256,2048]{1,0:T(8,128)(2,1)S(1)}, bf16[256,2048]{1,0:T(8,128)(2,1)S(1)}, u32[]{:S(2)}, u32[]{:S(2)}) collective-permute-start(bf16[256,2048]{1,0:T(8,128)(2,1)S(1)} %get-tuple-element.110), channel_id=1, source_target_pairs={{0,1},{1,0},{2,3},{3,2},{4,5},{5,4},{6,7},{7,6},{8,9},{9,8},{10,11... | collective-permute-start | bytes 3145736 | tf_op jit(solution)/shard_map/ppermute | solution.py:408
  66.8 5.6 %slice-start.1 = ((s8[5767168]{0:T(1024)(128)(4,1)}), s8[1572864]{0:T(1024)(128)(4,1)S(1)}, s32[]{:S(2)}) async-start(s8[5767168]{0:T(1024)(128)(4,1)} %bitcast.17), calls=%async_computation.2 | async-start | bytes 3145728
  68.7 8.6 %collective-permute-start.13 = (bf16[48,2048]{1,0:T(8,128)(2,1)S(1)}, bf16[48,2048]{1,0:T(8,128)(2,1)S(1)}, u32[]{:S(2)}, u32[]{:S(2)}) collective-permute-start(bf16[48,2048]{1,0:T(8,128)(2,1)S(1)} %get-tuple-element.115), channel_id=1, source_target_pairs={{0,2},{2,4},{4,6},{6,0},{1,3},{3,5},{5,7},{7,1},{8,10},{10,12},{12... | collective-permute-start | bytes 589832 | tf_op jit(solution)/shard_map/ppermute | solution.py:557
  69.2 11.9 %collective-permute-start.14 = (bf16[48,2048]{1,0:T(8,128)(2,1)S(1)}, bf16[48,2048]{1,0:T(8,128)(2,1)S(1)}, u32[]{:S(2)}, u32[]{:S(2)}) collective-permute-start(bf16[48,2048]{1,0:T(8,128)(2,1)S(1)} %get-tuple-element.116), channel_id=1, source_target_pairs={{0,4},{2,6},{4,0},{6,2},{1,5},{3,7},{5,1},{7,3},{8,12},{10,14},{12... | collective-permute-start | bytes 589832 | tf_op jit(solution)/shard_map/ppermute | solution.py:557
  72.3 8.9 %collective-permute-start.15 = (bf16[48,2048]{1,0:T(8,128)(2,1)S(1)}, bf16[48,2048]{1,0:T(8,128)(2,1)S(1)}, u32[]{:S(2)}, u32[]{:S(2)}) collective-permute-start(bf16[48,2048]{1,0:T(8,128)(2,1)S(1)} %get-tuple-element.117), channel_id=1, source_target_pairs={{0,6},{2,0},{4,2},{6,4},{1,7},{3,1},{5,3},{7,5},{8,14},{10,8},{12,... | collective-permute-start | bytes 589832 | tf_op jit(solution)/shard_map/ppermute | solution.py:557
  81.1 20.9 %collective-permute-start.16 = (bf16[128,2048]{1,0:T(8,128)(2,1)S(1)}, bf16[128,2048]{1,0:T(8,128)(2,1)S(1)}, u32[]{:S(2)}, u32[]{:S(2)}) collective-permute-start(bf16[128,2048]{1,0:T(8,128)(2,1)S(1)} %get-tuple-element.139.own_ref), channel_id=1, source_target_pairs={{0,2},{2,0},{4,6},{6,4},{1,3},{3,1},{5,7},{7,5},{8,10},{10,8},{12,... | collective-permute-start | bytes 1572872 | tf_op jit(solution)/shard_map/ppermute | solution.py:413
  87.2 10.5 %collective-permute-start.17 = (bf16[48,2048]{1,0:T(8,128)(2,1)}, bf16[48,2048]{1,0:T(8,128)(2,1)S(1)}, u32[]{:S(2)}, u32[]{:S(2)}) collective-permute-start(bf16[48,2048]{1,0:T(8,128)(2,1)} %get-tuple-element.132), channel_id=1, source_target_pairs={{0,6},{2,0},{4,2},{6,4},{1,7},{3,1},{5,3},{7,5},{8,14},{10,8},{12,... | collective-permute-start | bytes 589832 | tf_op jit(solution)/shard_map/ppermute | solution.py:580
  88.7 12.5 %collective-permute-start.18 = (bf16[48,2048]{1,0:T(8,128)(2,1)}, bf16[48,2048]{1,0:T(8,128)(2,1)S(1)}, u32[]{:S(2)}, u32[]{:S(2)}) collective-permute-start(bf16[48,2048]{1,0:T(8,128)(2,1)} %get-tuple-element.133), channel_id=1, source_target_pairs={{0,4},{2,6},{4,0},{6,2},{1,5},{3,7},{5,1},{7,3},{8,12},{10,14},{12... | collective-permute-start | bytes 589832 | tf_op jit(solution)/shard_map/ppermute | solution.py:580
  89.9 12.2 %collective-permute-start.19 = (bf16[48,2048]{1,0:T(8,128)(2,1)}, bf16[48,2048]{1,0:T(8,128)(2,1)}, u32[]{:S(2)}, u32[]{:S(2)}) collective-permute-start(bf16[48,2048]{1,0:T(8,128)(2,1)} %get-tuple-element.134), channel_id=1, source_target_pairs={{0,2},{2,4},{4,6},{6,0},{1,3},{3,5},{5,7},{7,1},{8,10},{10,12},{12... | collective-permute-start | bytes 589832 | tf_op jit(solution)/shard_map/ppermute | solution.py:580
  92.6 3.7 %copy-start = (bf16[48,48,2048]{2,1,0:T(8,128)(2,1)S(1)}, bf16[48,48,2048]{2,1,0:T(8,128)(2,1)}, u32[]{:S(2)}) copy-start(bf16[48,48,2048]{2,1,0:T(8,128)(2,1)} %all-gather.3.cloned.1.call-done) | copy-start | bytes 28311556
  102.1 2.8 %collective-permute-start.20 = (bf16[128,2048]{1,0:T(8,128)(2,1)S(1)}, bf16[128,2048]{1,0:T(8,128)(2,1)S(1)}, u32[]{:S(2)}, u32[]{:S(2)}) collective-permute-start(bf16[128,2048]{1,0:T(8,128)(2,1)S(1)} %collective-permute-done.16.own_ref), channel_id=1, source_target_pairs={{0,1},{1,0},{2,3},{3,2},{4,5},{5,4},{6,7},{7,6},{8,9},{9,8},{10,11... | collective-permute-start | bytes 1572872 | tf_op jit(solution)/shard_map/ppermute | solution.py:408
  108.3 2.0 %collective-permute-start.21 = (bf16[128,2048]{1,0:T(8,128)(2,1)S(1)}, bf16[128,2048]{1,0:T(8,128)(2,1)S(1)}, u32[]{:S(2)}, u32[]{:S(2)}) collective-permute-start(bf16[128,2048]{1,0:T(8,128)(2,1)S(1)} %get-tuple-element.138), channel_id=1, source_target_pairs={{0,1},{1,0},{2,3},{3,2},{4,5},{5,4},{6,7},{7,6},{8,9},{9,8},{10,11... | collective-permute-start | bytes 1572872 | tf_op jit(solution)/shard_map/ppermute | solution.py:408
  110.4 14.7 %collective-permute-start.22 = (bf16[128,2048]{1,0:T(8,128)(2,1)S(1)}, bf16[128,2048]{1,0:T(8,128)(2,1)S(1)}, u32[]{:S(2)}, u32[]{:S(2)}) collective-permute-start(bf16[128,2048]{1,0:T(8,128)(2,1)S(1)} %add_convert_fusion.1), channel_id=1, source_target_pairs={{0,2},{2,0},{4,6},{6,4},{1,3},{3,1},{5,7},{7,5},{8,10},{10,8},{12,... | collective-permute-start | bytes 1572872 | tf_op jit(solution)/shard_map/ppermute | solution.py:413
  125.2 2.4 %collective-permute-start.23 = (bf16[128,2048]{1,0:T(8,128)(2,1)S(1)}, bf16[128,2048]{1,0:T(8,128)(2,1)S(1)}, u32[]{:S(2)}, u32[]{:S(2)}) collective-permute-start(bf16[128,2048]{1,0:T(8,128)(2,1)S(1)} %get-tuple-element.150), channel_id=1, source_target_pairs={{0,1},{1,0},{2,3},{3,2},{4,5},{5,4},{6,7},{7,6},{8,9},{9,8},{10,11... | collective-permute-start | bytes 1572872 | tf_op jit(solution)/shard_map/ppermute | solution.py:408
Sparse Core Ops, SparseCore 0:
  14.2 78.3 all-gather.2
